TPU v7x, 32 devices: a whole 2x2x4 slice. The times are simulated.
32 devices in a mesh: grp: 2 (over y), hold: 4 (over z), tp: 2 (over x), rep: 2 (over core).
Axes of the slice: x: 2, y: 2, z: 4, core: 2. Of those that a mesh axis runs over, the one named last changes fastest.
Arguments:
- cache: bfloat16 [8, 4, 8, 5120], P(('grp', 'hold'), None, ('tp', 'rep')), parts along dimension 0, may hold values from -6 to 6
- ln_gain: float32 [1280], replicated, may hold values from 0.5 to 1.5
- w_fc1: bfloat16 [5120, 2560], P('hold', ('tp', 'rep')), may hold values from -0.078125 to 0.078125
- w_fc2: bfloat16 [2560, 4096], P('hold', ('tp', 'rep'))
- norm_gain: float32 [4096], P(('tp', 'rep')), may hold values from 0.5 to 1.5
- w_key: bfloat16 [4096, 1024], P(('tp', 'rep'), 'hold'), may hold values from -0.09375 to 0.09375
- matching: int32 [8, 4], P('grp'), parts along dimension 0, may hold values from 0 to 3, as said below
- counts: int32 [8, 4, 4], P(('grp', 'hold'), None, ('tp', 'rep')), parts along dimension 0, may hold values from 1 to 2
Outputs:
- keys: bfloat16 [8, 4, 8, 1024], P(('grp', 'hold'), None, ('tp', 'rep')), parts along dimension 0
There are 2 independent parts, one for each index of `grp`. A program takes and returns all parts, laid end to end along the dimension named above; an argument that names none is the same for every part. Nothing has to cross between parts.
Inputs may be any that keep to these rules, and one draw needn't show every extreme that they name: Every row and every column of matching holds each owner once (each round is a perfect matching of holders to owners, and over the rounds each holder meets each owner once).
All inputs are finite; a program needn't handle non-finite values.
Results may differ from a plain program's by a relative error of at most 0.0068.
Values may be sent and summed in bfloat16 or wider, within the bound.
No kernel may reach another device: no remote copies, remote signals or barrier semaphores. Data moves between devices by JAX's collectives and lax.ppermute only.
A program may use at most 64 MiB of HBM per device.

v0:
```python
import jax
import jax.numpy as jnp
from jax import lax
from jax.sharding import PartitionSpec as P

DM = 4096


EPSILON = 1e-06


def patch_norm(rows, ln_gain):
    width = ln_gain.shape[0]
    patches = rows.astype(jnp.float32).reshape(rows.shape[0], -1, width)
    scale = lax.rsqrt(jnp.mean(patches * patches, axis=2, keepdims=True) + EPSILON)
    return (patches * scale * ln_gain).reshape(rows.shape[0], -1).astype(jnp.bfloat16)


def merger_features(rows, ln_gain, w_fc1, w_fc2, norm_gain):
    normed = patch_norm(rows, ln_gain)
    first_cols = lax.all_gather(w_fc1, "hold", axis=0, tiled=True)
    product = jnp.dot(
        lax.all_gather(normed, ("tp", "rep"), axis=0, tiled=True),
        first_cols,
        preferred_element_type=jnp.float32,
    )
    hidden = jax.nn.gelu(product, approximate=False).astype(jnp.bfloat16)
    second_cols = lax.all_gather(w_fc2, "hold", axis=0, tiled=True)
    merged = jnp.dot(
        lax.all_gather(hidden, ("tp", "rep"), axis=1, tiled=True),
        second_cols,
        preferred_element_type=jnp.float32,
    )
    squares = lax.psum(jnp.sum(merged * merged, axis=1), ("tp", "rep"))
    scale = lax.rsqrt(squares / DM + EPSILON)
    return (merged * scale[:, None] * norm_gain).astype(jnp.bfloat16)


def per_device(cache, ln_gain, w_fc1, w_fc2, norm_gain, w_key, matching, counts):
    rounds = cache.shape[1]
    block = cache.shape[2]
    holder_index = lax.axis_index("hold")
    owner_column = lax.dynamic_slice_in_dim(matching, holder_index, 1, 1)[:, 0]
    send_order = jnp.argsort(owner_column)
    source_of = jnp.argmax(matching == holder_index, axis=1)
    local_counts = counts[0, :, 0]
    sent_counts = jnp.take(local_counts, send_order)
    outgoing = jnp.take(cache[0], send_order, axis=0)
    arrived, arrived_counts = (
        lax.all_to_all(outgoing, "hold", split_axis=0, concat_axis=0, tiled=True),
        lax.all_to_all(
            sent_counts.reshape(rounds, 1), "hold", split_axis=0, concat_axis=0, tiled=True
        ),
    )
    own_blocks = jnp.take(arrived, source_of, axis=0)
    own_counts = jnp.take(arrived_counts[:, 0], source_of)
    features = merger_features(
        own_blocks.reshape(rounds * block, -1), ln_gain, w_fc1, w_fc2, norm_gain
    )
    key_cols = lax.all_gather(w_key, "hold", axis=1, tiled=True)
    keys = lax.psum_scatter(
        jnp.dot(features, key_cols, preferred_element_type=jnp.float32),
        ("tp", "rep"),
        scatter_dimension=0,
        tiled=True,
    )
    keys = keys.reshape(rounds, block, -1)
    valid = jnp.arange(block, dtype=jnp.int32)[None, :] < own_counts[:, None]
    keys = jnp.where(valid[:, :, None], keys, jnp.zeros_like(keys))
    return keys.astype(jnp.bfloat16)[None]


def solution(mesh):
    return jax.shard_map(
        per_device,
        mesh=mesh,
        in_specs=(
            P(("grp", "hold"), None, ("tp", "rep"), None),
            P(),
            P("hold", ("tp", "rep")),
            P("hold", ("tp", "rep")),
            P(("tp", "rep")),
            P(("tp", "rep"), "hold"),
            P("grp", None),
            P(("grp", "hold"), None, ("tp", "rep")),
        ),
        out_specs=P(("grp", "hold"), None, ("tp", "rep"), None),
        check_vma=False,
    )
```

profile of v0, /device:TPU:0, one launch (start us, length us, event | category | flops | bytes accessed | tf_op | source)
XLA Modules:
  0.0 305.8 jit_solution(12086911881729339934)
XLA Ops:
  6.5 0.0 copy-start
  6.5 0.0 all-gather.4.cloned.1.call-start
  6.5 0.7 all-gather.4.cloned.1.call-update
  7.3 0.0 all-gather.6.cloned.1.call-start
  7.3 0.7 all-gather.6.cloned.1.call-update
  8.0 0.9 dynamic-slice_reduce_fusion
  8.9 0.7 sort.17
  9.6 1.3 gather_fusion
  11.0 0.7 copy.11
  11.6 6.3 %all-to-all-start = ((s32[4,1,1]{2,1,0:T(1,128)}), s32[4,1,1]{2,1,0:T(1,128)S(1)}, u32[]{:S(2)}, u32[]{:S(2)}) async-start(s32[4,1,1]{2,1,0:T(1,128)} %copy.11), calls=%async_computation | async-start | bytes 4096 | tf_op jit(solution)/shard_map/all_to_all | solution.py:51
  17.9 0.0 all-gather.8.cloned.1.call-start
  17.9 0.7 all-gather.8.cloned.1.call-update
  18.7 1.3 iota_reduce_fusion
  20.0 0.0 copy-done
  20.0 0.7 gather_fusion.2
  20.7 0.7 mul.69
  21.5 0.8 broadcast_select_fusion.1
  22.2 1.2 all-to-all-done
  23.4 3.9 %all-to-all-start.1 = ((bf16[4,2,5120]{2,1,0:T(2,128)(2,1)}), bf16[4,2,5120]{2,1,0:T(2,128)(2,1)S(1)}, u32[]{:S(2)}, u32[]{:S(2)}) async-start(bf16[4,2,5120]{2,1,0:T(2,128)(2,1)} %broadcast_select_fusion.1), calls=%async_computation.1 | async-start | bytes 163840 | tf_op jit(solution)/shard_map/all_to_all | solution.py:50
  27.3 0.0 reduce-scatter.2.cloned.1.call-start
  27.3 0.2 reduce.19
  27.5 0.6 gather_fusion.1
  28.1 6.8 %all-to-all-done.1 = bf16[4,2,5120]{2,1,0:T(2,128)(2,1)S(1)} async-done(((bf16[4,2,5120]{2,1,0:T(2,128)(2,1)}), bf16[4,2,5120]{2,1,0:T(2,128)(2,1)S(1)}, u32[]{:S(2)}, u32[]{:S(2)}) %all-to-all-start.1) | async-done | bytes 81952 | tf_op jit(solution)/shard_map/all_to_all | solution.py:50
  35.0 0.7 gather_fusion.3
  35.7 0.1 fusion.14
  35.8 0.2 mul.65
  36.0 0.1 reduce_sum.18
  36.1 0.1 copy.12
  36.2 0.1 fusion
  36.3 0.1 reshape.75
  36.4 0.1 mul.66
  36.5 6.1 %all_gather.15 = bf16[32,5120]{1,0:T(8,128)(2,1)S(1)} all-gather(bf16[8,5120]{1,0:T(8,128)(2,1)S(1)} %multiply_convert_fusion), channel_id=1, replica_groups=mesh['grp'=2,'hold'=4,'tp'=2,'rep'=2] {'tp','rep'}, dimensions={0}, use_global_device_ids=true | all-gather | bytes 409600 | tf_op jit(solution)/shard_map/all_gather | solution.py:23
  42.7 0.0 copy-start.1
  42.7 90.4 %all-gather.4.cloned.1.call-done = bf16[5120,640]{1,0:T(8,128)(2,1)} async-done(((bf16[1280,640]{1,0:T(8,128)(2,1)}), bf16[5120,640]{1,0:T(8,128)(2,1)}) %all-gather.4.cloned.1.call-update) | async-done | bytes 6553616 | tf_op jit(solution)/shard_map/all_gather | solution.py:21
  133.0 4.1 %fusion.3 = bf16[32,640]{1,0:T(8,128)(2,1)S(1)} fusion(bf16[32,5120]{1,0:T(8,128)(2,1)S(1)} %all_gather.15, bf16[5120,640]{1,0:T(8,128)(2,1)} %all-gather.4.cloned.1.call-done), kind=kOutput, calls=%fused_computation.13 | convolution fusion | flops 211046400 | bytes 6922240 | tf_op jit(solution)/shard_map/dot_general | solution.py:22
  137.1 5.5 %all_gather.17 = bf16[32,2560]{1,0:T(8,128)(2,1)S(1)} all-gather(bf16[32,640]{1,0:T(8,128)(2,1)S(1)} %fusion.3), channel_id=1, replica_groups=mesh['grp'=2,'hold'=4,'tp'=2,'rep'=2] {'tp','rep'}, dimensions={1}, use_global_device_ids=true | all-gather | bytes 204800 | tf_op jit(solution)/shard_map/all_gather | solution.py:30
  142.7 88.2 %all-gather.6.cloned.1.call-done = bf16[2560,1024]{1,0:T(8,128)(2,1)} async-done(((bf16[640,1024]{1,0:T(8,128)(2,1)}), bf16[2560,1024]{1,0:T(8,128)(2,1)}) %all-gather.6.cloned.1.call-update) | async-done | bytes 5242896 | tf_op jit(solution)/shard_map/all_gather | solution.py:28
  230.8 3.6 %multiply_reduce_fusion = (f32[32]{0:T(128)S(1)}, f32[32,1024]{1,0:T(8,128)S(1)}) fusion(bf16[32,2560]{1,0:T(8,128)(2,1)S(1)} %all_gather.17, bf16[2560,1024]{1,0:T(8,128)(2,1)} %all-gather.6.cloned.1.call-done), kind=kOutput, calls=%fused_computation.8 | convolution fusion | flops 167837664 | bytes 5537920 | tf_op jit(solution)/shard_map/dot_general | solution.py:29
  234.4 6.8 %psum.7 = f32[32]{0:T(128)S(1)} all-reduce(f32[32]{0:T(128)S(1)} %get-tuple-element.15), channel_id=1, replica_groups=mesh['grp'=2,'hold'=4,'tp'=2,'rep'=2] {'tp','rep'}, use_global_device_ids=true, to_apply=%region_4.7 | all-reduce | flops 32 | bytes 256 | tf_op jit(solution)/shard_map/psum | solution.py:34
  241.3 35.8 %all-gather.8.cloned.1.call-done = bf16[1024,1024]{1,0:T(8,128)(2,1)} async-done(((bf16[1024,256]{1,0:T(8,128)(2,1)}), bf16[1024,1024]{1,0:T(8,128)(2,1)}) %all-gather.8.cloned.1.call-update) | async-done | bytes 2097168 | tf_op jit(solution)/shard_map/all_gather | solution.py:60
  277.1 0.0 copy-done.1
  277.1 2.7 fusion.11
  279.8 0.0 reduce-scatter.2.cloned.1.call-update
  279.8 0.1 iota_compare_fusion
  279.9 17.9 %reduce-scatter.2.cloned.1.call-done = f32[8,1024]{1,0:T(8,128)} async-done(((f32[32,1024]{1,0:T(8,128)}), f32[8,1024]{1,0:T(8,128)}) %reduce-scatter.2.cloned.1.call-update) | async-done | bytes 32784 | tf_op jit(solution)/shard_map/reduce_scatter | solution.py:61
  297.8 0.8 reshape.74
  298.6 0.7 select_convert_fusion
  (11 shorter events, 0.1 us)
Async XLA Ops:
  6.5 13.5 %copy-start = (bf16[1,4,2,5120]{3,2,1,0:T(2,128)(2,1)S(1)}, bf16[1,4,2,5120]{3,2,1,0:T(2,128)(2,1)}, u32[]{:S(2)}) copy-start(bf16[1,4,2,5120]{3,2,1,0:T(2,128)(2,1)} %param.12) | copy-start | bytes 245764
  6.5 126.5 %all-gather.4.cloned.1.call-start = ((), (), s32[]{:S(2)}) async-start(), calls=%async_computation.3 | async-start | bytes 8192000 | tf_op jit(solution)/shard_map/all_gather | solution.py:21
  7.3 223.6 %all-gather.6.cloned.1.call-start = ((), (), s32[]{:S(2)}) async-start(), calls=%async_computation.4 | async-start | bytes 6553600 | tf_op jit(solution)/shard_map/all_gather | solution.py:28
  11.6 11.8 %all-to-all-start = ((s32[4,1,1]{2,1,0:T(1,128)}), s32[4,1,1]{2,1,0:T(1,128)S(1)}, u32[]{:S(2)}, u32[]{:S(2)}) async-start(s32[4,1,1]{2,1,0:T(1,128)} %copy.11), calls=%async_computation | async-start | bytes 4096 | tf_op jit(solution)/shard_map/all_to_all | solution.py:51
  17.9 259.1 %all-gather.8.cloned.1.call-start = ((), (), s32[]{:S(2)}) async-start(), calls=%async_computation.5 | async-start | bytes 2621440 | tf_op jit(solution)/shard_map/all_gather | solution.py:60
  23.4 11.5 %all-to-all-start.1 = ((bf16[4,2,5120]{2,1,0:T(2,128)(2,1)}), bf16[4,2,5120]{2,1,0:T(2,128)(2,1)S(1)}, u32[]{:S(2)}, u32[]{:S(2)}) async-start(bf16[4,2,5120]{2,1,0:T(2,128)(2,1)} %broadcast_select_fusion.1), calls=%async_computation.1 | async-start | bytes 163840 | tf_op jit(solution)/shard_map/all_to_all | solution.py:50
  27.3 270.5 %reduce-scatter.2.cloned.1.call-start = ((), (), s32[]{:S(2)}) async-start(), calls=%async_computation.6 | async-start | bytes 163840 | tf_op jit(solution)/shard_map/reduce_scatter | solution.py:61
  42.7 234.4 %copy-start.1 = (f32[1024]{0:T(1024)S(1)}, f32[1024]{0:T(1024)}, u32[]{:S(2)}) copy-start(f32[1024]{0:T(1024)} %param.16) | copy-start | bytes 12292
Sparse Core Ops, SparseCore 0:
  8.9 124.0 all-gather.3
  134.6 96.2 all-gather.5
  232.4 44.6 all-gather.7
  279.9 17.7 reduce-scatter.1
where the time goes:
time: 306 us
  waiting for transfers between devices  242 us (79%)
  blocking collectives  18.5 us (6%)
  between operations  13.2 us (4%)
  matrix products  10.5 us (3%)
  starting transfers between devices  10.3 us (3%)
  local copies, waits for them, and re-layouts  6.85 us (2%)
  other arithmetic  4.22 us (1%)
    all_gather x1, waiting for transfers between devices, merger_features(): first_cols = lax.all_gather(w_fc1, 'hold', axis=0, tiled=True)  90.4 us
    all_gather x1, waiting for transfers between devices, merger_features(): second_cols = lax.all_gather(w_fc2, 'hold', axis=0, tiled=True)  88.2 us
    all_gather x1, waiting for transfers between devices, per_device(): key_cols = lax.all_gather(w_key, 'hold', axis=1, tiled=True)  35.8 us
    reduce_scatter x1, waiting for transfers between devices, per_device(): lax.psum_scatter(jnp.dot(features, key_cols, preferred_element_type=jnp.f...  17.9 us
    psum x1, blocking collectives, merger_features(): squares = lax.psum(jnp.sum(merged * merged, axis=1), ('tp', 'rep'))  6.84 us
    all_to_all x1, waiting for transfers between devices, per_device(): lax.all_to_all(outgoing, 'hold', split_axis=0, concat_axis=0, tiled=True)  6.81 us
    all_to_all x1, starting transfers between devices, per_device(): lax.all_to_all(sent_counts.reshape(rounds, 1), 'hold', split_axis=0, conc...  6.32 us
  transfers between devices with their start and end apart: 6, of which 6 were waited for; matrix products, arithmetic and copies ran while one was open for 6% of the time, Pallas kernels for 0%

commit v1 on v0

v1 whole, which is shorter than its diff:
```python
import jax
import jax.numpy as jnp
from jax import lax
from jax.sharding import PartitionSpec as P

EPSILON = 1e-06
GROUP_AXES = ("tp", "rep")
ALL_AXES = ("hold", "tp", "rep")


def patch_norm(rows, ln_gain):
    width = ln_gain.shape[0]
    patches = rows.astype(jnp.float32).reshape(rows.shape[0], -1, width)
    scale = lax.rsqrt(jnp.mean(patches * patches, axis=2, keepdims=True) + EPSILON)
    return patches * scale * ln_gain


def merger_features(rows, ln_gain, w_fc1, w_fc2, norm_gain, width):
    normed = patch_norm(rows, ln_gain).reshape(rows.shape[0], -1).astype(jnp.bfloat16)
    first_cols = lax.all_gather(w_fc1, "hold", axis=0, tiled=True)
    product = jnp.dot(
        lax.all_gather(normed, GROUP_AXES, axis=0, tiled=True),
        first_cols,
        preferred_element_type=jnp.float32,
    )
    hidden = jax.nn.gelu(product, approximate=False).astype(jnp.bfloat16)
    second_cols = lax.all_gather(w_fc2, "hold", axis=0, tiled=True)
    merged = jnp.dot(
        lax.all_gather(hidden, GROUP_AXES, axis=1, tiled=True),
        second_cols,
        preferred_element_type=jnp.float32,
    )
    squares = lax.psum(jnp.sum(merged * merged, axis=1), GROUP_AXES)
    scale = lax.rsqrt(squares / width + EPSILON)
    return (merged * scale[:, None] * norm_gain).astype(jnp.bfloat16)


def rows_to_owners(cache, ln_gain, w_fc1, w_fc2, norm_gain, w_key, matching, counts, width):
    rounds = cache.shape[1]
    block = cache.shape[2]
    holder_index = lax.axis_index("hold")
    owner_column = lax.dynamic_slice_in_dim(matching, holder_index, 1, 1)[:, 0]
    send_order = jnp.argsort(owner_column)
    source_of = jnp.argmax(matching == holder_index, axis=1)
    sent_counts = jnp.take(counts[0, :, 0], send_order)
    outgoing = jnp.take(cache[0], send_order, axis=0)
    arrived = lax.all_to_all(outgoing, "hold", split_axis=0, concat_axis=0, tiled=True)
    arrived_counts = lax.all_to_all(
        sent_counts.reshape(rounds, 1), "hold", split_axis=0, concat_axis=0, tiled=True
    )
    own_blocks = jnp.take(arrived, source_of, axis=0)
    own_counts = jnp.take(arrived_counts[:, 0], source_of)
    features = merger_features(
        own_blocks.reshape(rounds * block, -1), ln_gain, w_fc1, w_fc2, norm_gain, width
    )
    key_cols = lax.all_gather(w_key, "hold", axis=1, tiled=True)
    keys = lax.psum_scatter(
        jnp.dot(features, key_cols, preferred_element_type=jnp.float32),
        GROUP_AXES,
        scatter_dimension=0,
        tiled=True,
    )
    keys = keys.reshape(rounds, block, -1)
    valid = jnp.arange(block, dtype=jnp.int32)[None, :] < own_counts[:, None]
    keys = jnp.where(valid[:, :, None], keys, jnp.zeros_like(keys))
    return keys.astype(jnp.bfloat16)[None]


def swap(x, axis, n, step):
    return lax.ppermute(x, axis, [(i, i ^ step) for i in range(n)])


def rows_past_weights(cache, ln_gain, w_fc1, w_fc2, norm_gain, w_key, matching, counts, width):
    n = lax.axis_size("hold")
    rounds, block, depth = cache.shape[1:]
    h = lax.axis_index("hold")
    t = lax.axis_index("tp") * lax.axis_size("rep") + lax.axis_index("rep")
    rows = rounds * block
    chunk = depth // n
    f32, bf16 = jnp.float32, jnp.bfloat16

    key_cols = lax.all_gather(w_key, "hold", axis=0, tiled=False)

    owner_column = lax.dynamic_slice_in_dim(matching, h, 1, 1)[:, 0]
    live = (jnp.arange(block)[None, :] < counts[0, :, 0][:, None]).astype(f32)
    place = (owner_column[None, :] == jnp.arange(n)[:, None]).astype(f32)
    pick = place[:, :, None] * live[None]
    normed = patch_norm(cache[0].reshape(rows, depth), ln_gain).astype(bf16).astype(f32)
    normed = normed.reshape(rounds, block, depth)
    by_owner = sum(pick[:, r, :, None] * normed[r][None] for r in range(rounds))
    by_chunk = by_owner.reshape(rows, n, chunk).transpose(1, 0, 2).astype(bf16)

    def chunk_of(s):
        return lax.dynamic_index_in_dim(by_chunk, h ^ s, 0, keepdims=False)

    mine = [chunk_of(0)] + [swap(chunk_of(s), "hold", n, s) for s in range(1, n)]
    group_rows = lax.all_gather(jnp.stack(mine), GROUP_AXES, axis=0, tiled=False)
    partial = jnp.dot(
        group_rows.reshape(n * n * rows, chunk), w_fc1, preferred_element_type=f32
    ).reshape(n, n, rows, -1)

    parts = []
    for k in range(n):
        perm = [(a * n + b, b * n + (a ^ k)) for a in range(n) for b in range(n)]
        parts.append(lax.ppermute(partial[:, k].astype(bf16), ALL_AXES, perm).astype(f32))
    product = sum(parts)
    hidden = jax.nn.gelu(product, approximate=False).astype(bf16)

    hidden = lax.all_gather(hidden, GROUP_AXES, axis=0, tiled=False)
    total = n * n * rows
    hidden = hidden.reshape(total, -1)
    to = jnp.arange(total)
    k_of, rest = to // (n * rows), to % (n * rows)
    slot_of, rest = rest // rows, rest % rows
    holder_of, b_of = rest // block, rest % block
    source = ((holder_of * n + slot_of) * n + (k_of ^ h)) * block + b_of
    order = (source[:, None] == jnp.arange(total)[None, :]).astype(bf16)
    hidden = jnp.dot(order, hidden, preferred_element_type=f32).astype(bf16)
    partial = jnp.dot(hidden, w_fc2, preferred_element_type=f32).reshape(n, n * rows, -1)
    merged = sum(
        [partial[0]]
        + [swap(partial[k].astype(bf16), "hold", n, k).astype(f32) for k in range(1, n)]
    )

    squares = jnp.sum(merged * merged, axis=1, keepdims=True)
    features = (merged * norm_gain).astype(bf16)
    keys = [jnp.dot(features, key_cols[i], preferred_element_type=f32) for i in range(n)]
    keys = jnp.concatenate(keys + [jnp.broadcast_to(squares, (n * rows, 128))], axis=1)
    keys = keys.reshape(n, rows, -1)

    def slot(u):
        return lax.dynamic_index_in_dim(keys, t ^ u, 0, keepdims=False)

    keys = slot(0) + sum(swap(slot(u), GROUP_AXES, n, u) for u in range(1, n))
    keys = keys[:, :-128] * lax.rsqrt(keys[:, -1:] / width + EPSILON)
    keys = keys.reshape(n, block, -1)
    source_of = (matching == h).astype(f32)
    keys = sum(source_of[:, i, None, None] * keys[i][None] for i in range(n))
    return keys.astype(bf16)[None]


def per_device(cache, ln_gain, w_fc1, w_fc2, norm_gain, w_key, matching, counts):
    hold = lax.axis_size("hold")
    group = lax.axis_size("tp") * lax.axis_size("rep")
    rounds, block, depth = cache.shape[1:]
    width = w_key.shape[0] * group
    few = hold * rounds * group * block <= w_fc1.shape[1]
    square = hold == group == rounds and hold & (hold - 1) == 0
    plan = rows_past_weights if few and square else rows_to_owners
    return plan(cache, ln_gain, w_fc1, w_fc2, norm_gain, w_key, matching, counts, width)


def solution(mesh):
    return jax.shard_map(
        per_device,
        mesh=mesh,
        in_specs=(
            P(("grp", "hold"), None, ("tp", "rep"), None),
            P(),
            P("hold", ("tp", "rep")),
            P("hold", ("tp", "rep")),
            P(("tp", "rep")),
            P(("tp", "rep"), "hold"),
            P("grp", None),
            P(("grp", "hold"), None, ("tp", "rep")),
        ),
        out_specs=P(("grp", "hold"), None, ("tp", "rep"), None),
        check_vma=False,
    )
```

time: 306 us -> 88.4 us (0.29)
  waiting for transfers between devices: 242 us -> 28.1 us
  starting transfers between devices: 10.3 us -> 16.5 us
  blocking collectives: 18.5 us -> 14.1 us
    all_gather x3 -> x1, waiting for transfers between devices: 214 us -> 0.02 us  [rows_past_weights(): key_cols = lax.all_gather(w_key, 'hold', axis=0, tiled=False)]
    ppermute x0 -> x13, waiting for transfers between devices: none -> 27.4 us  [the longest x4 14.9 us: rows_past_weights(): lax.ppermute(partial[:, k].astype(bf16), ALL_AXES, perm).astype(f32)]
    reduce_scatter x1 -> x0, waiting for transfers between devices: 17.9 us -> none  [per_device(): lax.psum_scatter(jnp.dot(features, key_cols, preferred_element_type=jnp.f...]
    ppermute x0 -> x13, starting transfers between devices: none -> 16.5 us  [the longest x9 12.1 us: swap(): return lax.ppermute(x, axis, [(i, i ^ step) for i in range(n)])]
    all_to_all x2 -> x0, starting transfers between devices: 10.2 us -> none  [the longest x1 6.32 us: per_device(): lax.all_to_all(sent_counts.reshape(rounds, 1), 'hold', split_axis=0, conc...]
    all_to_all x2 -> x0, waiting for transfers between devices: 7.99 us -> none  [the longest x1 6.81 us: per_device(): lax.all_to_all(outgoing, 'hold', split_axis=0, concat_axis=0, tiled=True)]
    psum x1 -> x0, blocking collectives: 6.84 us -> none  [merger_features(): squares = lax.psum(jnp.sum(merged * merged, axis=1), ('tp', 'rep'))]
    gather x4 -> x0, local copies, waits for them, and re-layouts: 3.37 us -> none  [the longest x1 1.29 us: per_device(): sent_counts = jnp.take(local_counts, send_order)]
  transfers between devices with their start and end apart: 6 -> 14, of which waited for: 6 -> 8; matrix products, arithmetic and copies ran while one was open for 6% -> 11% of each run, Pallas kernels for 0% -> 0%
where the time goes in v1:
time: 88.4 us; the launch traced here: 87.8 us
  waiting for transfers between devices  28.1 us (32%)
  starting transfers between devices  16.5 us (19%)
  blocking collectives  14.1 us (16%)
  between operations  13.7 us (15%)
  matrix products  7.53 us (9%)
  local copies, waits for them, and re-layouts  4.57 us (5%)
  other arithmetic  3.34 us (4%)
    ppermute x4, waiting for transfers between devices, rows_past_weights(): lax.ppermute(partial[:, k].astype(bf16), ALL_AXES, perm).astype(f32)  14.9 us
    ppermute x9, waiting for transfers between devices, swap(): return lax.ppermute(x, axis, [(i, i ^ step) for i in range(n)])  12.5 us
    ppermute x9, starting transfers between devices, swap(): return lax.ppermute(x, axis, [(i, i ^ step) for i in range(n)])  12.1 us
    all_gather x1, blocking collectives, rows_past_weights(): hidden = lax.all_gather(hidden, GROUP_AXES, axis=0, tiled=False)  7.85 us
    all_gather x1, blocking collectives, rows_past_weights(): lax.all_gather(jnp.stack(mine), GROUP_AXES, axis=0, tiled=False)  6.23 us
    dot_general x4, matrix products, rows_past_weights(): jnp.dot(features, key_cols[i], preferred_element_type=f32)  4.95 us
    ppermute x4, starting transfers between devices, rows_past_weights(): lax.ppermute(partial[:, k].astype(bf16), ALL_AXES, perm).astype(f32)  4.43 us
    dot_general x1, matrix products, rows_past_weights(): jnp.dot(hidden, w_fc2, preferred_element_type=f32).reshape(n, n * rows, -1)  2.14 us
  transfers between devices with their start and end apart: 14, of which 8 were waited for; matrix products, arithmetic and copies ran while one was open for 11% of the time, Pallas kernels for 0%

profile of v1, /device:TPU:0, one launch (start us, length us, event | category | flops | bytes accessed | tf_op | source)
XLA Modules:
  0.0 87.8 jit_solution(9407199402601596820)
XLA Ops:
  6.5 0.7 all-gather.5.cloned.1.call-update
  7.3 0.9 fusion.30
  8.1 0.1 fusion.31
  8.2 0.7 fusion.32
  8.9 1.0 %reshape.232 = f32[8,4,1280]{2,1,0:T(4,128)S(1)} reshape(bf16[1,4,2,5120]{3,2,1,0:T(2,128)(2,1)} %param.8) | data formatting | bytes 245760 | tf_op jit(solution)/shard_map/convert_element_type | solution.py:13
  9.9 0.1 multiply_reduce_fusion
  10.0 0.8 fusion.17
  10.9 0.1 broadcast_multiply_fusion
  10.9 0.1 mul.273
  11.0 0.1 mul.284
  11.1 0.1 mul.290
  11.2 0.1 mul.296
  11.4 0.2 mul.282
  11.6 0.2 mul.288
  11.9 0.2 mul.294
  12.1 0.2 mul.300
  12.3 0.2 add_convert_fusion
  12.5 0.2 constant_dynamic-slice_fusion.3
  12.7 3.1 %collective-permute-start = (bf16[8,1280]{1,0:T(8,128)(2,1)S(1)}, bf16[8,1280]{1,0:T(8,128)(2,1)S(1)}, u32[]{:S(2)}, u32[]{:S(2)}) collective-permute-start(bf16[8,1280]{1,0:T(8,128)(2,1)S(1)} %bitcast.90), channel_id=1, source_target_pairs={{0,4},{4,0},{8,12},{12,8},{1,5},{5,1},{9,13},{13,9},{2,6},{6,2},{1... | collective-permute-start | bytes 61448 | tf_op jit(solution)/shard_map/ppermute | solution.py:70
  15.8 2.6 %collective-permute-start.1 = (bf16[8,1280]{1,0:T(8,128)(2,1)S(1)}, bf16[8,1280]{1,0:T(8,128)(2,1)S(1)}, u32[]{:S(2)}, u32[]{:S(2)}) collective-permute-start(bf16[8,1280]{1,0:T(8,128)(2,1)S(1)} %bitcast.91), channel_id=1, source_target_pairs={{0,8},{4,12},{8,0},{12,4},{1,9},{5,13},{9,1},{13,5},{2,10},{6,14},... | collective-permute-start | bytes 61448 | tf_op jit(solution)/shard_map/ppermute | solution.py:70
  18.4 0.0 collective-permute-start.2
  18.4 0.0 collective-permute-done
  18.4 2.3 %collective-permute-done.1 = bf16[8,1280]{1,0:T(8,128)(2,1)S(1)} collective-permute-done((bf16[8,1280]{1,0:T(8,128)(2,1)S(1)}, bf16[8,1280]{1,0:T(8,128)(2,1)S(1)}, u32[]{:S(2)}, u32[]{:S(2)}) %collective-permute-start.1) | collective-permute-done | bytes 20512 | tf_op jit(solution)/shard_map/ppermute | solution.py:70
  20.7 3.5 %collective-permute-done.2 = bf16[8,1280]{1,0:T(8,128)(2,1)S(1)} collective-permute-done((bf16[8,1280]{1,0:T(8,128)(2,1)S(1)}, bf16[8,1280]{1,0:T(8,128)(2,1)S(1)}, u32[]{:S(2)}, u32[]{:S(2)}) %collective-permute-start.2) | collective-permute-done | bytes 20512 | tf_op jit(solution)/shard_map/ppermute | solution.py:70
  24.2 0.0 copy-start.1
  24.2 6.2 %all-gather = bf16[16,8,1280]{2,1,0:T(8,128)(2,1)S(1)} all-gather(bf16[4,8,1280]{2,1,0:T(8,128)(2,1)S(1)} %pad_maximum_fusion), channel_id=2, replica_groups=mesh['grp'=2,'hold'=4,'tp'=2,'rep'=2] {'tp','rep'}, dimensions={0}, use_global_device_ids=true | all-gather | bytes 409600 | tf_op jit(solution)/shard_map/all_gather | solution.py:97
  30.4 0.4 fusion.2
  30.9 0.0 copy-start.2
  30.9 0.0 copy-start.3
  30.9 0.7 collective-permute-start.3
  31.6 1.7 %collective-permute-start.4 = (bf16[4,8,640]{2,1,0:T(8,128)(2,1)S(1)}, bf16[4,8,640]{2,1,0:T(8,128)(2,1)S(1)}, u32[]{:S(2)}, u32[]{:S(2)}) collective-permute-start(bf16[4,8,640]{2,1,0:T(8,128)(2,1)S(1)} %get-tuple-element.15), channel_id=1, source_target_pairs={{0,1},{1,5},{2,9},{3,13},{4,0},{5,4},{6,8},{7,12},{8,3},{9,7},{10,... | collective-permute-start | bytes 122888 | tf_op jit(solution)/shard_map/ppermute | solution.py:105
  33.2 1.5 %collective-permute-start.5 = (bf16[4,8,640]{2,1,0:T(8,128)(2,1)S(1)}, bf16[4,8,640]{2,1,0:T(8,128)(2,1)S(1)}, u32[]{:S(2)}, u32[]{:S(2)}) collective-permute-start(bf16[4,8,640]{2,1,0:T(8,128)(2,1)S(1)} %get-tuple-element.17), channel_id=1, source_target_pairs={{0,2},{1,6},{2,10},{3,14},{4,3},{5,7},{6,11},{7,15},{8,0},{9,4},{1... | collective-permute-start | bytes 122888 | tf_op jit(solution)/shard_map/ppermute | solution.py:105
  34.8 0.6 collective-permute-start.6
  35.4 0.0 collective-permute-done.3
  35.4 5.0 %collective-permute-done.4 = bf16[4,8,640]{2,1,0:T(8,128)(2,1)S(1)} collective-permute-done((bf16[4,8,640]{2,1,0:T(8,128)(2,1)S(1)}, bf16[4,8,640]{2,1,0:T(8,128)(2,1)S(1)}, u32[]{:S(2)}, u32[]{:S(2)}) %collective-permute-start.4) | collective-permute-done | bytes 40992 | tf_op jit(solution)/shard_map/ppermute | solution.py:105
  40.3 10.0 %collective-permute-done.5 = bf16[4,8,640]{2,1,0:T(8,128)(2,1)S(1)} collective-permute-done((bf16[4,8,640]{2,1,0:T(8,128)(2,1)S(1)}, bf16[4,8,640]{2,1,0:T(8,128)(2,1)S(1)}, u32[]{:S(2)}, u32[]{:S(2)}) %collective-permute-start.5) | collective-permute-done | bytes 40992 | tf_op jit(solution)/shard_map/ppermute | solution.py:105
  50.3 0.0 collective-permute-done.6
  50.3 0.2 fusion.16
  50.5 7.8 %all-gather.1 = bf16[16,8,640]{2,1,0:T(8,128)(2,1)} all-gather(bf16[4,8,640]{2,1,0:T(8,128)(2,1)S(1)} %fusion.16), channel_id=3, replica_groups=mesh['grp'=2,'hold'=4,'tp'=2,'rep'=2] {'tp','rep'}, dimensions={0}, use_global_device_ids=true | all-gather | bytes 204800 | tf_op jit(solution)/shard_map/all_gather | solution.py:109
  58.3 2.1 %fusion.39 = (bf16[128,1024]{1,0:T(8,128)(2,1)}, f32[128,1024]{1,0:T(8,128)S(1)}) fusion(bf16[640,1024]{1,0:T(8,128)(2,1)S(1)} %copy-done.1, bf16[16,8,640]{2,1,0:T(8,128)(2,1)} %all-gather.1, s32[128]{0:T(128)S(1)} %fusion.33), kind=kOutput, calls=%fused_computation.106 | convolution fusion | flops 188973056 | bytes 2261504 | tf_op jit(solution)/shard_map/dot_general | solution.py:119
  60.5 0.9 %fusion.36 = (bf16[32,1024]{1,0:T(8,128)(2,1)S(1)}, bf16[32,1024]{1,0:T(8,128)(2,1)S(1)}, bf16[32,1024]{1,0:T(8,128)(2,1)S(1)}) fusion(bf16[128,1024]{1,0:T(8,128)(2,1)} %get-tuple-element.37), kind=kLoop, calls=%fused_computation.103 | loop fusion | bytes 393216 | tf_op jit(solution)/shard_map/slice | solution.py:122
  61.4 0.1 collective-permute-start.7
  61.5 1.3 %collective-permute-start.8 = (bf16[32,1024]{1,0:T(8,128)(2,1)S(1)}, bf16[32,1024]{1,0:T(8,128)(2,1)S(1)}, u32[]{:S(2)}, u32[]{:S(2)}) collective-permute-start(bf16[32,1024]{1,0:T(8,128)(2,1)S(1)} %get-tuple-element.13), channel_id=1, source_target_pairs={{0,8},{4,12},{8,0},{12,4},{1,9},{5,13},{9,1},{13,5},{2,10},{6,14},... | collective-permute-start | bytes 196616 | tf_op jit(solution)/shard_map/ppermute | solution.py:70
  62.8 3.0 %collective-permute-start.9 = (bf16[32,1024]{1,0:T(8,128)(2,1)S(1)}, bf16[32,1024]{1,0:T(8,128)(2,1)S(1)}, u32[]{:S(2)}, u32[]{:S(2)}) collective-permute-start(bf16[32,1024]{1,0:T(8,128)(2,1)S(1)} %get-tuple-element.12), channel_id=1, source_target_pairs={{0,12},{4,8},{8,4},{12,0},{1,13},{5,9},{9,5},{13,1},{2,14},{6,10},... | collective-permute-start | bytes 196616 | tf_op jit(solution)/shard_map/ppermute | solution.py:70
  65.9 0.9 collective-permute-done.7
  66.7 3.4 %collective-permute-done.8 = bf16[32,1024]{1,0:T(8,128)(2,1)S(1)} collective-permute-done((bf16[32,1024]{1,0:T(8,128)(2,1)S(1)}, bf16[32,1024]{1,0:T(8,128)(2,1)S(1)}, u32[]{:S(2)}, u32[]{:S(2)}) %collective-permute-start.8) | collective-permute-done | bytes 65568 | tf_op jit(solution)/shard_map/ppermute | solution.py:70
  70.1 0.0 collective-permute-done.9
  70.1 0.1 multiply_reduce_fusion.1
  70.3 0.0 all-gather.5.cloned.1.call-done
  70.3 1.2 %convolution_dynamic-update-slice_fusion.3 = f32[32,1152]{1,0:T(8,128)S(1)} fusion(bf16[32,1024]{1,0:T(8,128)(2,1)S(1)} %get-tuple-element.10, bf16[4096,256]{1,0:T(8,128)(2,1)} %all-gather.5.cloned.1.call-done), kind=kOutput, calls=%fused_computation.8 | convolution fusion | flops 16777215 | bytes 622592 | tf_op jit(solution)/shard_map/dot_general | solution.py:127
  71.5 1.2 %convolution_dynamic-update-slice_fusion.2 = f32[32,1152]{1,0:T(8,128)S(1)} fusion(f32[32,1152]{1,0:T(8,128)S(1)} %convolution_dynamic-update-slice_fusion.3, bf16[32,1024]{1,0:T(8,128)(2,1)S(1)} %get-tuple-element.10, bf16[4096,256]{1,0:T(8,128)(2,1)} %all-gather.5.cloned.1.call-done), kind=kOutput, calls=%fused_computation.7 | convolution fusion | flops 16777216 | bytes 622592 | tf_op jit(solution)/shard_map/dot_general | solution.py:127
  72.8 1.2 %convolution_dynamic-update-slice_fusion.1 = f32[32,1152]{1,0:T(8,128)S(1)} fusion(f32[32,1152]{1,0:T(8,128)S(1)} %convolution_dynamic-update-slice_fusion.2, bf16[32,1024]{1,0:T(8,128)(2,1)S(1)} %get-tuple-element.10, bf16[4096,256]{1,0:T(8,128)(2,1)} %all-gather.5.cloned.1.call-done), kind=kOutput, calls=%fused_computation.6 | convolution fusion | flops 16777216 | bytes 622592 | tf_op jit(solution)/shard_map/dot_general | solution.py:127
  74.0 1.2 %convolution_dynamic-update-slice_fusion = f32[32,1152]{1,0:T(8,128)S(1)} fusion(f32[32,1152]{1,0:T(8,128)S(1)} %convolution_dynamic-update-slice_fusion.1, bf16[32,1024]{1,0:T(8,128)(2,1)S(1)} %get-tuple-element.10, bf16[4096,256]{1,0:T(8,128)(2,1)} %all-gather.5.cloned.1.call-done), kind=kOutput, calls=%fused_computation.5 | convolution fusion | flops 16777216 | bytes 622592 | tf_op jit(solution)/shard_map/dot_general | solution.py:127
  75.3 0.1 constant_dynamic-update-slice_fusion
  75.4 0.1 collective-permute-start.10
  75.4 1.1 %collective-permute-start.11 = (f32[8,1152]{1,0:T(8,128)S(1)}, f32[8,1152]{1,0:T(8,128)S(1)}, u32[]{:S(2)}, u32[]{:S(2)}) collective-permute-start(f32[8,1152]{1,0:T(8,128)S(1)} %get-tuple-element.22), channel_id=1, source_target_pairs={{0,2},{1,3},{2,0},{3,1},{4,6},{5,7},{6,4},{7,5},{8,10},{9,11},{10,... | collective-permute-start | bytes 110600 | tf_op jit(solution)/shard_map/ppermute | solution.py:70
  76.5 0.8 collective-permute-start.12
  77.3 0.2 slice_reduce_fusion.3
  77.5 0.0 collective-permute-done.10
  77.5 1.9 %collective-permute-done.11 = f32[8,1152]{1,0:T(8,128)S(1)} collective-permute-done((f32[8,1152]{1,0:T(8,128)S(1)}, f32[8,1152]{1,0:T(8,128)S(1)}, u32[]{:S(2)}, u32[]{:S(2)}) %collective-permute-start.11) | collective-permute-done | bytes 36896 | tf_op jit(solution)/shard_map/ppermute | solution.py:70
  79.5 0.5 collective-permute-done.12
  80.0 0.2 fusion.29
  80.2 0.1 slice_multiply_fusion
  80.3 0.7 add_convert_fusion.1
  (28 shorter events, 0.4 us)
Async XLA Ops:
  6.5 23.9 %copy-start = (bf16[1280,640]{1,0:T(8,128)(2,1)S(1)}, bf16[1280,640]{1,0:T(8,128)(2,1)}, u32[]{:S(2)}) copy-start(bf16[1280,640]{1,0:T(8,128)(2,1)} %param.10) | copy-start | bytes 4915204
  6.5 63.8 %all-gather.5.cloned.1.call-start = ((), (), s32[]{:S(2)}) async-start(), calls=%async_computation | async-start | bytes 2621440 | tf_op jit(solution)/shard_map/all_gather | solution.py:82
  12.7 5.7 %collective-permute-start = (bf16[8,1280]{1,0:T(8,128)(2,1)S(1)}, bf16[8,1280]{1,0:T(8,128)(2,1)S(1)}, u32[]{:S(2)}, u32[]{:S(2)}) collective-permute-start(bf16[8,1280]{1,0:T(8,128)(2,1)S(1)} %bitcast.90), channel_id=1, source_target_pairs={{0,4},{4,0},{8,12},{12,8},{1,5},{5,1},{9,13},{13,9},{2,6},{6,2},{1... | collective-permute-start | bytes 61448 | tf_op jit(solution)/shard_map/ppermute | solution.py:70
  15.8 4.9 %collective-permute-start.1 = (bf16[8,1280]{1,0:T(8,128)(2,1)S(1)}, bf16[8,1280]{1,0:T(8,128)(2,1)S(1)}, u32[]{:S(2)}, u32[]{:S(2)}) collective-permute-start(bf16[8,1280]{1,0:T(8,128)(2,1)S(1)} %bitcast.91), channel_id=1, source_target_pairs={{0,8},{4,12},{8,0},{12,4},{1,9},{5,13},{9,1},{13,5},{2,10},{6,14},... | collective-permute-start | bytes 61448 | tf_op jit(solution)/shard_map/ppermute | solution.py:70
  18.4 5.8 %collective-permute-start.2 = (bf16[8,1280]{1,0:T(8,128)(2,1)S(1)}, bf16[8,1280]{1,0:T(8,128)(2,1)S(1)}, u32[]{:S(2)}, u32[]{:S(2)}) collective-permute-start(bf16[8,1280]{1,0:T(8,128)(2,1)S(1)} %bitcast.92), channel_id=1, source_target_pairs={{0,12},{4,8},{8,4},{12,0},{1,13},{5,9},{9,5},{13,1},{2,14},{6,10},... | collective-permute-start | bytes 61448 | tf_op jit(solution)/shard_map/ppermute | solution.py:70
  24.2 34.2 %copy-start.1 = (bf16[640,1024]{1,0:T(8,128)(2,1)S(1)}, bf16[640,1024]{1,0:T(8,128)(2,1)}, u32[]{:S(2)}) copy-start(bf16[640,1024]{1,0:T(8,128)(2,1)} %param.11) | copy-start | bytes 3932164
  30.9 35.0 %copy-start.2 = (s32[4,4]{1,0:T(4,128)S(1)}, s32[4,4]{1,0:T(4,128)}, u32[]{:S(2)}) copy-start(s32[4,4]{1,0:T(4,128)} %param.14) | copy-start | bytes 196
  30.9 39.3 %copy-start.3 = (f32[1024]{0:T(1024)S(1)}, f32[1024]{0:T(1024)}, u32[]{:S(2)}) copy-start(f32[1024]{0:T(1024)} %param.12) | copy-start | bytes 12292
  30.9 4.5 %collective-permute-start.3 = (bf16[4,8,640]{2,1,0:T(8,128)(2,1)S(1)}, bf16[4,8,640]{2,1,0:T(8,128)(2,1)S(1)}, u32[]{:S(2)}, u32[]{:S(2)}) collective-permute-start(bf16[4,8,640]{2,1,0:T(8,128)(2,1)S(1)} %get-tuple-element.14), channel_id=1, source_target_pairs={{0,0},{1,4},{2,8},{3,12},{4,1},{5,5},{6,9},{7,13},{8,2},{9,6},{10,... | collective-permute-start | bytes 122888 | tf_op jit(solution)/shard_map/ppermute | solution.py:105
  31.6 8.7 %collective-permute-start.4 = (bf16[4,8,640]{2,1,0:T(8,128)(2,1)S(1)}, bf16[4,8,640]{2,1,0:T(8,128)(2,1)S(1)}, u32[]{:S(2)}, u32[]{:S(2)}) collective-permute-start(bf16[4,8,640]{2,1,0:T(8,128)(2,1)S(1)} %get-tuple-element.15), channel_id=1, source_target_pairs={{0,1},{1,5},{2,9},{3,13},{4,0},{5,4},{6,8},{7,12},{8,3},{9,7},{10,... | collective-permute-start | bytes 122888 | tf_op jit(solution)/shard_map/ppermute | solution.py:105
  33.2 17.0 %collective-permute-start.5 = (bf16[4,8,640]{2,1,0:T(8,128)(2,1)S(1)}, bf16[4,8,640]{2,1,0:T(8,128)(2,1)S(1)}, u32[]{:S(2)}, u32[]{:S(2)}) collective-permute-start(bf16[4,8,640]{2,1,0:T(8,128)(2,1)S(1)} %get-tuple-element.17), channel_id=1, source_target_pairs={{0,2},{1,6},{2,10},{3,14},{4,3},{5,7},{6,11},{7,15},{8,0},{9,4},{1... | collective-permute-start | bytes 122888 | tf_op jit(solution)/shard_map/ppermute | solution.py:105
  34.8 15.5 %collective-permute-start.6 = (bf16[4,8,640]{2,1,0:T(8,128)(2,1)S(1)}, bf16[4,8,640]{2,1,0:T(8,128)(2,1)S(1)}, u32[]{:S(2)}, u32[]{:S(2)}) collective-permute-start(bf16[4,8,640]{2,1,0:T(8,128)(2,1)S(1)} %get-tuple-element.16), channel_id=1, source_target_pairs={{0,3},{1,7},{2,11},{3,15},{4,2},{5,6},{6,10},{7,14},{8,1},{9,5},{1... | collective-permute-start | bytes 122888 | tf_op jit(solution)/shard_map/ppermute | solution.py:105
  61.4 5.3 %collective-permute-start.7 = (bf16[32,1024]{1,0:T(8,128)(2,1)S(1)}, bf16[32,1024]{1,0:T(8,128)(2,1)S(1)}, u32[]{:S(2)}, u32[]{:S(2)}) collective-permute-start(bf16[32,1024]{1,0:T(8,128)(2,1)S(1)} %get-tuple-element.11), channel_id=1, source_target_pairs={{0,4},{4,0},{8,12},{12,8},{1,5},{5,1},{9,13},{13,9},{2,6},{6,2},{1... | collective-permute-start | bytes 196616 | tf_op jit(solution)/shard_map/ppermute | solution.py:70
  61.5 8.6 %collective-permute-start.8 = (bf16[32,1024]{1,0:T(8,128)(2,1)S(1)}, bf16[32,1024]{1,0:T(8,128)(2,1)S(1)}, u32[]{:S(2)}, u32[]{:S(2)}) collective-permute-start(bf16[32,1024]{1,0:T(8,128)(2,1)S(1)} %get-tuple-element.13), channel_id=1, source_target_pairs={{0,8},{4,12},{8,0},{12,4},{1,9},{5,13},{9,1},{13,5},{2,10},{6,14},... | collective-permute-start | bytes 196616 | tf_op jit(solution)/shard_map/ppermute | solution.py:70
  62.8 7.3 %collective-permute-start.9 = (bf16[32,1024]{1,0:T(8,128)(2,1)S(1)}, bf16[32,1024]{1,0:T(8,128)(2,1)S(1)}, u32[]{:S(2)}, u32[]{:S(2)}) collective-permute-start(bf16[32,1024]{1,0:T(8,128)(2,1)S(1)} %get-tuple-element.12), channel_id=1, source_target_pairs={{0,12},{4,8},{8,4},{12,0},{1,13},{5,9},{9,5},{13,1},{2,14},{6,10},... | collective-permute-start | bytes 196616 | tf_op jit(solution)/shard_map/ppermute | solution.py:70
  75.4 2.2 %collective-permute-start.10 = (f32[8,1152]{1,0:T(8,128)S(1)}, f32[8,1152]{1,0:T(8,128)S(1)}, u32[]{:S(2)}, u32[]{:S(2)}) collective-permute-start(f32[8,1152]{1,0:T(8,128)S(1)} %get-tuple-element.24), channel_id=1, source_target_pairs={{0,1},{1,0},{2,3},{3,2},{4,5},{5,4},{6,7},{7,6},{8,9},{9,8},{10,11... | collective-permute-start | bytes 110600 | tf_op jit(solution)/shard_map/ppermute | solution.py:70
  75.4 4.0 %collective-permute-start.11 = (f32[8,1152]{1,0:T(8,128)S(1)}, f32[8,1152]{1,0:T(8,128)S(1)}, u32[]{:S(2)}, u32[]{:S(2)}) collective-permute-start(f32[8,1152]{1,0:T(8,128)S(1)} %get-tuple-element.22), channel_id=1, source_target_pairs={{0,2},{1,3},{2,0},{3,1},{4,6},{5,7},{6,4},{7,5},{8,10},{9,11},{10,... | collective-permute-start | bytes 110600 | tf_op jit(solution)/shard_map/ppermute | solution.py:70
  76.5 3.4 %collective-permute-start.12 = (f32[8,1152]{1,0:T(8,128)S(1)}, f32[8,1152]{1,0:T(8,128)S(1)}, u32[]{:S(2)}, u32[]{:S(2)}) collective-permute-start(f32[8,1152]{1,0:T(8,128)S(1)} %get-tuple-element.23), channel_id=1, source_target_pairs={{0,3},{1,2},{2,1},{3,0},{4,7},{5,6},{6,5},{7,4},{8,11},{9,10},{10,... | collective-permute-start | bytes 110600 | tf_op jit(solution)/shard_map/ppermute | solution.py:70
Sparse Core Ops, SparseCore 0:
  8.9 55.8 all-gather.4

commit v2 on v0

v2 whole, which is shorter than its diff:
```python
import functools

import jax
import jax.numpy as jnp
from jax import lax
from jax.experimental import pallas as pl
from jax.experimental.pallas import tpu as pltpu
from jax.sharding import PartitionSpec as P

EPSILON = 1e-06
GROUP_AXES = ("tp", "rep")
ALL_AXES = ("hold", "tp", "rep")


def patch_norm(rows, ln_gain):
    width = ln_gain.shape[0]
    patches = rows.astype(jnp.float32).reshape(rows.shape[0], -1, width)
    scale = lax.rsqrt(jnp.mean(patches * patches, axis=2, keepdims=True) + EPSILON)
    return patches * scale * ln_gain


def merger_features(rows, ln_gain, w_fc1, w_fc2, norm_gain, width):
    normed = patch_norm(rows, ln_gain).reshape(rows.shape[0], -1).astype(jnp.bfloat16)
    first_cols = lax.all_gather(w_fc1, "hold", axis=0, tiled=True)
    product = jnp.dot(
        lax.all_gather(normed, GROUP_AXES, axis=0, tiled=True),
        first_cols,
        preferred_element_type=jnp.float32,
    )
    hidden = jax.nn.gelu(product, approximate=False).astype(jnp.bfloat16)
    second_cols = lax.all_gather(w_fc2, "hold", axis=0, tiled=True)
    merged = jnp.dot(
        lax.all_gather(hidden, GROUP_AXES, axis=1, tiled=True),
        second_cols,
        preferred_element_type=jnp.float32,
    )
    squares = lax.psum(jnp.sum(merged * merged, axis=1), GROUP_AXES)
    scale = lax.rsqrt(squares / width + EPSILON)
    return (merged * scale[:, None] * norm_gain).astype(jnp.bfloat16)


def rows_to_owners(cache, ln_gain, w_fc1, w_fc2, norm_gain, w_key, matching, counts, width):
    rounds = cache.shape[1]
    block = cache.shape[2]
    holder_index = lax.axis_index("hold")
    owner_column = lax.dynamic_slice_in_dim(matching, holder_index, 1, 1)[:, 0]
    send_order = jnp.argsort(owner_column)
    source_of = jnp.argmax(matching == holder_index, axis=1)
    sent_counts = jnp.take(counts[0, :, 0], send_order)
    outgoing = jnp.take(cache[0], send_order, axis=0)
    arrived = lax.all_to_all(outgoing, "hold", split_axis=0, concat_axis=0, tiled=True)
    arrived_counts = lax.all_to_all(
        sent_counts.reshape(rounds, 1), "hold", split_axis=0, concat_axis=0, tiled=True
    )
    own_blocks = jnp.take(arrived, source_of, axis=0)
    own_counts = jnp.take(arrived_counts[:, 0], source_of)
    features = merger_features(
        own_blocks.reshape(rounds * block, -1), ln_gain, w_fc1, w_fc2, norm_gain, width
    )
    key_cols = lax.all_gather(w_key, "hold", axis=1, tiled=True)
    keys = lax.psum_scatter(
        jnp.dot(features, key_cols, preferred_element_type=jnp.float32),
        GROUP_AXES,
        scatter_dimension=0,
        tiled=True,
    )
    keys = keys.reshape(rounds, block, -1)
    valid = jnp.arange(block, dtype=jnp.int32)[None, :] < own_counts[:, None]
    keys = jnp.where(valid[:, :, None], keys, jnp.zeros_like(keys))
    return keys.astype(jnp.bfloat16)[None]


def swap(x, axis, n, step):
    return lax.ppermute(x, axis, [(i, i ^ step) for i in range(n)])


def call(body, outs, *args, flops=0, scratch=(), **specs):
    moved = sum(x.size * x.dtype.itemsize for x in args)
    return pl.pallas_call(
        body,
        out_shape=outs,
        scratch_shapes=scratch,
        cost_estimate=pl.CostEstimate(flops=flops, bytes_accessed=moved, transcendentals=0),
        compiler_params=pltpu.CompilerParams(vmem_limit_bytes=16 << 20),
        **specs,
    )(*args)


def dot(a, b):
    return jnp.dot(a, b, preferred_element_type=jnp.float32)


def norm_kernel(cache, ln_gain, matching, counts, w_fc1, w_key, *refs):
    outs, w_held, key_rows = refs[:4], refs[4], refs[5:9]
    x_in, gain_in, plan_in, live_in, held, sems = refs[9:]
    n = len(outs)
    h = lax.axis_index("hold")
    share = key_rows[0].shape[0]
    pairs = [(cache, x_in), (ln_gain, gain_in), (matching, plan_in), (counts, live_in)]
    for s in range(n):
        start = pl.multiple_of((h ^ s) * share, 128)
        pairs.append((w_key.at[pl.ds(start, share)], key_rows[s]))
    pairs.append((w_fc1, w_held))
    copies = [pltpu.make_async_copy(a, b, sems.at[i]) for i, (a, b) in enumerate(pairs)]
    for copy in copies:
        copy.start()
    for copy in copies[:4]:
        copy.wait()
    _, rounds, block, depth = cache.shape
    width = ln_gain.shape[0]
    chunk = depth // n
    gain = gain_in[...].reshape(1, width)
    column = lax.broadcasted_iota(jnp.int32, matching.shape, 1) == h
    owner = jnp.sum(jnp.where(column, plan_in[...], 0), axis=1, keepdims=True)
    b_of = lax.broadcasted_iota(jnp.int32, (block, 1), 0)
    for p in range(depth // width):
        cols = pl.ds(p * width, width)
        normed = []
        for r in range(rounds):
            x = x_in[0, r, :, cols].astype(jnp.float32)
            scale = lax.rsqrt(jnp.mean(x * x, axis=1, keepdims=True) + EPSILON)
            scale = jnp.where(b_of < live_in[:, r : r + 1], scale, 0.0)
            normed.append(x * scale * gain)
        for j in range(rounds):
            picked = sum(
                jnp.where(owner[r : r + 1] == j, normed[r], 0.0) for r in range(rounds)
            )
            held[j * block : (j + 1) * block, cols] = picked
    for s in range(n):
        start = pl.multiple_of((h ^ s) * chunk, 128)
        outs[s][...] = held[:, pl.ds(start, chunk)].astype(jnp.bfloat16)
    for copy in copies[4:]:
        copy.wait()


def first_kernel(mine, other, *refs):
    weights, outs = refs[:2], refs[2:6]
    rows, sums = refs[6:]
    h, rep = lax.axis_index("hold"), lax.axis_index("rep")
    half = mine.shape[0]
    size = half // 4
    for b, part in enumerate((mine, other)):
        part = part[...].astype(jnp.float32)
        for s in range(4):
            start = pl.multiple_of(b * half + (h ^ s) * size, 8)
            rows[pl.ds(start, size), :] = part[s * size : (s + 1) * size]
    x = rows[...].astype(jnp.bfloat16)
    for i, weight in enumerate(weights):
        sums[rep ^ i] = dot(x, weight[...])
    for k, out in enumerate(outs):
        start = pl.multiple_of(((h ^ k) & 1) * half, 16)
        out[...] = sums[(h ^ k) >> 1, pl.ds(start, half), :].astype(jnp.bfloat16)


def second_kernel(first, second, w_mine, w_other, *refs):
    outs, sums = refs[:4], refs[4]
    h = lax.axis_index("hold")
    half = first.shape[0]
    bb = half // 16
    to = lax.broadcasted_iota(jnp.int32, (2 * half, half), 0)
    source = lax.broadcasted_iota(jnp.int32, (2 * half, half), 1)
    u, owner = to // half, (to % half) // (4 * bb)
    holder, b_of = (to % (4 * bb)) // bb, to % bb
    wanted = (u ^ (h >> 1)) * half + (holder * 4 + owner) * bb + b_of
    moved = 0.0
    for p, part in enumerate((first, second)):
        order = jnp.where(source + p * half == wanted, 1.0, 0.0)
        moved += dot(order.astype(jnp.bfloat16), part[...])
    moved = moved.astype(jnp.bfloat16)
    cols = outs[0].shape[1] // 2
    for p, weight in enumerate((w_mine, w_other)):
        sums[p] = dot(moved, weight[...])
        for k in range(4):
            start = pl.multiple_of((h ^ k) * cols, 128)
            part = sums[p, :, pl.ds(start, cols)].astype(jnp.bfloat16)
            outs[k][:, p * cols : (p + 1) * cols] = part


def key_kernel(*refs):
    parts, blocks, gains = refs[:4], refs[4:6], refs[6:8]
    kept, sent, held = refs[8:]
    h = lax.axis_index("hold")
    merged = sum(part[...].astype(jnp.float32) for part in parts)
    squares = jnp.sum(merged * merged, axis=1, keepdims=True)
    cols = merged.shape[1] // 2
    start = pl.multiple_of(h * cols, 128)
    features = []
    for p in range(2):
        gain = gains[p][pl.ds(start, cols)].reshape(1, cols)
        features.append((merged[:, p * cols : (p + 1) * cols] * gain).astype(jnp.bfloat16))
    width = blocks[0].shape[1]
    for s in range(4):
        start = pl.multiple_of((h ^ s) * width, 128)
        held[:, pl.ds(start, width)] = sum(
            dot(features[p], blocks[p][s * cols : (s + 1) * cols, :]) for p in range(2)
        )
    half = kept.shape[0]
    keys = 4 * width
    kept[:, :keys] = held[:half, :]
    kept[:, keys:] = jnp.broadcast_to(squares[:half], (half, 128))
    sent[:, :keys] = held[half:, :].astype(jnp.bfloat16)
    high = squares[half:].astype(jnp.bfloat16).astype(jnp.float32)
    lane = lax.broadcasted_iota(jnp.int32, (half, 128), 1)
    pair = jnp.where(lane < 64, high, squares[half:] - high)
    sent[:, keys:] = pair.astype(jnp.bfloat16)


def group_kernel(kept, came, *refs):
    outs, held = refs[:4], refs[4]
    h = lax.axis_index("hold")
    keys = kept.shape[1] - 128
    held[:, :keys] = kept[:, :keys] + came[:, :keys].astype(jnp.float32)
    pair = came[:, keys:].astype(jnp.float32)
    squares = kept[:, keys:] + pair[:, :1] + pair[:, 127:]
    held[:, keys:] = squares
    rows = outs[0].shape[0]
    for k in range(4):
        outs[k][...] = held[pl.ds(pl.multiple_of((h ^ k) * rows, 8), rows), :]


def last_kernel(width, *refs):
    parts, matching, out = refs[:4], refs[4], refs[5]
    h = lax.axis_index("hold")
    total = sum(part[...] for part in parts)
    keys = total[:, :-128] * lax.rsqrt(total[:, -1:] / width + EPSILON)
    _, rounds, block, _ = out.shape
    for r in range(rounds):
        picked = sum(
            jnp.where(matching[r : r + 1, i : i + 1] == h, keys[i * block : (i + 1) * block], 0.0)
            for i in range(rounds)
        )
        out[0, r] = picked.astype(jnp.bfloat16)


def rows_past_weights(cache, ln_gain, w_fc1, w_fc2, norm_gain, w_key, matching, counts, width):
    n = lax.axis_size("hold")
    rounds, block, depth = cache.shape[1:]
    rows = rounds * block
    chunk = depth // n
    hidden_cols, out_cols, key_cols = w_fc1.shape[1], w_fc2.shape[1], w_key.shape[1]
    share = w_key.shape[0] // n
    f32, bf16 = jnp.float32, jnp.bfloat16
    vmem = pltpu.VMEM

    def like(dims, kind=bf16):
        return jax.ShapeDtypeStruct(dims, kind)

    w_fc1_other = swap(w_fc1, "rep", 2, 1)
    w_fc2_other = swap(w_fc2, "rep", 2, 1)
    gain_other = swap(norm_gain, "rep", 2, 1)
    counts = counts.reshape(1, rounds)
    cache_in, w_fc1_in, w_key_in, ln_in, matching_in, counts_in = (
        pltpu.with_memory_space_constraint(x, pltpu.HBM)
        for x in (cache, w_fc1, w_key, ln_gain, matching, counts)
    )
    *chunks, w_fc1_mine, key_0, key_1, key_2, key_3 = call(
        norm_kernel,
        [like((rows, chunk))] * n + [like(w_fc1.shape)] + [like((share, key_cols))] * n,
        cache_in,
        ln_in,
        matching_in,
        counts_in,
        w_fc1_in,
        w_key_in,
        in_specs=[pl.BlockSpec(memory_space=pltpu.HBM)] * 6,
        scratch=[
            vmem(cache.shape, bf16),
            vmem(ln_gain.shape, f32),
            vmem(matching.shape, jnp.int32),
            vmem(counts.shape, jnp.int32),
            vmem((rows, depth), f32),
            pltpu.SemaphoreType.DMA((9,)),
        ],
    )
    group_rows = jnp.concatenate(
        [swap(chunks[s], "hold", n, s) if s else chunks[s] for s in range(n)], axis=0
    )
    group_rows, w_fc1_other, w_fc2_other, gain_other, key_1, key_2, key_3 = (
        lax.optimization_barrier(
            (group_rows, w_fc1_other, w_fc2_other, gain_other, key_1, key_2, key_3)
        )
    )
    key_1, key_2, key_3 = (
        swap(part, "hold", n, s + 1) for s, part in enumerate((key_1, key_2, key_3))
    )

    partial = call(
        first_kernel,
        [like((4 * rows, hidden_cols))] * n,
        group_rows,
        swap(group_rows, "tp", 2, 1),
        w_fc1_mine,
        w_fc1_other,
        scratch=[vmem((8 * rows, chunk), f32), vmem((2, 8 * rows, hidden_cols), f32)],
        flops=32 * rows * w_fc1.size,
    )
    *partial, key_1 = lax.optimization_barrier((*partial, key_1))
    parts = [swap(partial[k], "hold", n, k) if k else partial[k] for k in range(n)]
    product = sum(part.astype(f32) for part in parts)
    hidden = jax.nn.gelu(product, approximate=False).astype(bf16)

    hidden, key_2, key_3 = lax.optimization_barrier((hidden, key_2, key_3))
    key_mine = jnp.concatenate([key_0, key_1, key_2, key_3])
    key_other = swap(key_mine, "rep", 2, 1)

    halves = []
    for g in range(2):
        perm = [
            (2 * a + b, 2 * (2 * b + (a >> 1)) + ((a & 1) ^ g)) for a in range(n) for b in range(2)
        ]
        halves.append(lax.ppermute(hidden, ("hold", "tp"), perm))

    merged = call(
        second_kernel,
        [like((8 * rows, 2 * share))] * n,
        *halves,
        w_fc2,
        w_fc2_other,
        scratch=[vmem((2, 8 * rows, out_cols), f32)],
        flops=32 * rows * w_fc2.size,
    )
    merged = [swap(merged[k], "hold", n, k) if k else merged[k] for k in range(n)]

    kept, sent = call(
        key_kernel,
        [like((4 * rows, n * key_cols + 128), f32), like((4 * rows, n * key_cols + 128))],
        *merged,
        key_mine,
        key_other,
        norm_gain,
        gain_other,
        scratch=[vmem((8 * rows, n * key_cols), f32)],
        flops=32 * rows * w_key.size,
    )
    keys = call(
        group_kernel,
        [like((rows, n * key_cols + 128), f32)] * n,
        kept,
        swap(sent, "tp", 2, 1),
        scratch=[vmem((4 * rows, n * key_cols + 128), f32)],
    )
    keys = [swap(keys[k], "hold", n, k) if k else keys[k] for k in range(n)]
    return call(
        functools.partial(last_kernel, width),
        like((1, rounds, block, n * key_cols)),
        *keys,
        matching,
    )


def per_device(cache, ln_gain, w_fc1, w_fc2, norm_gain, w_key, matching, counts):
    sizes = lax.axis_size("hold"), lax.axis_size("tp"), lax.axis_size("rep")
    rounds, block, depth = cache.shape[1:]
    group = sizes[1] * sizes[2]
    width = w_key.shape[0] * group
    few = sizes[0] * rounds * group * block <= w_fc1.shape[1]
    fits = sizes == (4, 2, 2) and rounds == 4 and block == 2
    plan = rows_past_weights if few and fits else rows_to_owners
    return plan(cache, ln_gain, w_fc1, w_fc2, norm_gain, w_key, matching, counts, width)


def solution(mesh):
    return jax.shard_map(
        per_device,
        mesh=mesh,
        in_specs=(
            P(("grp", "hold"), None, ("tp", "rep"), None),
            P(),
            P("hold", ("tp", "rep")),
            P("hold", ("tp", "rep")),
            P(("tp", "rep")),
            P(("tp", "rep"), "hold"),
            P("grp", None),
            P(("grp", "hold"), None, ("tp", "rep")),
        ),
        out_specs=P(("grp", "hold"), None, ("tp", "rep"), None),
        check_vma=False,
    )
```

time: 306 us -> 63.4 us (0.21)
  waiting for transfers between devices: 242 us -> 27.5 us
  starting transfers between devices: 10.3 us -> 30.9 us
  blocking collectives: 18.5 us -> 0 us
  between operations: 13.2 us -> 0.16 us
  matrix products: 10.5 us -> 0 us
  local copies, waits for them, and re-layouts: 6.85 us -> 0.05 us
  Pallas kernels: 0 us -> 4.45 us
  other arithmetic: 4.22 us -> 0.22 us
    all_gather x3 -> x0, waiting for transfers between devices: 214 us -> none  [the longest x1 90.4 us: merger_features(): first_cols = lax.all_gather(w_fc1, 'hold', axis=0, tiled=True)]
    ppermute x0 -> x23, starting transfers between devices: none -> 30.9 us  [the longest x21 29.7 us: swap(): return lax.ppermute(x, axis, [(i, i ^ step) for i in range(n)])]
    ppermute x0 -> x23, waiting for transfers between devices: none -> 27.5 us  [the longest x21 24.6 us: swap(): return lax.ppermute(x, axis, [(i, i ^ step) for i in range(n)])]
    reduce_scatter x1 -> x0, waiting for transfers between devices: 17.9 us -> none  [per_device(): lax.psum_scatter(jnp.dot(features, key_cols, preferred_element_type=jnp.f...]
    all_gather x2 -> x0, blocking collectives: 11.6 us -> none  [the longest x1 6.1 us: merger_features(): lax.all_gather(normed, ('tp', 'rep'), axis=0, tiled=True)]
    dot_general x3 -> x0, matrix products: 10.5 us -> none  [the longest x1 4.13 us: merger_features(): jnp.dot(lax.all_gather(normed, ('tp', 'rep'), axis=0, tiled=True), first_...]
    all_to_all x2 -> x0, starting transfers between devices: 10.2 us -> none  [the longest x1 6.32 us: per_device(): lax.all_to_all(sent_counts.reshape(rounds, 1), 'hold', split_axis=0, conc...]
    all_to_all x2 -> x0, waiting for transfers between devices: 7.99 us -> none  [the longest x1 6.81 us: per_device(): lax.all_to_all(outgoing, 'hold', split_axis=0, concat_axis=0, tiled=True)]
  transfers between devices with their start and end apart: 6 -> 23, of which waited for: 6 -> 10; matrix products, arithmetic and copies ran while one was open for 6% -> 0% of each run, Pallas kernels for 0% -> 5%
where the time goes in v2:
time: 63.4 us; the launch traced here: 63.3 us
  starting transfers between devices  30.9 us (49%)
  waiting for transfers between devices  27.5 us (43%)
  Pallas kernels  4.45 us (7%)
    ppermute x21, starting transfers between devices, swap(): return lax.ppermute(x, axis, [(i, i ^ step) for i in range(n)])  29.7 us
    ppermute x21, waiting for transfers between devices, swap(): return lax.ppermute(x, axis, [(i, i ^ step) for i in range(n)])  24.6 us
    pallas_call x6, Pallas kernels, call(): pl.pallas_call(body, out_shape=outs, scratch_shapes=scratch, cost_estimat...  4.45 us
    ppermute x2, waiting for transfers between devices, rows_past_weights(): halves.append(lax.ppermute(hidden, ('hold', 'tp'), perm))  2.81 us
  transfers between devices with their start and end apart: 23, of which 10 were waited for; matrix products, arithmetic and copies ran while one was open for 0% of the time, Pallas kernels for 5%

profile of v2, /device:TPU:0, one launch (start us, length us, event | category | flops | bytes accessed | tf_op | source)
XLA Modules:
  0.0 63.3 jit_solution(9279271078499528893)
XLA Ops:
  0.0 0.0 copy-start.2
  0.0 0.5 collective-permute-start.3
  0.5 0.1 collective-permute-start.4
  0.5 1.9 %shard_map.82 = (bf16[8,1280]{1,0:T(8,128)(2,1)S(1)}, bf16[8,1280]{1,0:T(8,128)(2,1)S(1)}, bf16[8,1280]{1,0:T(8,128)(2,1)S(1)}, bf16[8,1280]{1,0:T(8,128)(2,1)S(...) custom-call(bf16[1,4,2,5120]{3,2,1,0:T(2,128)(2,1)} %cache.1, ...), custom_call_target="tpu_custom_call" | custom-call | bytes 2249808 | tf_op jit(solution)/shard_map/pallas_call | solution.py:79
  2.4 3.1 %collective-permute-start = (bf16[8,1280]{1,0:T(8,128)(2,1)S(1)}, bf16[8,1280]{1,0:T(8,128)(2,1)S(1)}, u32[]{:S(2)}, u32[]{:S(2)}) collective-permute-start(bf16[8,1280]{1,0:T(8,128)(2,1)S(1)} %get-tuple-element.44), channel_id=1, source_target_pairs={{0,4},{4,0},{8,12},{12,8},{1,5},{5,1},{9,13},{13,9},{2,6},{6,2},{1... | collective-permute-start | bytes 61448 | tf_op jit(solution)/shard_map/ppermute | solution.py:74
  5.5 2.6 %collective-permute-start.1 = (bf16[8,1280]{1,0:T(8,128)(2,1)S(1)}, bf16[8,1280]{1,0:T(8,128)(2,1)S(1)}, u32[]{:S(2)}, u32[]{:S(2)}) collective-permute-start(bf16[8,1280]{1,0:T(8,128)(2,1)S(1)} %get-tuple-element.45), channel_id=1, source_target_pairs={{0,8},{4,12},{8,0},{12,4},{1,9},{5,13},{9,1},{13,5},{2,10},{6,14},... | collective-permute-start | bytes 61448 | tf_op jit(solution)/shard_map/ppermute | solution.py:74
  8.1 0.0 collective-permute-start.2
  8.1 0.0 collective-permute-done
  8.1 0.0 copy-done.2
  8.1 0.1 collective-permute-start.5
  8.2 2.1 %collective-permute-done.1 = bf16[8,1280]{1,0:T(8,128)(2,1)S(1)} collective-permute-done((bf16[8,1280]{1,0:T(8,128)(2,1)S(1)}, bf16[8,1280]{1,0:T(8,128)(2,1)S(1)}, u32[]{:S(2)}, u32[]{:S(2)}) %collective-permute-start.1) | collective-permute-done | bytes 20512 | tf_op jit(solution)/shard_map/ppermute | solution.py:74
  10.3 3.4 %collective-permute-done.2 = bf16[8,1280]{1,0:T(8,128)(2,1)S(1)} collective-permute-done((bf16[8,1280]{1,0:T(8,128)(2,1)S(1)}, bf16[8,1280]{1,0:T(8,128)(2,1)S(1)}, u32[]{:S(2)}, u32[]{:S(2)}) %collective-permute-start.2) | collective-permute-done | bytes 20512 | tf_op jit(solution)/shard_map/ppermute | solution.py:74
  13.6 0.0 collective-permute-done.5.refs_7_
  13.7 0.0 collective-permute-done.4.w_other
  13.7 0.0 collective-permute-done.3.refs_1_
  13.7 1.6 %collective-permute-start.6 = (bf16[32,1280]{1,0:T(8,128)(2,1)S(1)}, bf16[32,1280]{1,0:T(8,128)(2,1)S(1)}, u32[]{:S(2)}, u32[]{:S(2)}) collective-permute-start(bf16[32,1280]{1,0:T(8,128)(2,1)S(1)} %pad_maximum_fusion.mine), channel_id=1, source_target_pairs={{0,2},{2,0},{1,3},{3,1},{4,6},{6,4},{5,7},{7,5},{8,10},{10,8},{9,1... | collective-permute-start | bytes 245768 | tf_op jit(solution)/shard_map/ppermute | solution.py:74
  15.2 0.0 collective-permute-start.7
  15.2 0.8 %collective-permute-start.11 = (bf16[256,256]{1,0:T(8,128)(2,1)S(1)}, bf16[256,256]{1,0:T(8,128)(2,1)S(1)}, u32[]{:S(2)}, u32[]{:S(2)}) collective-permute-start(bf16[256,256]{1,0:T(8,128)(2,1)S(1)} %get-tuple-element.62), channel_id=1, source_target_pairs={{0,8},{4,12},{8,0},{12,4},{1,9},{5,13},{9,1},{13,5},{2,10},{6,14},... | collective-permute-start | bytes 393224 | tf_op jit(solution)/shard_map/ppermute | solution.py:74
  16.1 3.6 %collective-permute-start.12 = (bf16[256,256]{1,0:T(8,128)(2,1)S(1)}, bf16[256,256]{1,0:T(8,128)(2,1)S(1)}, u32[]{:S(2)}, u32[]{:S(2)}) collective-permute-start(bf16[256,256]{1,0:T(8,128)(2,1)S(1)} %get-tuple-element.63), channel_id=1, source_target_pairs={{0,12},{4,8},{8,4},{12,0},{1,13},{5,9},{9,5},{13,1},{2,14},{6,10},... | collective-permute-start | bytes 393224 | tf_op jit(solution)/shard_map/ppermute | solution.py:74
  19.7 0.0 collective-permute-done.6.other
  19.7 0.0 copy-start
  19.7 0.6 %shard_map.83 = (bf16[32,640]{1,0:T(8,128)(2,1)S(1)}, bf16[32,640]{1,0:T(8,128)(2,1)S(1)}, bf16[32,640]{1,0:T(8,128)(2,1)S(1)}, bf16[32,640]{1,0:T(8,128)(2,1)S(1)}) custom-call(bf16[32,1280]{1,0:T(8,128)(2,1)S(1)} %pad_maximum_fusion.mine, bf16[32,1280]{1,0:T(8,128)(2,1)S(1)} %collective-permute-done.6.other, ...), custom_call_target="tpu_custom_call" | custom-call | flops 209715200 | bytes 3440640 | tf_op jit(solution)/shard_map/pallas_call | solution.py:79
  20.4 0.0 collective-permute-done.7
  20.4 0.7 %collective-permute-start.8 = (bf16[32,640]{1,0:T(8,128)(2,1)S(1)}, bf16[32,640]{1,0:T(8,128)(2,1)S(1)}, u32[]{:S(2)}, u32[]{:S(2)}) collective-permute-start(bf16[32,640]{1,0:T(8,128)(2,1)S(1)} %get-tuple-element.59), channel_id=1, source_target_pairs={{0,4},{4,0},{8,12},{12,8},{1,5},{5,1},{9,13},{13,9},{2,6},{6,2},{1... | collective-permute-start | bytes 122888 | tf_op jit(solution)/shard_map/ppermute | solution.py:74
  21.1 0.6 collective-permute-start.9
  21.6 3.2 %collective-permute-start.10 = (bf16[32,640]{1,0:T(8,128)(2,1)S(1)}, bf16[32,640]{1,0:T(8,128)(2,1)S(1)}, u32[]{:S(2)}, u32[]{:S(2)}) collective-permute-start(bf16[32,640]{1,0:T(8,128)(2,1)S(1)} %get-tuple-element.61), channel_id=1, source_target_pairs={{0,12},{4,8},{8,4},{12,0},{1,13},{5,9},{9,5},{13,1},{2,14},{6,10},... | collective-permute-start | bytes 122888 | tf_op jit(solution)/shard_map/ppermute | solution.py:74
  24.8 1.5 %collective-permute-done.8 = bf16[32,640]{1,0:T(8,128)(2,1)S(1)} collective-permute-done((bf16[32,640]{1,0:T(8,128)(2,1)S(1)}, bf16[32,640]{1,0:T(8,128)(2,1)S(1)}, u32[]{:S(2)}, u32[]{:S(2)}) %collective-permute-start.8) | collective-permute-done | bytes 40992 | tf_op jit(solution)/shard_map/ppermute | solution.py:74
  26.4 4.9 %collective-permute-done.9 = bf16[32,640]{1,0:T(8,128)(2,1)S(1)} collective-permute-done((bf16[32,640]{1,0:T(8,128)(2,1)S(1)}, bf16[32,640]{1,0:T(8,128)(2,1)S(1)}, u32[]{:S(2)}, u32[]{:S(2)}) %collective-permute-start.9) | collective-permute-done | bytes 40992 | tf_op jit(solution)/shard_map/ppermute | solution.py:74
  31.3 0.0 collective-permute-done.10
  31.3 0.2 fusion.2
  31.5 0.0 collective-permute-done.11
  31.5 0.0 collective-permute-done.12
  31.5 0.0 copy-start.1
  31.6 0.1 collective-permute-start.18
  31.6 0.6 collective-permute-start.14
  32.2 0.7 %collective-permute-start.13 = (bf16[32,640]{1,0:T(8,128)(2,1)S(1)}, bf16[32,640]{1,0:T(8,128)(2,1)S(1)}, u32[]{:S(2)}, u32[]{:S(2)}) collective-permute-start(bf16[32,640]{1,0:T(8,128)(2,1)S(1)} %fusion.2), channel_id=1, source_target_pairs={{0,0},{2,8},{4,2},{6,10},{8,4},{10,12},{12,6},{14,14},{1,1},{3,9},... | collective-permute-start | bytes 122888 | tf_op jit(solution)/shard_map/ppermute | solution.py:311
  32.9 2.8 %collective-permute-done.14.second = bf16[32,640]{1,0:T(8,128)(2,1)S(1)} collective-permute-done((bf16[32,640]{1,0:T(8,128)(2,1)S(1)}, bf16[32,640]{1,0:T(8,128)(2,1)S(1)}, u32[]{:S(2)}, u32[]{:S(2)}) %collective-permute-start.14) | collective-permute-done | bytes 40992 | tf_op jit(solution)/shard_map/ppermute | solution.py:311
  35.7 0.0 collective-permute-done.13.first
  35.7 0.0 copy-done
  35.7 0.8 %shard_map.84 = (bf16[64,512]{1,0:T(8,128)(2,1)S(1)}, bf16[64,512]{1,0:T(8,128)(2,1)S(1)}, bf16[64,512]{1,0:T(8,128)(2,1)S(1)}, bf16[64,512]{1,0:T(8,128)(2,1)S(1)}) custom-call(bf16[32,640]{1,0:T(8,128)(2,1)S(1)} %collective-permute-done.13.first, bf16[32,640]{1,0:T(8,128)(2,1)S(1)} %collective-permute-done.14.second, bf16[640,1024]{1,0:T(8,128)(2,1)S(1)} %copy-done, ...), custom_call_target="tpu_custom_call" | custom-call | flops 167772160 | bytes 2703360 | tf_op jit(solution)/shard_map/pallas_call | solution.py:79
  36.5 4.0 %collective-permute-start.15 = (bf16[64,512]{1,0:T(8,128)(2,1)S(1)}, bf16[64,512]{1,0:T(8,128)(2,1)S(1)}, u32[]{:S(2)}, u32[]{:S(2)}) collective-permute-start(bf16[64,512]{1,0:T(8,128)(2,1)S(1)} %get-tuple-element.67), channel_id=1, source_target_pairs={{0,4},{4,0},{8,12},{12,8},{1,5},{5,1},{9,13},{13,9},{2,6},{6,2},{1... | collective-permute-start | bytes 196616 | tf_op jit(solution)/shard_map/ppermute | solution.py:74
  40.4 2.8 %collective-permute-start.16 = (bf16[64,512]{1,0:T(8,128)(2,1)S(1)}, bf16[64,512]{1,0:T(8,128)(2,1)S(1)}, u32[]{:S(2)}, u32[]{:S(2)}) collective-permute-start(bf16[64,512]{1,0:T(8,128)(2,1)S(1)} %get-tuple-element.68), channel_id=1, source_target_pairs={{0,8},{4,12},{8,0},{12,4},{1,9},{5,13},{9,1},{13,5},{2,10},{6,14},... | collective-permute-start | bytes 196616 | tf_op jit(solution)/shard_map/ppermute | solution.py:74
  43.2 0.9 %collective-permute-start.17 = (bf16[64,512]{1,0:T(8,128)(2,1)S(1)}, bf16[64,512]{1,0:T(8,128)(2,1)S(1)}, u32[]{:S(2)}, u32[]{:S(2)}) collective-permute-start(bf16[64,512]{1,0:T(8,128)(2,1)S(1)} %get-tuple-element.69), channel_id=1, source_target_pairs={{0,12},{4,8},{8,4},{12,0},{1,13},{5,9},{9,5},{13,1},{2,14},{6,10},... | collective-permute-start | bytes 196616 | tf_op jit(solution)/shard_map/ppermute | solution.py:74
  44.1 0.0 collective-permute-done.15.refs_1_
  44.1 3.7 %collective-permute-done.16.refs_2_ = bf16[64,512]{1,0:T(8,128)(2,1)S(1)} collective-permute-done((bf16[64,512]{1,0:T(8,128)(2,1)S(1)}, bf16[64,512]{1,0:T(8,128)(2,1)S(1)}, u32[]{:S(2)}, u32[]{:S(2)}) %collective-permute-start.16) | collective-permute-done | bytes 65568 | tf_op jit(solution)/shard_map/ppermute | solution.py:74
  47.8 1.5 %collective-permute-done.17.refs_3_ = bf16[64,512]{1,0:T(8,128)(2,1)S(1)} collective-permute-done((bf16[64,512]{1,0:T(8,128)(2,1)S(1)}, bf16[64,512]{1,0:T(8,128)(2,1)S(1)}, u32[]{:S(2)}, u32[]{:S(2)}) %collective-permute-start.17) | collective-permute-done | bytes 65568 | tf_op jit(solution)/shard_map/ppermute | solution.py:74
  49.3 0.0 collective-permute-done.18.refs_5_
  49.3 0.3 shard_map.85
  49.6 0.8 %collective-permute-start.19 = (bf16[32,1152]{1,0:T(8,128)(2,1)S(1)}, bf16[32,1152]{1,0:T(8,128)(2,1)S(1)}, u32[]{:S(2)}, u32[]{:S(2)}) collective-permute-start(bf16[32,1152]{1,0:T(8,128)(2,1)S(1)} %get-tuple-element.76), channel_id=1, source_target_pairs={{0,2},{2,0},{1,3},{3,1},{4,6},{6,4},{5,7},{7,5},{8,10},{10,8},{9,1... | collective-permute-start | bytes 221192 | tf_op jit(solution)/shard_map/ppermute | solution.py:74
  50.4 3.6 %collective-permute-done.19.came = bf16[32,1152]{1,0:T(8,128)(2,1)S(1)} collective-permute-done((bf16[32,1152]{1,0:T(8,128)(2,1)S(1)}, bf16[32,1152]{1,0:T(8,128)(2,1)S(1)}, u32[]{:S(2)}, u32[]{:S(2)}) %collective-permute-start.19) | collective-permute-done | bytes 73760 | tf_op jit(solution)/shard_map/ppermute | solution.py:74
  54.1 0.1 shard_map.86
  54.1 0.1 collective-permute-start.20
  54.3 2.4 %collective-permute-start.21 = (f32[8,1152]{1,0:T(8,128)S(1)}, f32[8,1152]{1,0:T(8,128)S(1)}, u32[]{:S(2)}, u32[]{:S(2)}) collective-permute-start(f32[8,1152]{1,0:T(8,128)S(1)} %get-tuple-element.79), channel_id=1, source_target_pairs={{0,8},{4,12},{8,0},{12,4},{1,9},{5,13},{9,1},{13,5},{2,10},{6,14},... | collective-permute-start | bytes 110600 | tf_op jit(solution)/shard_map/ppermute | solution.py:74
  56.7 1.9 %collective-permute-start.22 = (f32[8,1152]{1,0:T(8,128)S(1)}, f32[8,1152]{1,0:T(8,128)S(1)}, u32[]{:S(2)}, u32[]{:S(2)}) collective-permute-start(f32[8,1152]{1,0:T(8,128)S(1)} %get-tuple-element.80), channel_id=1, source_target_pairs={{0,12},{4,8},{8,4},{12,0},{1,13},{5,9},{9,5},{13,1},{2,14},{6,10},... | collective-permute-start | bytes 110600 | tf_op jit(solution)/shard_map/ppermute | solution.py:74
  58.6 0.0 collective-permute-done.20.refs_1_
  58.6 0.5 collective-permute-done.21.refs_2_
  59.1 3.3 %collective-permute-done.22.refs_3_ = f32[8,1152]{1,0:T(8,128)S(1)} collective-permute-done((f32[8,1152]{1,0:T(8,128)S(1)}, f32[8,1152]{1,0:T(8,128)S(1)}, u32[]{:S(2)}, u32[]{:S(2)}) %collective-permute-start.22) | collective-permute-done | bytes 36896 | tf_op jit(solution)/shard_map/ppermute | solution.py:74
  62.5 0.0 copy-done.1
  62.5 0.8 %shard_map.87 = bf16[1,4,2,1024]{3,2,1,0:T(2,128)(2,1)} custom-call(f32[8,1152]{1,0:T(8,128)S(1)} %get-tuple-element.77.refs_0_, f32[8,1152]{1,0:T(8,128)S(1)} %collective-permute-done.20.refs_1_, f32[8,1152]{1,0:T(8,128)S(1)} %collective-permute-done.21.refs_2_, f32[8,1152]{1,0:T(8,128)S(1)} %collective-permute-done.22.refs_3_, s32[4,4]{1,0:T(4,128)S(1)} %copy-done.1), custom_call_target="tpu_custom_call" | custom-call | bytes 147520 | tf_op jit(solution)/shard_map/pallas_call | solution.py:79
  (5 shorter events, 0.0 us)
Async XLA Ops:
  0.0 8.1 %copy-start.2 = (f32[1024]{0:T(1024)S(1)}, f32[1024]{0:T(1024)}, u32[]{:S(2)}) copy-start(f32[1024]{0:T(1024)} %refs_6_.1) | copy-start | bytes 12292
  0.0 13.7 %collective-permute-start.3 = (bf16[1280,640]{1,0:T(8,128)(2,1)}, bf16[1280,640]{1,0:T(8,128)(2,1)S(1)}, u32[]{:S(2)}, u32[]{:S(2)}) collective-permute-start(bf16[1280,640]{1,0:T(8,128)(2,1)} %w_fc1.1), channel_id=1, source_target_pairs={{0,1},{1,0},{2,3},{3,2},{4,5},{5,4},{6,7},{7,6},{8,9},{9,8},{10,11... | collective-permute-start | bytes 4915208 | tf_op jit(solution)/shard_map/ppermute | solution.py:74
  0.5 13.2 %collective-permute-start.4 = (bf16[640,1024]{1,0:T(8,128)(2,1)}, bf16[640,1024]{1,0:T(8,128)(2,1)S(1)}, u32[]{:S(2)}, u32[]{:S(2)}) collective-permute-start(bf16[640,1024]{1,0:T(8,128)(2,1)} %w_mine.1), channel_id=1, source_target_pairs={{0,1},{1,0},{2,3},{3,2},{4,5},{5,4},{6,7},{7,6},{8,9},{9,8},{10,11... | collective-permute-start | bytes 3932168 | tf_op jit(solution)/shard_map/ppermute | solution.py:74
  2.4 5.7 %collective-permute-start = (bf16[8,1280]{1,0:T(8,128)(2,1)S(1)}, bf16[8,1280]{1,0:T(8,128)(2,1)S(1)}, u32[]{:S(2)}, u32[]{:S(2)}) collective-permute-start(bf16[8,1280]{1,0:T(8,128)(2,1)S(1)} %get-tuple-element.44), channel_id=1, source_target_pairs={{0,4},{4,0},{8,12},{12,8},{1,5},{5,1},{9,13},{13,9},{2,6},{6,2},{1... | collective-permute-start | bytes 61448 | tf_op jit(solution)/shard_map/ppermute | solution.py:74
  5.5 4.8 %collective-permute-start.1 = (bf16[8,1280]{1,0:T(8,128)(2,1)S(1)}, bf16[8,1280]{1,0:T(8,128)(2,1)S(1)}, u32[]{:S(2)}, u32[]{:S(2)}) collective-permute-start(bf16[8,1280]{1,0:T(8,128)(2,1)S(1)} %get-tuple-element.45), channel_id=1, source_target_pairs={{0,8},{4,12},{8,0},{12,4},{1,9},{5,13},{9,1},{13,5},{2,10},{6,14},... | collective-permute-start | bytes 61448 | tf_op jit(solution)/shard_map/ppermute | solution.py:74
  8.1 5.6 %collective-permute-start.2 = (bf16[8,1280]{1,0:T(8,128)(2,1)S(1)}, bf16[8,1280]{1,0:T(8,128)(2,1)S(1)}, u32[]{:S(2)}, u32[]{:S(2)}) collective-permute-start(bf16[8,1280]{1,0:T(8,128)(2,1)S(1)} %get-tuple-element.46), channel_id=1, source_target_pairs={{0,12},{4,8},{8,4},{12,0},{1,13},{5,9},{9,5},{13,1},{2,14},{6,10},... | collective-permute-start | bytes 61448 | tf_op jit(solution)/shard_map/ppermute | solution.py:74
  8.1 5.6 %collective-permute-start.5 = (f32[1024]{0:T(1024)S(1)}, f32[1024]{0:T(1024)S(1)}, u32[]{:S(2)}, u32[]{:S(2)}) collective-permute-start(f32[1024]{0:T(1024)S(1)} %copy-done.2), channel_id=1, source_target_pairs={{0,1},{1,0},{2,3},{3,2},{4,5},{5,4},{6,7},{7,6},{8,9},{9,8},{10,11... | collective-permute-start | bytes 12296 | tf_op jit(solution)/shard_map/ppermute | solution.py:74
  13.7 6.0 %collective-permute-start.6 = (bf16[32,1280]{1,0:T(8,128)(2,1)S(1)}, bf16[32,1280]{1,0:T(8,128)(2,1)S(1)}, u32[]{:S(2)}, u32[]{:S(2)}) collective-permute-start(bf16[32,1280]{1,0:T(8,128)(2,1)S(1)} %pad_maximum_fusion.mine), channel_id=1, source_target_pairs={{0,2},{2,0},{1,3},{3,1},{4,6},{6,4},{5,7},{7,5},{8,10},{10,8},{9,1... | collective-permute-start | bytes 245768 | tf_op jit(solution)/shard_map/ppermute | solution.py:74
  15.2 5.1 %collective-permute-start.7 = (bf16[256,256]{1,0:T(8,128)(2,1)S(1)}, bf16[256,256]{1,0:T(8,128)(2,1)S(1)}, u32[]{:S(2)}, u32[]{:S(2)}) collective-permute-start(bf16[256,256]{1,0:T(8,128)(2,1)S(1)} %get-tuple-element.57), channel_id=1, source_target_pairs={{0,4},{4,0},{8,12},{12,8},{1,5},{5,1},{9,13},{13,9},{2,6},{6,2},{1... | collective-permute-start | bytes 393224 | tf_op jit(solution)/shard_map/ppermute | solution.py:74
  15.2 16.2 %collective-permute-start.11 = (bf16[256,256]{1,0:T(8,128)(2,1)S(1)}, bf16[256,256]{1,0:T(8,128)(2,1)S(1)}, u32[]{:S(2)}, u32[]{:S(2)}) collective-permute-start(bf16[256,256]{1,0:T(8,128)(2,1)S(1)} %get-tuple-element.62), channel_id=1, source_target_pairs={{0,8},{4,12},{8,0},{12,4},{1,9},{5,13},{9,1},{13,5},{2,10},{6,14},... | collective-permute-start | bytes 393224 | tf_op jit(solution)/shard_map/ppermute | solution.py:74
  16.1 15.4 %collective-permute-start.12 = (bf16[256,256]{1,0:T(8,128)(2,1)S(1)}, bf16[256,256]{1,0:T(8,128)(2,1)S(1)}, u32[]{:S(2)}, u32[]{:S(2)}) collective-permute-start(bf16[256,256]{1,0:T(8,128)(2,1)S(1)} %get-tuple-element.63), channel_id=1, source_target_pairs={{0,12},{4,8},{8,4},{12,0},{1,13},{5,9},{9,5},{13,1},{2,14},{6,10},... | collective-permute-start | bytes 393224 | tf_op jit(solution)/shard_map/ppermute | solution.py:74
  19.7 16.0 %copy-start = (bf16[640,1024]{1,0:T(8,128)(2,1)S(1)}, bf16[640,1024]{1,0:T(8,128)(2,1)}, u32[]{:S(2)}) copy-start(bf16[640,1024]{1,0:T(8,128)(2,1)} %w_mine.1) | copy-start | bytes 3932164
  20.4 6.0 %collective-permute-start.8 = (bf16[32,640]{1,0:T(8,128)(2,1)S(1)}, bf16[32,640]{1,0:T(8,128)(2,1)S(1)}, u32[]{:S(2)}, u32[]{:S(2)}) collective-permute-start(bf16[32,640]{1,0:T(8,128)(2,1)S(1)} %get-tuple-element.59), channel_id=1, source_target_pairs={{0,4},{4,0},{8,12},{12,8},{1,5},{5,1},{9,13},{13,9},{2,6},{6,2},{1... | collective-permute-start | bytes 122888 | tf_op jit(solution)/shard_map/ppermute | solution.py:74
  21.1 10.2 %collective-permute-start.9 = (bf16[32,640]{1,0:T(8,128)(2,1)S(1)}, bf16[32,640]{1,0:T(8,128)(2,1)S(1)}, u32[]{:S(2)}, u32[]{:S(2)}) collective-permute-start(bf16[32,640]{1,0:T(8,128)(2,1)S(1)} %get-tuple-element.60), channel_id=1, source_target_pairs={{0,8},{4,12},{8,0},{12,4},{1,9},{5,13},{9,1},{13,5},{2,10},{6,14},... | collective-permute-start | bytes 122888 | tf_op jit(solution)/shard_map/ppermute | solution.py:74
  21.6 9.6 %collective-permute-start.10 = (bf16[32,640]{1,0:T(8,128)(2,1)S(1)}, bf16[32,640]{1,0:T(8,128)(2,1)S(1)}, u32[]{:S(2)}, u32[]{:S(2)}) collective-permute-start(bf16[32,640]{1,0:T(8,128)(2,1)S(1)} %get-tuple-element.61), channel_id=1, source_target_pairs={{0,12},{4,8},{8,4},{12,0},{1,13},{5,9},{9,5},{13,1},{2,14},{6,10},... | collective-permute-start | bytes 122888 | tf_op jit(solution)/shard_map/ppermute | solution.py:74
  31.5 30.9 %copy-start.1 = (s32[4,4]{1,0:T(4,128)S(1)}, s32[4,4]{1,0:T(4,128)}, u32[]{:S(2)}) copy-start(s32[4,4]{1,0:T(4,128)} %refs_4_.1) | copy-start | bytes 196
  31.6 17.8 %collective-permute-start.18 = (bf16[1024,256]{1,0:T(8,128)(2,1)S(1)}, bf16[1024,256]{1,0:T(8,128)(2,1)S(1)}, u32[]{:S(2)}, u32[]{:S(2)}) collective-permute-start(bf16[1024,256]{1,0:T(8,128)(2,1)S(1)} %constant_dynamic-update-slice_fusion.refs_4_), channel_id=1, source_target_pairs={{0,1},{1,0},{2,3},{3,2},{4,5},{5,4},{6,7},{7,6},{8,9},{9,8},{10,11... | collective-permute-start | bytes 1572872 | tf_op jit(solution)/shard_map/ppermute | solution.py:74
  31.6 4.1 %collective-permute-start.14 = (bf16[32,640]{1,0:T(8,128)(2,1)S(1)}, bf16[32,640]{1,0:T(8,128)(2,1)S(1)}, u32[]{:S(2)}, u32[]{:S(2)}) collective-permute-start(bf16[32,640]{1,0:T(8,128)(2,1)S(1)} %fusion.2), channel_id=1, source_target_pairs={{0,2},{2,10},{4,0},{6,8},{8,6},{10,14},{12,4},{14,12},{1,3},{3,11}... | collective-permute-start | bytes 122888 | tf_op jit(solution)/shard_map/ppermute | solution.py:311
  32.2 3.5 %collective-permute-start.13 = (bf16[32,640]{1,0:T(8,128)(2,1)S(1)}, bf16[32,640]{1,0:T(8,128)(2,1)S(1)}, u32[]{:S(2)}, u32[]{:S(2)}) collective-permute-start(bf16[32,640]{1,0:T(8,128)(2,1)S(1)} %fusion.2), channel_id=1, source_target_pairs={{0,0},{2,8},{4,2},{6,10},{8,4},{10,12},{12,6},{14,14},{1,1},{3,9},... | collective-permute-start | bytes 122888 | tf_op jit(solution)/shard_map/ppermute | solution.py:311
  36.5 7.6 %collective-permute-start.15 = (bf16[64,512]{1,0:T(8,128)(2,1)S(1)}, bf16[64,512]{1,0:T(8,128)(2,1)S(1)}, u32[]{:S(2)}, u32[]{:S(2)}) collective-permute-start(bf16[64,512]{1,0:T(8,128)(2,1)S(1)} %get-tuple-element.67), channel_id=1, source_target_pairs={{0,4},{4,0},{8,12},{12,8},{1,5},{5,1},{9,13},{13,9},{2,6},{6,2},{1... | collective-permute-start | bytes 196616 | tf_op jit(solution)/shard_map/ppermute | solution.py:74
  40.4 7.4 %collective-permute-start.16 = (bf16[64,512]{1,0:T(8,128)(2,1)S(1)}, bf16[64,512]{1,0:T(8,128)(2,1)S(1)}, u32[]{:S(2)}, u32[]{:S(2)}) collective-permute-start(bf16[64,512]{1,0:T(8,128)(2,1)S(1)} %get-tuple-element.68), channel_id=1, source_target_pairs={{0,8},{4,12},{8,0},{12,4},{1,9},{5,13},{9,1},{13,5},{2,10},{6,14},... | collective-permute-start | bytes 196616 | tf_op jit(solution)/shard_map/ppermute | solution.py:74
  43.2 6.1 %collective-permute-start.17 = (bf16[64,512]{1,0:T(8,128)(2,1)S(1)}, bf16[64,512]{1,0:T(8,128)(2,1)S(1)}, u32[]{:S(2)}, u32[]{:S(2)}) collective-permute-start(bf16[64,512]{1,0:T(8,128)(2,1)S(1)} %get-tuple-element.69), channel_id=1, source_target_pairs={{0,12},{4,8},{8,4},{12,0},{1,13},{5,9},{9,5},{13,1},{2,14},{6,10},... | collective-permute-start | bytes 196616 | tf_op jit(solution)/shard_map/ppermute | solution.py:74
  49.6 4.4 %collective-permute-start.19 = (bf16[32,1152]{1,0:T(8,128)(2,1)S(1)}, bf16[32,1152]{1,0:T(8,128)(2,1)S(1)}, u32[]{:S(2)}, u32[]{:S(2)}) collective-permute-start(bf16[32,1152]{1,0:T(8,128)(2,1)S(1)} %get-tuple-element.76), channel_id=1, source_target_pairs={{0,2},{2,0},{1,3},{3,1},{4,6},{6,4},{5,7},{7,5},{8,10},{10,8},{9,1... | collective-permute-start | bytes 221192 | tf_op jit(solution)/shard_map/ppermute | solution.py:74
  54.1 4.5 %collective-permute-start.20 = (f32[8,1152]{1,0:T(8,128)S(1)}, f32[8,1152]{1,0:T(8,128)S(1)}, u32[]{:S(2)}, u32[]{:S(2)}) collective-permute-start(f32[8,1152]{1,0:T(8,128)S(1)} %get-tuple-element.78), channel_id=1, source_target_pairs={{0,4},{4,0},{8,12},{12,8},{1,5},{5,1},{9,13},{13,9},{2,6},{6,2},{1... | collective-permute-start | bytes 110600 | tf_op jit(solution)/shard_map/ppermute | solution.py:74
  54.3 4.9 %collective-permute-start.21 = (f32[8,1152]{1,0:T(8,128)S(1)}, f32[8,1152]{1,0:T(8,128)S(1)}, u32[]{:S(2)}, u32[]{:S(2)}) collective-permute-start(f32[8,1152]{1,0:T(8,128)S(1)} %get-tuple-element.79), channel_id=1, source_target_pairs={{0,8},{4,12},{8,0},{12,4},{1,9},{5,13},{9,1},{13,5},{2,10},{6,14},... | collective-permute-start | bytes 110600 | tf_op jit(solution)/shard_map/ppermute | solution.py:74
  56.7 5.8 %collective-permute-start.22 = (f32[8,1152]{1,0:T(8,128)S(1)}, f32[8,1152]{1,0:T(8,128)S(1)}, u32[]{:S(2)}, u32[]{:S(2)}) collective-permute-start(f32[8,1152]{1,0:T(8,128)S(1)} %get-tuple-element.80), channel_id=1, source_target_pairs={{0,12},{4,8},{8,4},{12,0},{1,13},{5,9},{9,5},{13,1},{2,14},{6,10},... | collective-permute-start | bytes 110600 | tf_op jit(solution)/shard_map/ppermute | solution.py:74

commit v3 on v2

--- a/solution.py
+++ b/solution.py
@@ -74,6 +74,11 @@
     return lax.ppermute(x, axis, [(i, i ^ step) for i in range(n)])
 
 
+def exchange(parts):
+    n = len(parts)
+    return [swap(parts[k], "hold", n, k) for k in range(n - 1, 0, -1)] + [parts[0]]
+
+
 def call(body, outs, *args, flops=0, scratch=(), **specs):
     moved = sum(x.size * x.dtype.itemsize for x in args)
     return pl.pallas_call(
@@ -90,66 +95,112 @@
     return jnp.dot(a, b, preferred_element_type=jnp.float32)
 
 
-def norm_kernel(cache, ln_gain, matching, counts, w_fc1, w_key, *refs):
-    outs, w_held, key_rows = refs[:4], refs[4], refs[5:9]
-    x_in, gain_in, plan_in, live_in, held, sems = refs[9:]
-    n = len(outs)
+def norm_rows(cache, gain, matching, held):
     h = lax.axis_index("hold")
-    share = key_rows[0].shape[0]
-    pairs = [(cache, x_in), (ln_gain, gain_in), (matching, plan_in), (counts, live_in)]
-    for s in range(n):
-        start = pl.multiple_of((h ^ s) * share, 128)
-        pairs.append((w_key.at[pl.ds(start, share)], key_rows[s]))
-    pairs.append((w_fc1, w_held))
-    copies = [pltpu.make_async_copy(a, b, sems.at[i]) for i, (a, b) in enumerate(pairs)]
-    for copy in copies:
-        copy.start()
-    for copy in copies[:4]:
-        copy.wait()
     _, rounds, block, depth = cache.shape
-    width = ln_gain.shape[0]
-    chunk = depth // n
-    gain = gain_in[...].reshape(1, width)
+    width = gain.shape[1]
     column = lax.broadcasted_iota(jnp.int32, matching.shape, 1) == h
-    owner = jnp.sum(jnp.where(column, plan_in[...], 0), axis=1, keepdims=True)
-    b_of = lax.broadcasted_iota(jnp.int32, (block, 1), 0)
+    owner = jnp.sum(jnp.where(column, matching[...], 0), axis=1, keepdims=True)
     for p in range(depth // width):
         cols = pl.ds(p * width, width)
         normed = []
         for r in range(rounds):
-            x = x_in[0, r, :, cols].astype(jnp.float32)
+            x = cache[0, r, :, cols].astype(jnp.float32)
             scale = lax.rsqrt(jnp.mean(x * x, axis=1, keepdims=True) + EPSILON)
-            scale = jnp.where(b_of < live_in[:, r : r + 1], scale, 0.0)
             normed.append(x * scale * gain)
         for j in range(rounds):
             picked = sum(
                 jnp.where(owner[r : r + 1] == j, normed[r], 0.0) for r in range(rounds)
             )
             held[j * block : (j + 1) * block, cols] = picked
-    for s in range(n):
-        start = pl.multiple_of((h ^ s) * chunk, 128)
-        outs[s][...] = held[:, pl.ds(start, chunk)].astype(jnp.bfloat16)
-    for copy in copies[4:]:
+
+
+def own_kernel(cache, ln_gain, matching, w_fc1, w_fc2, w_key, *refs):
+    out, held_1, held_2, *key_rows = refs[:6]
+    x_in, gain_in, plan_in, sems = refs[6:]
+    h, grp = lax.axis_index("hold"), lax.axis_index("grp")
+    pairs = [(cache, x_in), (ln_gain, gain_in), (matching, plan_in), (w_fc1, held_1), (w_fc2, held_2)]
+    share = key_rows[0].shape[0]
+    for place, end in zip((h, h ^ 1, h ^ 3 ^ grp), key_rows, strict=True):
+        pairs.append((w_key.at[pl.ds(pl.multiple_of(place * share, 128), share)], end))
+    copies = [pltpu.make_async_copy(a, b, sems.at[i]) for i, (a, b) in enumerate(pairs)]
+    for copy in copies:
+        copy.start()
+    for copy in copies[:3]:
         copy.wait()
-
-
-def first_kernel(mine, other, *refs):
-    weights, outs = refs[:2], refs[2:6]
-    rows, sums = refs[6:]
+    norm_rows(x_in, gain_in[...].reshape(1, -1), plan_in, out)
+    for copy in copies[3:]:
+        copy.wait()
+
+
+def both_kernel(own, cache, ln_gain, matching, *refs):
+    outs, held = refs[:4], refs[4]
+    h = lax.axis_index("hold")
+    norm_rows(cache, ln_gain[...].reshape(1, -1), matching, held)
+    chunk = outs[0].shape[1]
+    for s, out in enumerate(outs):
+        cols = pl.ds(pl.multiple_of((h ^ s) * chunk, 128), chunk)
+        out[...] = jnp.concatenate([own[:, cols], held[:, cols]], axis=0).astype(jnp.bfloat16)
+
+
+def first_kernel(*refs):
+    pieces, weights, outs = refs[3::-1], refs[4:6], refs[6:10]
+    rows, sums = refs[10:]
     h, rep = lax.axis_index("hold"), lax.axis_index("rep")
-    half = mine.shape[0]
-    size = half // 4
-    for b, part in enumerate((mine, other)):
-        part = part[...].astype(jnp.float32)
-        for s in range(4):
-            start = pl.multiple_of(b * half + (h ^ s) * size, 8)
-            rows[pl.ds(start, size), :] = part[s * size : (s + 1) * size]
+    size = pieces[0].shape[0] // 2
+    half = 4 * size
+    for k, piece in enumerate(pieces):
+        part = piece[...].astype(jnp.float32)
+        for b in range(2):
+            start = pl.multiple_of(b * half + (h ^ k) * size, 8)
+            rows[pl.ds(start, size), :] = part[b * size : (b + 1) * size]
     x = rows[...].astype(jnp.bfloat16)
     for i, weight in enumerate(weights):
         sums[rep ^ i] = dot(x, weight[...])
     for k, out in enumerate(outs):
         start = pl.multiple_of(((h ^ k) & 1) * half, 16)
         out[...] = sums[(h ^ k) >> 1, pl.ds(start, half), :].astype(jnp.bfloat16)
+
+
+ERFC_NEAR = (
+    2.326819970068386e-2,
+    -1.387039388740657e-1,
+    3.687424674597105e-1,
+    -5.824733027278666e-1,
+    6.210004621745983e-1,
+    -4.944515323274145e-1,
+    3.404879937665872e-1,
+    -2.741127028184656e-1,
+    5.638259427386472e-1,
+)
+ERFC_FAR = (
+    -1.047766399936249e1,
+    1.297719955372516e1,
+    -7.495518717768503e0,
+    2.921019019210786e0,
+    -1.015265279202700e0,
+    4.218463358204948e-1,
+    -2.820767439740514e-1,
+    5.641895067754075e-1,
+)
+
+
+def erfc(x):
+    size = jnp.maximum(jnp.abs(x), 1.0)
+    inverse = 1.0 / size
+    square = inverse * inverse
+    near, far = jnp.zeros_like(x), jnp.zeros_like(x)
+    for c in ERFC_NEAR:
+        near = near * square + c
+    for c in ERFC_FAR:
+        far = far * square + c
+    tail = jnp.exp(-size * size) * inverse * jnp.where(size < 2.0, near, far)
+    return jnp.where(jnp.abs(x) < 1.0, 1.0 - lax.erf(x), jnp.where(x < 0, 2.0 - tail, tail))
+
+
+def gelu_kernel(*refs):
+    x = sum(part[...].astype(jnp.float32) for part in refs[:4])
+    refs[4][...] = (0.5 * x * erfc(-x * 0.5**0.5)).astype(jnp.bfloat16)
 
 
 def second_kernel(first, second, w_mine, w_other, *refs):
@@ -176,58 +227,76 @@
             outs[k][:, p * cols : (p + 1) * cols] = part
 
 
+def two_terms(x):
+    high = x.astype(jnp.bfloat16).astype(jnp.float32)
+    lane = lax.broadcasted_iota(jnp.int32, (x.shape[0], 128), 1)
+    return jnp.where(lane < 64, high, x - high)
+
+
 def key_kernel(*refs):
     parts, blocks, gains = refs[:4], refs[4:6], refs[6:8]
     kept, sent, held = refs[8:]
-    h = lax.axis_index("hold")
+    h, grp = lax.axis_index("hold"), lax.axis_index("grp")
     merged = sum(part[...].astype(jnp.float32) for part in parts)
     squares = jnp.sum(merged * merged, axis=1, keepdims=True)
     cols = merged.shape[1] // 2
     start = pl.multiple_of(h * cols, 128)
-    features = []
+    rows = []
     for p in range(2):
         gain = gains[p][pl.ds(start, cols)].reshape(1, cols)
-        features.append((merged[:, p * cols : (p + 1) * cols] * gain).astype(jnp.bfloat16))
+        rows.append((merged[:, p * cols : (p + 1) * cols] * gain).astype(jnp.bfloat16))
     width = blocks[0].shape[1]
-    for s in range(4):
-        start = pl.multiple_of((h ^ s) * width, 128)
-        held[:, pl.ds(start, width)] = sum(
-            dot(features[p], blocks[p][s * cols : (s + 1) * cols, :]) for p in range(2)
+    for i, place in enumerate((h, h ^ 1, h ^ 3 ^ grp, h ^ 2 ^ grp)):
+        held[:, pl.ds(pl.multiple_of(place * width, 128), width)] = sum(
+            dot(rows[p], blocks[p][i * cols : (i + 1) * cols, :]) for p in range(2)
         )
     half = kept.shape[0]
     keys = 4 * width
     kept[:, :keys] = held[:half, :]
     kept[:, keys:] = jnp.broadcast_to(squares[:half], (half, 128))
     sent[:, :keys] = held[half:, :].astype(jnp.bfloat16)
-    high = squares[half:].astype(jnp.bfloat16).astype(jnp.float32)
-    lane = lax.broadcasted_iota(jnp.int32, (half, 128), 1)
-    pair = jnp.where(lane < 64, high, squares[half:] - high)
-    sent[:, keys:] = pair.astype(jnp.bfloat16)
-
-
-def group_kernel(kept, came, *refs):
+    sent[:, keys:] = two_terms(squares[half:]).astype(jnp.bfloat16)
+
+
+def group_kernel(kept, came, matching, counts, *refs):
     outs, held = refs[:4], refs[4]
     h = lax.axis_index("hold")
     keys = kept.shape[1] - 128
     held[:, :keys] = kept[:, :keys] + came[:, :keys].astype(jnp.float32)
     pair = came[:, keys:].astype(jnp.float32)
-    squares = kept[:, keys:] + pair[:, :1] + pair[:, 127:]
-    held[:, keys:] = squares
+    held[:, keys:] = two_terms(kept[:, keys : keys + 1] + pair[:, :1] + pair[:, 127:])
     rows = outs[0].shape[0]
+    rounds = matching.shape[0]
+    column = lax.broadcasted_iota(jnp.int32, matching.shape, 1) == h
+    owner = jnp.sum(jnp.where(column, matching[...], 0), axis=1, keepdims=True)
+    lane = lax.broadcasted_iota(jnp.int32, (rows, 128), 1)
     for k in range(4):
-        outs[k][...] = held[pl.ds(pl.multiple_of((h ^ k) * rows, 8), rows), :]
+        part = held[pl.ds(pl.multiple_of((h ^ k) * rows, 8), rows), :]
+        live = sum(
+            jnp.where(owner[r : r + 1] == (h ^ k), counts[:, r : r + 1], 0) for r in range(rounds)
+        )
+        tail = jnp.where(lane == 32, live.astype(jnp.float32), part[:, keys:])
+        outs[k][:, :keys] = part[:, :keys].astype(jnp.bfloat16)
+        outs[k][:, keys:] = tail.astype(jnp.bfloat16)
 
 
 def last_kernel(width, *refs):
-    parts, matching, out = refs[:4], refs[4], refs[5]
+    parts, matching, out, held = refs[3::-1], refs[4], refs[5], refs[6]
     h = lax.axis_index("hold")
-    total = sum(part[...] for part in parts)
-    keys = total[:, :-128] * lax.rsqrt(total[:, -1:] / width + EPSILON)
-    _, rounds, block, _ = out.shape
+    _, rounds, block, features = out.shape
+    total = sum(part[...].astype(jnp.float32) for part in parts)
+    squares = total[:, features : features + 1] + total[:, -1:]
+    keys = total[:, :features] * lax.rsqrt(squares / width + EPSILON)
+    for k, part in enumerate(parts):
+        held[pl.ds(h ^ k, 1), :] = part[:1, features:].astype(jnp.float32)
+    b_of = lax.broadcasted_iota(jnp.int32, (block, 1), 0).astype(jnp.float32)
+    blocks = []
+    for i in range(rounds):
+        live = held[i : i + 1, 32:33]
+        blocks.append(jnp.where(b_of < live, keys[i * block : (i + 1) * block], 0.0))
     for r in range(rounds):
         picked = sum(
-            jnp.where(matching[r : r + 1, i : i + 1] == h, keys[i * block : (i + 1) * block], 0.0)
-            for i in range(rounds)
+            jnp.where(matching[r : r + 1, i : i + 1] == h, blocks[i], 0.0) for i in range(rounds)
         )
         out[0, r] = picked.astype(jnp.bfloat16)
 
@@ -245,63 +314,65 @@
     def like(dims, kind=bf16):
         return jax.ShapeDtypeStruct(dims, kind)
 
+    cache_other = swap(cache, "tp", 2, 1)
     w_fc1_other = swap(w_fc1, "rep", 2, 1)
-    w_fc2_other = swap(w_fc2, "rep", 2, 1)
     gain_other = swap(norm_gain, "rep", 2, 1)
-    counts = counts.reshape(1, rounds)
-    cache_in, w_fc1_in, w_key_in, ln_in, matching_in, counts_in = (
+    cache_in, w_fc1_in, w_fc2_in, w_key_in, ln_in, matching_in = (
         pltpu.with_memory_space_constraint(x, pltpu.HBM)
-        for x in (cache, w_fc1, w_key, ln_gain, matching, counts)
-    )
-    *chunks, w_fc1_mine, key_0, key_1, key_2, key_3 = call(
-        norm_kernel,
-        [like((rows, chunk))] * n + [like(w_fc1.shape)] + [like((share, key_cols))] * n,
+        for x in (cache, w_fc1, w_fc2, w_key, ln_gain, matching)
+    )
+    own, w_fc1_mine, w_fc2_mine, key_0, key_1, key_far = call(
+        own_kernel,
+        [like((rows, depth), f32), like(w_fc1.shape), like(w_fc2.shape)]
+        + [like((share, key_cols))] * 3,
         cache_in,
         ln_in,
         matching_in,
-        counts_in,
         w_fc1_in,
+        w_fc2_in,
         w_key_in,
         in_specs=[pl.BlockSpec(memory_space=pltpu.HBM)] * 6,
         scratch=[
             vmem(cache.shape, bf16),
             vmem(ln_gain.shape, f32),
             vmem(matching.shape, jnp.int32),
-            vmem(counts.shape, jnp.int32),
-            vmem((rows, depth), f32),
-            pltpu.SemaphoreType.DMA((9,)),
+            pltpu.SemaphoreType.DMA((8,)),
         ],
-    )
-    group_rows = jnp.concatenate(
-        [swap(chunks[s], "hold", n, s) if s else chunks[s] for s in range(n)], axis=0
-    )
-    group_rows, w_fc1_other, w_fc2_other, gain_other, key_1, key_2, key_3 = (
-        lax.optimization_barrier(
-            (group_rows, w_fc1_other, w_fc2_other, gain_other, key_1, key_2, key_3)
-        )
-    )
-    key_1, key_2, key_3 = (
-        swap(part, "hold", n, s + 1) for s, part in enumerate((key_1, key_2, key_3))
-    )
-
+        flops=8 << 30,
+    )
+    key_1 = swap(key_1, "hold", n, 1)
+    perm = [(n * g + a, n * g + (a ^ 3 ^ g)) for g in range(2) for a in range(n)]
+    key_far = lax.ppermute(key_far, ("grp", "hold"), perm)
+    own, cache_other, w_fc1_other, gain_other = lax.optimization_barrier(
+        (own, cache_other, w_fc1_other, gain_other)
+    )
+    pieces = call(
+        both_kernel,
+        [like((2 * rows, chunk))] * n,
+        own,
+        cache_other,
+        ln_gain,
+        matching,
+        scratch=[vmem((rows, depth), f32)],
+        flops=8 << 30,
+    )
+    pieces = exchange(pieces)
     partial = call(
         first_kernel,
         [like((4 * rows, hidden_cols))] * n,
-        group_rows,
-        swap(group_rows, "tp", 2, 1),
+        *pieces,
         w_fc1_mine,
         w_fc1_other,
         scratch=[vmem((8 * rows, chunk), f32), vmem((2, 8 * rows, hidden_cols), f32)],
         flops=32 * rows * w_fc1.size,
     )
-    *partial, key_1 = lax.optimization_barrier((*partial, key_1))
-    parts = [swap(partial[k], "hold", n, k) if k else partial[k] for k in range(n)]
-    product = sum(part.astype(f32) for part in parts)
-    hidden = jax.nn.gelu(product, approximate=False).astype(bf16)
-
-    hidden, key_2, key_3 = lax.optimization_barrier((hidden, key_2, key_3))
-    key_mine = jnp.concatenate([key_0, key_1, key_2, key_3])
-    key_other = swap(key_mine, "rep", 2, 1)
+    *partial, key_1, key_far, w_fc2_sent = lax.optimization_barrier(
+        (*partial, key_1, key_far, w_fc2_mine)
+    )
+    w_fc2_other = swap(w_fc2_sent, "rep", 2, 1)
+    parts = exchange(partial)
+    key_near = swap(key_far, "grp", 2, 1)
+    hidden = call(gelu_kernel, like(parts[0].shape), *parts, flops=8 << 30)
 
     halves = []
     for g in range(2):
@@ -314,13 +385,15 @@
         second_kernel,
         [like((8 * rows, 2 * share))] * n,
         *halves,
-        w_fc2,
+        w_fc2_mine,
         w_fc2_other,
         scratch=[vmem((2, 8 * rows, out_cols), f32)],
         flops=32 * rows * w_fc2.size,
     )
-    merged = [swap(merged[k], "hold", n, k) if k else merged[k] for k in range(n)]
-
+    *merged, key_near = lax.optimization_barrier((*merged, key_near))
+    key_mine = jnp.concatenate([key_0, key_1, key_far, key_near])
+    key_other = swap(key_mine, "rep", 2, 1)
+    merged = exchange(merged)
     kept, sent = call(
         key_kernel,
         [like((4 * rows, n * key_cols + 128), f32), like((4 * rows, n * key_cols + 128))],
@@ -334,17 +407,20 @@
     )
     keys = call(
         group_kernel,
-        [like((rows, n * key_cols + 128), f32)] * n,
+        [like((rows, n * key_cols + 128))] * n,
         kept,
         swap(sent, "tp", 2, 1),
+        matching,
+        counts.reshape(1, rounds),
         scratch=[vmem((4 * rows, n * key_cols + 128), f32)],
     )
-    keys = [swap(keys[k], "hold", n, k) if k else keys[k] for k in range(n)]
+    keys = exchange(keys)
     return call(
         functools.partial(last_kernel, width),
         like((1, rounds, block, n * key_cols)),
         *keys,
         matching,
+        scratch=[vmem((rounds, 128), f32)],
     )
 
 

time: 63.4 us -> 59 us (0.931)
  waiting for transfers between devices: 27.5 us -> 19.9 us
  starting transfers between devices: 30.9 us -> 33.6 us
  Pallas kernels: 4.45 us -> 5.16 us
    ppermute x21 -> x20, waiting for transfers between devices: 24.6 us -> 17.1 us  [swap(): return lax.ppermute(x, axis, [(i, i ^ step) for i in range(n)])]
    ppermute x0 -> x1, starting transfers between devices: none -> 2.47 us  [rows_past_weights(): key_far = lax.ppermute(key_far, ('grp', 'hold'), perm)]
    pallas_call x6 -> x8, Pallas kernels: 4.45 us -> 5.16 us  [call(): pl.pallas_call(body, out_shape=outs, scratch_shapes=scratch, cost_estimat...]
    ppermute x21 -> x20, starting transfers between devices: 29.7 us -> 29.9 us  [swap(): return lax.ppermute(x, axis, [(i, i ^ step) for i in range(n)])]
  transfers between devices with their start and end apart: 23 -> 23, of which waited for: 10 -> 10; matrix products, arithmetic and copies ran while one was open for 0% -> 0% of each run, Pallas kernels for 5% -> 7%
where the time goes in v3:
time: 59 us; the launch traced here: 58.9 us
  starting transfers between devices  33.6 us (57%)
  waiting for transfers between devices  19.9 us (34%)
  Pallas kernels  5.16 us (9%)
    ppermute x20, starting transfers between devices, swap(): return lax.ppermute(x, axis, [(i, i ^ step) for i in range(n)])  29.9 us
    ppermute x20, waiting for transfers between devices, swap(): return lax.ppermute(x, axis, [(i, i ^ step) for i in range(n)])  17.1 us
    pallas_call x8, Pallas kernels, call(): pl.pallas_call(body, out_shape=outs, scratch_shapes=scratch, cost_estimat...  5.16 us
    ppermute x2, waiting for transfers between devices, rows_past_weights(): halves.append(lax.ppermute(hidden, ('hold', 'tp'), perm))  2.78 us
    ppermute x1, starting transfers between devices, rows_past_weights(): key_far = lax.ppermute(key_far, ('grp', 'hold'), perm)  2.47 us
    ppermute x2, starting transfers between devices, rows_past_weights(): halves.append(lax.ppermute(hidden, ('hold', 'tp'), perm))  1.24 us
  transfers between devices with their start and end apart: 23, of which 10 were waited for; matrix products, arithmetic and copies ran while one was open for 0% of the time, Pallas kernels for 7%

profile of v3, /device:TPU:0, one launch (start us, length us, event | category | flops | bytes accessed | tf_op | source)
XLA Modules:
  0.0 58.9 jit_solution(5266857578117354772)
XLA Ops:
  0.0 0.0 copy-start
  0.0 0.0 copy-start.3
  0.0 0.5 collective-permute-start.1
  0.5 0.1 collective-permute-start.2
  0.5 2.9 %collective-permute-start = (bf16[1,4,2,5120]{3,2,1,0:T(2,128)(2,1)}, bf16[1,4,2,5120]{3,2,1,0:T(2,128)(2,1)S(1)}, u32[]{:S(2)}, u32[]{:S(2)}) collective-permute-start(bf16[1,4,2,5120]{3,2,1,0:T(2,128)(2,1)} %cache.1), channel_id=1, source_target_pairs={{0,2},{2,0},{1,3},{3,1},{4,6},{6,4},{5,7},{7,5},{8,10},{10,8},{9,1... | collective-permute-start | bytes 245768 | tf_op jit(solution)/shard_map/ppermute | solution.py:74
  3.5 2.0 %shard_map.82 = (f32[8,5120]{1,0:T(8,128)S(1)}, bf16[1280,640]{1,0:T(8,128)(2,1)S(1)}, bf16[640,1024]{1,0:T(8,128)(2,1)S(1)}, bf16[256,256]{1,0:T(8,128)(2,1)S(1...) custom-call(bf16[1,4,2,5120]{3,2,1,0:T(2,128)(2,1)} %cache.1, f32[1280]{0:T(1024)} %ln_gain.3, ...), custom_call_target="tpu_custom_call" | custom-call | flops 8589934592 | bytes 3560512 | tf_op jit(solution)/shard_map/pallas_call | solution.py:84
  5.5 1.6 %collective-permute-start.6 = (bf16[256,256]{1,0:T(8,128)(2,1)S(1)}, bf16[256,256]{1,0:T(8,128)(2,1)S(1)}, u32[]{:S(2)}, u32[]{:S(2)}) collective-permute-start(bf16[256,256]{1,0:T(8,128)(2,1)S(1)} %get-tuple-element.58), channel_id=1, source_target_pairs={{0,4},{4,0},{8,12},{12,8},{1,5},{5,1},{9,13},{13,9},{2,6},{6,2},{1... | collective-permute-start | bytes 393224 | tf_op jit(solution)/shard_map/ppermute | solution.py:74
  7.1 2.5 %collective-permute-start.7 = (bf16[256,256]{1,0:T(8,128)(2,1)S(1)}, bf16[256,256]{1,0:T(8,128)(2,1)S(1)}, u32[]{:S(2)}, u32[]{:S(2)}) collective-permute-start(bf16[256,256]{1,0:T(8,128)(2,1)S(1)} %get-tuple-element.59), channel_id=1, source_target_pairs={{0,12},{4,8},{8,4},{12,0},{16,24},{20,28},{24,16},{28,20},{1,13},{... | collective-permute-start | bytes 393224 | tf_op jit(solution)/shard_map/ppermute | solution.py:345
  9.6 0.0 collective-permute-done.2.refs_7_
  9.6 0.0 collective-permute-done.cache
  9.6 0.0 collective-permute-done.1.refs_5_
  9.6 0.0 copy-done
  9.6 0.0 copy-done.3
  9.6 0.3 shard_map.83
  9.9 1.4 %collective-permute-start.3 = (bf16[16,1280]{1,0:T(8,128)(2,1)S(1)}, bf16[16,1280]{1,0:T(8,128)(2,1)S(1)}, u32[]{:S(2)}, u32[]{:S(2)}) collective-permute-start(bf16[16,1280]{1,0:T(8,128)(2,1)S(1)} %get-tuple-element.48), channel_id=1, source_target_pairs={{0,12},{4,8},{8,4},{12,0},{1,13},{5,9},{9,5},{13,1},{2,14},{6,10},... | collective-permute-start | bytes 122888 | tf_op jit(solution)/shard_map/ppermute | solution.py:74
  11.3 0.8 %collective-permute-start.4 = (bf16[16,1280]{1,0:T(8,128)(2,1)S(1)}, bf16[16,1280]{1,0:T(8,128)(2,1)S(1)}, u32[]{:S(2)}, u32[]{:S(2)}) collective-permute-start(bf16[16,1280]{1,0:T(8,128)(2,1)S(1)} %get-tuple-element.49), channel_id=1, source_target_pairs={{0,8},{4,12},{8,0},{12,4},{1,9},{5,13},{9,1},{13,5},{2,10},{6,14},... | collective-permute-start | bytes 122888 | tf_op jit(solution)/shard_map/ppermute | solution.py:74
  12.1 2.2 %collective-permute-start.5 = (bf16[16,1280]{1,0:T(8,128)(2,1)S(1)}, bf16[16,1280]{1,0:T(8,128)(2,1)S(1)}, u32[]{:S(2)}, u32[]{:S(2)}) collective-permute-start(bf16[16,1280]{1,0:T(8,128)(2,1)S(1)} %get-tuple-element.50), channel_id=1, source_target_pairs={{0,4},{4,0},{8,12},{12,8},{1,5},{5,1},{9,13},{13,9},{2,6},{6,2},{1... | collective-permute-start | bytes 122888 | tf_op jit(solution)/shard_map/ppermute | solution.py:74
  14.3 3.1 %collective-permute-done.3.refs_0_ = bf16[16,1280]{1,0:T(8,128)(2,1)S(1)} collective-permute-done((bf16[16,1280]{1,0:T(8,128)(2,1)S(1)}, bf16[16,1280]{1,0:T(8,128)(2,1)S(1)}, u32[]{:S(2)}, u32[]{:S(2)}) %collective-permute-start.3) | collective-permute-done | bytes 40992 | tf_op jit(solution)/shard_map/ppermute | solution.py:74
  17.4 1.8 %collective-permute-done.4.refs_1_ = bf16[16,1280]{1,0:T(8,128)(2,1)S(1)} collective-permute-done((bf16[16,1280]{1,0:T(8,128)(2,1)S(1)}, bf16[16,1280]{1,0:T(8,128)(2,1)S(1)}, u32[]{:S(2)}, u32[]{:S(2)}) %collective-permute-start.4) | collective-permute-done | bytes 40992 | tf_op jit(solution)/shard_map/ppermute | solution.py:74
  19.2 0.0 collective-permute-done.5.refs_2_
  19.2 0.6 %shard_map.84 = (bf16[32,640]{1,0:T(8,128)(2,1)S(1)}, bf16[32,640]{1,0:T(8,128)(2,1)S(1)}, bf16[32,640]{1,0:T(8,128)(2,1)S(1)}, bf16[32,640]{1,0:T(8,128)(2,1)S(1)}) custom-call(bf16[16,1280]{1,0:T(8,128)(2,1)S(1)} %collective-permute-done.3.refs_0_, bf16[16,1280]{1,0:T(8,128)(2,1)S(1)} %collective-permute-done.4.refs_1_, ...), custom_call_target="tpu_custom_call" | custom-call | flops 209715200 | bytes 3440640 | tf_op jit(solution)/shard_map/pallas_call | solution.py:84
  19.9 0.0 collective-permute-done.6
  19.9 0.0 collective-permute-done.7
  19.9 0.1 collective-permute-start.13
  20.0 2.7 %collective-permute-start.8 = (bf16[32,640]{1,0:T(8,128)(2,1)S(1)}, bf16[32,640]{1,0:T(8,128)(2,1)S(1)}, u32[]{:S(2)}, u32[]{:S(2)}) collective-permute-start(bf16[32,640]{1,0:T(8,128)(2,1)S(1)} %get-tuple-element.61), channel_id=1, source_target_pairs={{0,12},{4,8},{8,4},{12,0},{1,13},{5,9},{9,5},{13,1},{2,14},{6,10},... | collective-permute-start | bytes 122888 | tf_op jit(solution)/shard_map/ppermute | solution.py:74
  22.7 0.0 collective-permute-start.9
  22.7 1.7 %collective-permute-start.10 = (bf16[32,640]{1,0:T(8,128)(2,1)S(1)}, bf16[32,640]{1,0:T(8,128)(2,1)S(1)}, u32[]{:S(2)}, u32[]{:S(2)}) collective-permute-start(bf16[32,640]{1,0:T(8,128)(2,1)S(1)} %get-tuple-element.63), channel_id=1, source_target_pairs={{0,4},{4,0},{8,12},{12,8},{1,5},{5,1},{9,13},{13,9},{2,6},{6,2},{1... | collective-permute-start | bytes 122888 | tf_op jit(solution)/shard_map/ppermute | solution.py:74
  24.4 1.6 %collective-permute-start.14 = (bf16[256,256]{1,0:T(8,128)(2,1)S(1)}, bf16[256,256]{1,0:T(8,128)(2,1)S(1)}, u32[]{:S(2)}, u32[]{:S(2)}) collective-permute-start(bf16[256,256]{1,0:T(8,128)(2,1)S(1)} %collective-permute-done.7), channel_id=1, source_target_pairs={{0,16},{16,0},{1,17},{17,1},{2,18},{18,2},{3,19},{19,3},{4,20},{20... | collective-permute-start | bytes 393224 | tf_op jit(solution)/shard_map/ppermute | solution.py:74
  26.1 0.1 collective-permute-done.8.refs_0_
  26.2 1.4 %collective-permute-done.9.refs_1_ = bf16[32,640]{1,0:T(8,128)(2,1)S(1)} collective-permute-done((bf16[32,640]{1,0:T(8,128)(2,1)S(1)}, bf16[32,640]{1,0:T(8,128)(2,1)S(1)}, u32[]{:S(2)}, u32[]{:S(2)}) %collective-permute-start.9) | collective-permute-done | bytes 40992 | tf_op jit(solution)/shard_map/ppermute | solution.py:74
  27.6 0.0 collective-permute-done.10.refs_2_
  27.6 0.2 shard_map.85
  27.8 0.0 copy-start.1
  27.8 0.6 collective-permute-start.12
  28.4 0.7 %collective-permute-start.11 = (bf16[32,640]{1,0:T(8,128)(2,1)S(1)}, bf16[32,640]{1,0:T(8,128)(2,1)S(1)}, u32[]{:S(2)}, u32[]{:S(2)}) collective-permute-start(bf16[32,640]{1,0:T(8,128)(2,1)S(1)} %shard_map.85), channel_id=1, source_target_pairs={{0,0},{2,8},{4,2},{6,10},{8,4},{10,12},{12,6},{14,14},{1,1},{3,9},... | collective-permute-start | bytes 122888 | tf_op jit(solution)/shard_map/ppermute | solution.py:382
  29.1 0.0 copy-start.2
  29.1 2.8 %collective-permute-done.12.second = bf16[32,640]{1,0:T(8,128)(2,1)S(1)} collective-permute-done((bf16[32,640]{1,0:T(8,128)(2,1)S(1)}, bf16[32,640]{1,0:T(8,128)(2,1)S(1)}, u32[]{:S(2)}, u32[]{:S(2)}) %collective-permute-start.12) | collective-permute-done | bytes 40992 | tf_op jit(solution)/shard_map/ppermute | solution.py:382
  31.9 0.0 collective-permute-done.11.first
  31.9 0.0 collective-permute-done.13.w_other
  31.9 0.8 %shard_map.86 = (bf16[64,512]{1,0:T(8,128)(2,1)S(1)}, bf16[64,512]{1,0:T(8,128)(2,1)S(1)}, bf16[64,512]{1,0:T(8,128)(2,1)S(1)}, bf16[64,512]{1,0:T(8,128)(2,1)S(1)}) custom-call(bf16[32,640]{1,0:T(8,128)(2,1)S(1)} %collective-permute-done.11.first, bf16[32,640]{1,0:T(8,128)(2,1)S(1)} %collective-permute-done.12.second, ...), custom_call_target="tpu_custom_call" | custom-call | flops 167772160 | bytes 2703360 | tf_op jit(solution)/shard_map/pallas_call | solution.py:84
  32.6 0.0 collective-permute-done.14
  32.7 0.1 collective-permute-start.18
  32.8 6.0 %collective-permute-start.15 = (bf16[64,512]{1,0:T(8,128)(2,1)S(1)}, bf16[64,512]{1,0:T(8,128)(2,1)S(1)}, u32[]{:S(2)}, u32[]{:S(2)}) collective-permute-start(bf16[64,512]{1,0:T(8,128)(2,1)S(1)} %get-tuple-element.71), channel_id=1, source_target_pairs={{0,12},{4,8},{8,4},{12,0},{1,13},{5,9},{9,5},{13,1},{2,14},{6,10},... | collective-permute-start | bytes 196616 | tf_op jit(solution)/shard_map/ppermute | solution.py:74
  38.8 0.0 collective-permute-start.16
  38.8 0.6 %collective-permute-start.17 = (bf16[64,512]{1,0:T(8,128)(2,1)S(1)}, bf16[64,512]{1,0:T(8,128)(2,1)S(1)}, u32[]{:S(2)}, u32[]{:S(2)}) collective-permute-start(bf16[64,512]{1,0:T(8,128)(2,1)S(1)} %get-tuple-element.73), channel_id=1, source_target_pairs={{0,4},{4,0},{8,12},{12,8},{1,5},{5,1},{9,13},{13,9},{2,6},{6,2},{1... | collective-permute-start | bytes 196616 | tf_op jit(solution)/shard_map/ppermute | solution.py:74
  39.4 2.1 %collective-permute-done.15.refs_0_ = bf16[64,512]{1,0:T(8,128)(2,1)S(1)} collective-permute-done((bf16[64,512]{1,0:T(8,128)(2,1)S(1)}, bf16[64,512]{1,0:T(8,128)(2,1)S(1)}, u32[]{:S(2)}, u32[]{:S(2)}) %collective-permute-start.15) | collective-permute-done | bytes 65568 | tf_op jit(solution)/shard_map/ppermute | solution.py:74
  41.6 4.1 %collective-permute-done.16.refs_1_ = bf16[64,512]{1,0:T(8,128)(2,1)S(1)} collective-permute-done((bf16[64,512]{1,0:T(8,128)(2,1)S(1)}, bf16[64,512]{1,0:T(8,128)(2,1)S(1)}, u32[]{:S(2)}, u32[]{:S(2)}) %collective-permute-start.16) | collective-permute-done | bytes 65568 | tf_op jit(solution)/shard_map/ppermute | solution.py:74
  45.7 0.0 collective-permute-done.17.refs_2_
  45.7 0.0 collective-permute-done.18.refs_5_
  45.7 0.0 copy-done.1
  45.7 0.3 shard_map.87
  46.0 3.0 %collective-permute-start.19 = (bf16[32,1152]{1,0:T(8,128)(2,1)S(1)}, bf16[32,1152]{1,0:T(8,128)(2,1)S(1)}, u32[]{:S(2)}, u32[]{:S(2)}) collective-permute-start(bf16[32,1152]{1,0:T(8,128)(2,1)S(1)} %get-tuple-element.80), channel_id=1, source_target_pairs={{0,2},{2,0},{1,3},{3,1},{4,6},{6,4},{5,7},{7,5},{8,10},{10,8},{9,1... | collective-permute-start | bytes 221192 | tf_op jit(solution)/shard_map/ppermute | solution.py:74
  49.0 2.5 %collective-permute-done.19.came = bf16[32,1152]{1,0:T(8,128)(2,1)S(1)} collective-permute-done((bf16[32,1152]{1,0:T(8,128)(2,1)S(1)}, bf16[32,1152]{1,0:T(8,128)(2,1)S(1)}, u32[]{:S(2)}, u32[]{:S(2)}) %collective-permute-start.19) | collective-permute-done | bytes 73760 | tf_op jit(solution)/shard_map/ppermute | solution.py:74
  51.5 0.0 copy-done.2
  51.5 0.2 shard_map.88
  51.7 1.6 %collective-permute-start.20 = (bf16[8,1152]{1,0:T(8,128)(2,1)S(1)}, bf16[8,1152]{1,0:T(8,128)(2,1)S(1)}, u32[]{:S(2)}, u32[]{:S(2)}) collective-permute-start(bf16[8,1152]{1,0:T(8,128)(2,1)S(1)} %get-tuple-element.81), channel_id=1, source_target_pairs={{0,12},{4,8},{8,4},{12,0},{1,13},{5,9},{9,5},{13,1},{2,14},{6,10},... | collective-permute-start | bytes 55304 | tf_op jit(solution)/shard_map/ppermute | solution.py:74
  53.3 0.0 collective-permute-start.21
  53.3 2.8 %collective-permute-start.22 = (bf16[8,1152]{1,0:T(8,128)(2,1)S(1)}, bf16[8,1152]{1,0:T(8,128)(2,1)S(1)}, u32[]{:S(2)}, u32[]{:S(2)}) collective-permute-start(bf16[8,1152]{1,0:T(8,128)(2,1)S(1)} %get-tuple-element.83), channel_id=1, source_target_pairs={{0,4},{4,0},{8,12},{12,8},{1,5},{5,1},{9,13},{13,9},{2,6},{6,2},{1... | collective-permute-start | bytes 55304 | tf_op jit(solution)/shard_map/ppermute | solution.py:74
  56.1 1.2 %collective-permute-done.20.refs_0_ = bf16[8,1152]{1,0:T(8,128)(2,1)S(1)} collective-permute-done((bf16[8,1152]{1,0:T(8,128)(2,1)S(1)}, bf16[8,1152]{1,0:T(8,128)(2,1)S(1)}, u32[]{:S(2)}, u32[]{:S(2)}) %collective-permute-start.20) | collective-permute-done | bytes 18464 | tf_op jit(solution)/shard_map/ppermute | solution.py:74
  57.3 0.8 %collective-permute-done.21.refs_1_ = bf16[8,1152]{1,0:T(8,128)(2,1)S(1)} collective-permute-done((bf16[8,1152]{1,0:T(8,128)(2,1)S(1)}, bf16[8,1152]{1,0:T(8,128)(2,1)S(1)}, u32[]{:S(2)}, u32[]{:S(2)}) %collective-permute-start.21) | collective-permute-done | bytes 18464 | tf_op jit(solution)/shard_map/ppermute | solution.py:74
  58.0 0.0 collective-permute-done.22.refs_2_
  58.1 0.8 %shard_map.89 = bf16[1,4,2,1024]{3,2,1,0:T(2,128)(2,1)} custom-call(bf16[8,1152]{1,0:T(8,128)(2,1)S(1)} %collective-permute-done.20.refs_0_, bf16[8,1152]{1,0:T(8,128)(2,1)S(1)} %collective-permute-done.21.refs_1_, bf16[8,1152]{1,0:T(8,128)(2,1)S(1)} %collective-permute-done.22.refs_2_, bf16[8,1152]{1,0:T(8,128)(2,1)S(1)} %get-tuple-element.84.refs_3_, ...), custom_call_target="tpu_custom_call" | custom-call | bytes 73792 | tf_op jit(solution)/shard_map/pallas_call | solution.py:84
  (4 shorter events, 0.0 us)
Async XLA Ops:
  0.0 9.6 %copy-start = (s32[4,4]{1,0:T(4,128)S(1)}, s32[4,4]{1,0:T(4,128)}, u32[]{:S(2)}) copy-start(s32[4,4]{1,0:T(4,128)} %refs_4_.1) | copy-start | bytes 196
  0.0 9.6 %copy-start.3 = (f32[1280]{0:T(1024)S(1)}, f32[1280]{0:T(1024)}, u32[]{:S(2)}) copy-start(f32[1280]{0:T(1024)} %ln_gain.3) | copy-start | bytes 15364
  0.0 9.6 %collective-permute-start.1 = (bf16[1280,640]{1,0:T(8,128)(2,1)}, bf16[1280,640]{1,0:T(8,128)(2,1)S(1)}, u32[]{:S(2)}, u32[]{:S(2)}) collective-permute-start(bf16[1280,640]{1,0:T(8,128)(2,1)} %w_fc1.1), channel_id=1, source_target_pairs={{0,1},{1,0},{2,3},{3,2},{4,5},{5,4},{6,7},{7,6},{8,9},{9,8},{10,11... | collective-permute-start | bytes 4915208 | tf_op jit(solution)/shard_map/ppermute | solution.py:74
  0.5 9.1 %collective-permute-start.2 = (f32[1024]{0:T(1024)}, f32[1024]{0:T(1024)S(1)}, u32[]{:S(2)}, u32[]{:S(2)}) collective-permute-start(f32[1024]{0:T(1024)} %refs_6_.1), channel_id=1, source_target_pairs={{0,1},{1,0},{2,3},{3,2},{4,5},{5,4},{6,7},{7,6},{8,9},{9,8},{10,11... | collective-permute-start | bytes 12296 | tf_op jit(solution)/shard_map/ppermute | solution.py:74
  0.5 9.1 %collective-permute-start = (bf16[1,4,2,5120]{3,2,1,0:T(2,128)(2,1)}, bf16[1,4,2,5120]{3,2,1,0:T(2,128)(2,1)S(1)}, u32[]{:S(2)}, u32[]{:S(2)}) collective-permute-start(bf16[1,4,2,5120]{3,2,1,0:T(2,128)(2,1)} %cache.1), channel_id=1, source_target_pairs={{0,2},{2,0},{1,3},{3,1},{4,6},{6,4},{5,7},{7,5},{8,10},{10,8},{9,1... | collective-permute-start | bytes 245768 | tf_op jit(solution)/shard_map/ppermute | solution.py:74
  5.5 14.4 %collective-permute-start.6 = (bf16[256,256]{1,0:T(8,128)(2,1)S(1)}, bf16[256,256]{1,0:T(8,128)(2,1)S(1)}, u32[]{:S(2)}, u32[]{:S(2)}) collective-permute-start(bf16[256,256]{1,0:T(8,128)(2,1)S(1)} %get-tuple-element.58), channel_id=1, source_target_pairs={{0,4},{4,0},{8,12},{12,8},{1,5},{5,1},{9,13},{13,9},{2,6},{6,2},{1... | collective-permute-start | bytes 393224 | tf_op jit(solution)/shard_map/ppermute | solution.py:74
  7.1 12.8 %collective-permute-start.7 = (bf16[256,256]{1,0:T(8,128)(2,1)S(1)}, bf16[256,256]{1,0:T(8,128)(2,1)S(1)}, u32[]{:S(2)}, u32[]{:S(2)}) collective-permute-start(bf16[256,256]{1,0:T(8,128)(2,1)S(1)} %get-tuple-element.59), channel_id=1, source_target_pairs={{0,12},{4,8},{8,4},{12,0},{16,24},{20,28},{24,16},{28,20},{1,13},{... | collective-permute-start | bytes 393224 | tf_op jit(solution)/shard_map/ppermute | solution.py:345
  9.9 7.5 %collective-permute-start.3 = (bf16[16,1280]{1,0:T(8,128)(2,1)S(1)}, bf16[16,1280]{1,0:T(8,128)(2,1)S(1)}, u32[]{:S(2)}, u32[]{:S(2)}) collective-permute-start(bf16[16,1280]{1,0:T(8,128)(2,1)S(1)} %get-tuple-element.48), channel_id=1, source_target_pairs={{0,12},{4,8},{8,4},{12,0},{1,13},{5,9},{9,5},{13,1},{2,14},{6,10},... | collective-permute-start | bytes 122888 | tf_op jit(solution)/shard_map/ppermute | solution.py:74
  11.3 7.9 %collective-permute-start.4 = (bf16[16,1280]{1,0:T(8,128)(2,1)S(1)}, bf16[16,1280]{1,0:T(8,128)(2,1)S(1)}, u32[]{:S(2)}, u32[]{:S(2)}) collective-permute-start(bf16[16,1280]{1,0:T(8,128)(2,1)S(1)} %get-tuple-element.49), channel_id=1, source_target_pairs={{0,8},{4,12},{8,0},{12,4},{1,9},{5,13},{9,1},{13,5},{2,10},{6,14},... | collective-permute-start | bytes 122888 | tf_op jit(solution)/shard_map/ppermute | solution.py:74
  12.1 7.1 %collective-permute-start.5 = (bf16[16,1280]{1,0:T(8,128)(2,1)S(1)}, bf16[16,1280]{1,0:T(8,128)(2,1)S(1)}, u32[]{:S(2)}, u32[]{:S(2)}) collective-permute-start(bf16[16,1280]{1,0:T(8,128)(2,1)S(1)} %get-tuple-element.50), channel_id=1, source_target_pairs={{0,4},{4,0},{8,12},{12,8},{1,5},{5,1},{9,13},{13,9},{2,6},{6,2},{1... | collective-permute-start | bytes 122888 | tf_op jit(solution)/shard_map/ppermute | solution.py:74
  19.9 12.0 %collective-permute-start.13 = (bf16[640,1024]{1,0:T(8,128)(2,1)S(1)}, bf16[640,1024]{1,0:T(8,128)(2,1)S(1)}, u32[]{:S(2)}, u32[]{:S(2)}) collective-permute-start(bf16[640,1024]{1,0:T(8,128)(2,1)S(1)} %get-tuple-element.65.w_mine), channel_id=1, source_target_pairs={{0,1},{1,0},{2,3},{3,2},{4,5},{5,4},{6,7},{7,6},{8,9},{9,8},{10,11... | collective-permute-start | bytes 3932168 | tf_op jit(solution)/shard_map/ppermute | solution.py:74
  20.0 6.2 %collective-permute-start.8 = (bf16[32,640]{1,0:T(8,128)(2,1)S(1)}, bf16[32,640]{1,0:T(8,128)(2,1)S(1)}, u32[]{:S(2)}, u32[]{:S(2)}) collective-permute-start(bf16[32,640]{1,0:T(8,128)(2,1)S(1)} %get-tuple-element.61), channel_id=1, source_target_pairs={{0,12},{4,8},{8,4},{12,0},{1,13},{5,9},{9,5},{13,1},{2,14},{6,10},... | collective-permute-start | bytes 122888 | tf_op jit(solution)/shard_map/ppermute | solution.py:74
  22.7 4.9 %collective-permute-start.9 = (bf16[32,640]{1,0:T(8,128)(2,1)S(1)}, bf16[32,640]{1,0:T(8,128)(2,1)S(1)}, u32[]{:S(2)}, u32[]{:S(2)}) collective-permute-start(bf16[32,640]{1,0:T(8,128)(2,1)S(1)} %get-tuple-element.62), channel_id=1, source_target_pairs={{0,8},{4,12},{8,0},{12,4},{1,9},{5,13},{9,1},{13,5},{2,10},{6,14},... | collective-permute-start | bytes 122888 | tf_op jit(solution)/shard_map/ppermute | solution.py:74
  22.7 4.9 %collective-permute-start.10 = (bf16[32,640]{1,0:T(8,128)(2,1)S(1)}, bf16[32,640]{1,0:T(8,128)(2,1)S(1)}, u32[]{:S(2)}, u32[]{:S(2)}) collective-permute-start(bf16[32,640]{1,0:T(8,128)(2,1)S(1)} %get-tuple-element.63), channel_id=1, source_target_pairs={{0,4},{4,0},{8,12},{12,8},{1,5},{5,1},{9,13},{13,9},{2,6},{6,2},{1... | collective-permute-start | bytes 122888 | tf_op jit(solution)/shard_map/ppermute | solution.py:74
  24.4 8.2 %collective-permute-start.14 = (bf16[256,256]{1,0:T(8,128)(2,1)S(1)}, bf16[256,256]{1,0:T(8,128)(2,1)S(1)}, u32[]{:S(2)}, u32[]{:S(2)}) collective-permute-start(bf16[256,256]{1,0:T(8,128)(2,1)S(1)} %collective-permute-done.7), channel_id=1, source_target_pairs={{0,16},{16,0},{1,17},{17,1},{2,18},{18,2},{3,19},{19,3},{4,20},{20... | collective-permute-start | bytes 393224 | tf_op jit(solution)/shard_map/ppermute | solution.py:74
  27.8 17.9 %copy-start.1 = (f32[1024]{0:T(1024)S(1)}, f32[1024]{0:T(1024)}, u32[]{:S(2)}) copy-start(f32[1024]{0:T(1024)} %refs_6_.1) | copy-start | bytes 12292
  27.8 4.1 %collective-permute-start.12 = (bf16[32,640]{1,0:T(8,128)(2,1)S(1)}, bf16[32,640]{1,0:T(8,128)(2,1)S(1)}, u32[]{:S(2)}, u32[]{:S(2)}) collective-permute-start(bf16[32,640]{1,0:T(8,128)(2,1)S(1)} %shard_map.85), channel_id=1, source_target_pairs={{0,2},{2,10},{4,0},{6,8},{8,6},{10,14},{12,4},{14,12},{1,3},{3,11}... | collective-permute-start | bytes 122888 | tf_op jit(solution)/shard_map/ppermute | solution.py:382
  28.4 3.5 %collective-permute-start.11 = (bf16[32,640]{1,0:T(8,128)(2,1)S(1)}, bf16[32,640]{1,0:T(8,128)(2,1)S(1)}, u32[]{:S(2)}, u32[]{:S(2)}) collective-permute-start(bf16[32,640]{1,0:T(8,128)(2,1)S(1)} %shard_map.85), channel_id=1, source_target_pairs={{0,0},{2,8},{4,2},{6,10},{8,4},{10,12},{12,6},{14,14},{1,1},{3,9},... | collective-permute-start | bytes 122888 | tf_op jit(solution)/shard_map/ppermute | solution.py:382
  29.1 22.4 %copy-start.2 = (s32[1,4,1]{1,2,0:T(1,128)S(1)}, s32[1,4,1]{1,2,0:T(1,128)}, u32[]{:S(2)}) copy-start(s32[1,4,1]{1,2,0:T(1,128)} %param.15) | copy-start | bytes 52
  32.7 13.0 %collective-permute-start.18 = (bf16[1024,256]{1,0:T(8,128)(2,1)S(1)}, bf16[1024,256]{1,0:T(8,128)(2,1)S(1)}, u32[]{:S(2)}, u32[]{:S(2)}) collective-permute-start(bf16[1024,256]{1,0:T(8,128)(2,1)S(1)} %constant_dynamic-update-slice_fusion.refs_4_), channel_id=1, source_target_pairs={{0,1},{1,0},{2,3},{3,2},{4,5},{5,4},{6,7},{7,6},{8,9},{9,8},{10,11... | collective-permute-start | bytes 1572872 | tf_op jit(solution)/shard_map/ppermute | solution.py:74
  32.8 8.8 %collective-permute-start.15 = (bf16[64,512]{1,0:T(8,128)(2,1)S(1)}, bf16[64,512]{1,0:T(8,128)(2,1)S(1)}, u32[]{:S(2)}, u32[]{:S(2)}) collective-permute-start(bf16[64,512]{1,0:T(8,128)(2,1)S(1)} %get-tuple-element.71), channel_id=1, source_target_pairs={{0,12},{4,8},{8,4},{12,0},{1,13},{5,9},{9,5},{13,1},{2,14},{6,10},... | collective-permute-start | bytes 196616 | tf_op jit(solution)/shard_map/ppermute | solution.py:74
  38.8 6.9 %collective-permute-start.16 = (bf16[64,512]{1,0:T(8,128)(2,1)S(1)}, bf16[64,512]{1,0:T(8,128)(2,1)S(1)}, u32[]{:S(2)}, u32[]{:S(2)}) collective-permute-start(bf16[64,512]{1,0:T(8,128)(2,1)S(1)} %get-tuple-element.72), channel_id=1, source_target_pairs={{0,8},{4,12},{8,0},{12,4},{1,9},{5,13},{9,1},{13,5},{2,10},{6,14},... | collective-permute-start | bytes 196616 | tf_op jit(solution)/shard_map/ppermute | solution.py:74
  38.8 6.8 %collective-permute-start.17 = (bf16[64,512]{1,0:T(8,128)(2,1)S(1)}, bf16[64,512]{1,0:T(8,128)(2,1)S(1)}, u32[]{:S(2)}, u32[]{:S(2)}) collective-permute-start(bf16[64,512]{1,0:T(8,128)(2,1)S(1)} %get-tuple-element.73), channel_id=1, source_target_pairs={{0,4},{4,0},{8,12},{12,8},{1,5},{5,1},{9,13},{13,9},{2,6},{6,2},{1... | collective-permute-start | bytes 196616 | tf_op jit(solution)/shard_map/ppermute | solution.py:74
  46.0 5.5 %collective-permute-start.19 = (bf16[32,1152]{1,0:T(8,128)(2,1)S(1)}, bf16[32,1152]{1,0:T(8,128)(2,1)S(1)}, u32[]{:S(2)}, u32[]{:S(2)}) collective-permute-start(bf16[32,1152]{1,0:T(8,128)(2,1)S(1)} %get-tuple-element.80), channel_id=1, source_target_pairs={{0,2},{2,0},{1,3},{3,1},{4,6},{6,4},{5,7},{7,5},{8,10},{10,8},{9,1... | collective-permute-start | bytes 221192 | tf_op jit(solution)/shard_map/ppermute | solution.py:74
  51.7 5.6 %collective-permute-start.20 = (bf16[8,1152]{1,0:T(8,128)(2,1)S(1)}, bf16[8,1152]{1,0:T(8,128)(2,1)S(1)}, u32[]{:S(2)}, u32[]{:S(2)}) collective-permute-start(bf16[8,1152]{1,0:T(8,128)(2,1)S(1)} %get-tuple-element.81), channel_id=1, source_target_pairs={{0,12},{4,8},{8,4},{12,0},{1,13},{5,9},{9,5},{13,1},{2,14},{6,10},... | collective-permute-start | bytes 55304 | tf_op jit(solution)/shard_map/ppermute | solution.py:74
  53.3 4.7 %collective-permute-start.21 = (bf16[8,1152]{1,0:T(8,128)(2,1)S(1)}, bf16[8,1152]{1,0:T(8,128)(2,1)S(1)}, u32[]{:S(2)}, u32[]{:S(2)}) collective-permute-start(bf16[8,1152]{1,0:T(8,128)(2,1)S(1)} %get-tuple-element.82), channel_id=1, source_target_pairs={{0,8},{4,12},{8,0},{12,4},{1,9},{5,13},{9,1},{13,5},{2,10},{6,14},... | collective-permute-start | bytes 55304 | tf_op jit(solution)/shard_map/ppermute | solution.py:74
  53.3 4.7 %collective-permute-start.22 = (bf16[8,1152]{1,0:T(8,128)(2,1)S(1)}, bf16[8,1152]{1,0:T(8,128)(2,1)S(1)}, u32[]{:S(2)}, u32[]{:S(2)}) collective-permute-start(bf16[8,1152]{1,0:T(8,128)(2,1)S(1)} %get-tuple-element.83), channel_id=1, source_target_pairs={{0,4},{4,0},{8,12},{12,8},{1,5},{5,1},{9,13},{13,9},{2,6},{6,2},{1... | collective-permute-start | bytes 55304 | tf_op jit(solution)/shard_map/ppermute | solution.py:74

commit v4 on v3

--- a/solution.py
+++ b/solution.py
@@ -74,9 +74,9 @@
     return lax.ppermute(x, axis, [(i, i ^ step) for i in range(n)])
 
 
-def exchange(parts):
+def exchange(parts, order):
     n = len(parts)
-    return [swap(parts[k], "hold", n, k) for k in range(n - 1, 0, -1)] + [parts[0]]
+    return [swap(parts[k], "hold", n, k) for k in order] + [parts[0]]
 
 
 def call(body, outs, *args, flops=0, scratch=(), **specs):
@@ -143,13 +143,13 @@
         out[...] = jnp.concatenate([own[:, cols], held[:, cols]], axis=0).astype(jnp.bfloat16)
 
 
-def first_kernel(*refs):
-    pieces, weights, outs = refs[3::-1], refs[4:6], refs[6:10]
+def first_kernel(places, *refs):
+    pieces, weights, outs = refs[:4], refs[4:6], refs[6:10]
     rows, sums = refs[10:]
     h, rep = lax.axis_index("hold"), lax.axis_index("rep")
     size = pieces[0].shape[0] // 2
     half = 4 * size
-    for k, piece in enumerate(pieces):
+    for k, piece in zip((*places, 0), pieces, strict=True):
         part = piece[...].astype(jnp.float32)
         for b in range(2):
             start = pl.multiple_of(b * half + (h ^ k) * size, 8)
@@ -280,14 +280,14 @@
         outs[k][:, keys:] = tail.astype(jnp.bfloat16)
 
 
-def last_kernel(width, *refs):
-    parts, matching, out, held = refs[3::-1], refs[4], refs[5], refs[6]
+def last_kernel(width, places, *refs):
+    parts, matching, out, held = refs[:4], refs[4], refs[5], refs[6]
     h = lax.axis_index("hold")
     _, rounds, block, features = out.shape
     total = sum(part[...].astype(jnp.float32) for part in parts)
     squares = total[:, features : features + 1] + total[:, -1:]
     keys = total[:, :features] * lax.rsqrt(squares / width + EPSILON)
-    for k, part in enumerate(parts):
+    for k, part in zip((*places, 0), parts, strict=True):
         held[pl.ds(h ^ k, 1), :] = part[:1, features:].astype(jnp.float32)
     b_of = lax.broadcasted_iota(jnp.int32, (block, 1), 0).astype(jnp.float32)
     blocks = []
@@ -314,38 +314,33 @@
     def like(dims, kind=bf16):
         return jax.ShapeDtypeStruct(dims, kind)
 
+    long = 8 << 30
+    hbm = pl.BlockSpec(memory_space=pltpu.HBM)
+    in_hbm = [
+        pltpu.with_memory_space_constraint(x, pltpu.HBM)
+        for x in (cache, ln_gain, matching, w_fc1, w_fc2, w_key)
+    ]
     cache_other = swap(cache, "tp", 2, 1)
-    w_fc1_other = swap(w_fc1, "rep", 2, 1)
-    gain_other = swap(norm_gain, "rep", 2, 1)
-    cache_in, w_fc1_in, w_fc2_in, w_key_in, ln_in, matching_in = (
-        pltpu.with_memory_space_constraint(x, pltpu.HBM)
-        for x in (cache, w_fc1, w_fc2, w_key, ln_gain, matching)
-    )
     own, w_fc1_mine, w_fc2_mine, key_0, key_1, key_far = call(
         own_kernel,
         [like((rows, depth), f32), like(w_fc1.shape), like(w_fc2.shape)]
         + [like((share, key_cols))] * 3,
-        cache_in,
-        ln_in,
-        matching_in,
-        w_fc1_in,
-        w_fc2_in,
-        w_key_in,
-        in_specs=[pl.BlockSpec(memory_space=pltpu.HBM)] * 6,
+        *in_hbm,
+        in_specs=[hbm] * 6,
         scratch=[
             vmem(cache.shape, bf16),
             vmem(ln_gain.shape, f32),
             vmem(matching.shape, jnp.int32),
             pltpu.SemaphoreType.DMA((8,)),
         ],
-        flops=8 << 30,
-    )
-    key_1 = swap(key_1, "hold", n, 1)
-    perm = [(n * g + a, n * g + (a ^ 3 ^ g)) for g in range(2) for a in range(n)]
-    key_far = lax.ppermute(key_far, ("grp", "hold"), perm)
-    own, cache_other, w_fc1_other, gain_other = lax.optimization_barrier(
-        (own, cache_other, w_fc1_other, gain_other)
-    )
+        flops=long,
+    )
+    w_fc1_other = swap(w_fc1, "rep", 2, 1)
+    gain_other = swap(norm_gain, "rep", 2, 1)
+    own, cache_other, w_fc2_sent, gain_other = lax.optimization_barrier(
+        (own, cache_other, w_fc2_mine, gain_other)
+    )
+    w_fc2_other = swap(w_fc2_sent, "rep", 2, 1)
     pieces = call(
         both_kernel,
         [like((2 * rows, chunk))] * n,
@@ -354,25 +349,28 @@
         ln_gain,
         matching,
         scratch=[vmem((rows, depth), f32)],
-        flops=8 << 30,
-    )
-    pieces = exchange(pieces)
+        flops=long,
+    )
+
+    *pieces, key_1, key_far = lax.optimization_barrier((*pieces, key_1, key_far))
+    key_1 = swap(key_1, "hold", n, 1)
+    perm = [(n * g + a, n * g + (a ^ 3 ^ g)) for g in range(2) for a in range(n)]
+    key_far = lax.ppermute(key_far, ("grp", "hold"), perm)
+
+    order = (3, 2, 1)
     partial = call(
-        first_kernel,
+        functools.partial(first_kernel, order),
         [like((4 * rows, hidden_cols))] * n,
-        *pieces,
+        *exchange(pieces, order),
         w_fc1_mine,
         w_fc1_other,
         scratch=[vmem((8 * rows, chunk), f32), vmem((2, 8 * rows, hidden_cols), f32)],
-        flops=32 * rows * w_fc1.size,
-    )
-    *partial, key_1, key_far, w_fc2_sent = lax.optimization_barrier(
-        (*partial, key_1, key_far, w_fc2_mine)
-    )
-    w_fc2_other = swap(w_fc2_sent, "rep", 2, 1)
-    parts = exchange(partial)
+        flops=long,
+    )
+    *partial, w_fc2_other = lax.optimization_barrier((*partial, w_fc2_other))
     key_near = swap(key_far, "grp", 2, 1)
-    hidden = call(gelu_kernel, like(parts[0].shape), *parts, flops=8 << 30)
+    parts = exchange(partial, (1, 3, 2))
+    hidden = call(gelu_kernel, like(parts[0].shape), *parts)
 
     halves = []
     for g in range(2):
@@ -380,7 +378,7 @@
             (2 * a + b, 2 * (2 * b + (a >> 1)) + ((a & 1) ^ g)) for a in range(n) for b in range(2)
         ]
         halves.append(lax.ppermute(hidden, ("hold", "tp"), perm))
-
+    *halves, key_1 = lax.optimization_barrier((*halves, key_1))
     merged = call(
         second_kernel,
         [like((8 * rows, 2 * share))] * n,
@@ -393,11 +391,10 @@
     *merged, key_near = lax.optimization_barrier((*merged, key_near))
     key_mine = jnp.concatenate([key_0, key_1, key_far, key_near])
     key_other = swap(key_mine, "rep", 2, 1)
-    merged = exchange(merged)
     kept, sent = call(
         key_kernel,
         [like((4 * rows, n * key_cols + 128), f32), like((4 * rows, n * key_cols + 128))],
-        *merged,
+        *exchange(merged, (2, 1, 3)),
         key_mine,
         key_other,
         norm_gain,
@@ -414,11 +411,11 @@
         counts.reshape(1, rounds),
         scratch=[vmem((4 * rows, n * key_cols + 128), f32)],
     )
-    keys = exchange(keys)
+    order = (3, 2, 1)
     return call(
-        functools.partial(last_kernel, width),
+        functools.partial(last_kernel, width, order),
         like((1, rounds, block, n * key_cols)),
-        *keys,
+        *exchange(keys, order),
         matching,
         scratch=[vmem((rounds, 128), f32)],
     )

time: 59 us -> 55.2 us (0.936)
  waiting for transfers between devices: 19.9 us -> 15.2 us
  starting transfers between devices: 33.6 us -> 34.4 us
    ppermute x20, waiting for transfers between devices: 17.1 us -> 12.6 us  [swap(): return lax.ppermute(x, axis, [(i, i ^ step) for i in range(n)])]
    ppermute x20, starting transfers between devices: 29.9 us -> 25.9 us  [swap(): return lax.ppermute(x, axis, [(i, i ^ step) for i in range(n)])]
    ppermute x2, starting transfers between devices: 1.24 us -> 4.63 us  [rows_past_weights(): halves.append(lax.ppermute(hidden, ('hold', 'tp'), perm))]
    ppermute x1, starting transfers between devices: 2.47 us -> 3.96 us  [rows_past_weights(): key_far = lax.ppermute(key_far, ('grp', 'hold'), perm)]
where the time goes in v4:
time: 55.2 us; the launch traced here: 55.1 us
  starting transfers between devices  34.4 us (62%)
  waiting for transfers between devices  15.2 us (28%)
  Pallas kernels  5.17 us (9%)
    ppermute x20, starting transfers between devices, swap(): return lax.ppermute(x, axis, [(i, i ^ step) for i in range(n)])  25.9 us
    ppermute x20, waiting for transfers between devices, swap(): return lax.ppermute(x, axis, [(i, i ^ step) for i in range(n)])  12.6 us
    pallas_call x8, Pallas kernels, call(): pl.pallas_call(body, out_shape=outs, scratch_shapes=scratch, cost_estimat...  5.17 us
    ppermute x2, starting transfers between devices, rows_past_weights(): halves.append(lax.ppermute(hidden, ('hold', 'tp'), perm))  4.63 us
    ppermute x1, starting transfers between devices, rows_past_weights(): key_far = lax.ppermute(key_far, ('grp', 'hold'), perm)  3.96 us
    ppermute x2, waiting for transfers between devices, rows_past_weights(): halves.append(lax.ppermute(hidden, ('hold', 'tp'), perm))  2.57 us
  transfers between devices with their start and end apart: 23, of which 10 were waited for; matrix products, arithmetic and copies ran while one was open for 0% of the time, Pallas kernels for 7%

profile of v4, /device:TPU:0, one launch (start us, length us, event | category | flops | bytes accessed | tf_op | source)
XLA Modules:
  0.0 55.1 jit_solution(3760398885419608099)
XLA Ops:
  0.0 0.0 copy-start
  0.0 0.0 copy-start.3
  0.0 2.9 %collective-permute-start = (bf16[1,4,2,5120]{3,2,1,0:T(2,128)(2,1)}, bf16[1,4,2,5120]{3,2,1,0:T(2,128)(2,1)S(1)}, u32[]{:S(2)}, u32[]{:S(2)}) collective-permute-start(bf16[1,4,2,5120]{3,2,1,0:T(2,128)(2,1)} %cache.1), channel_id=1, source_target_pairs={{0,2},{2,0},{1,3},{3,1},{4,6},{6,4},{5,7},{7,5},{8,10},{10,8},{9,1... | collective-permute-start | bytes 245768 | tf_op jit(solution)/shard_map/ppermute | solution.py:74
  2.9 0.0 collective-permute-start.1
  2.9 0.5 collective-permute-start.5
  3.5 2.0 %shard_map.82 = (f32[8,5120]{1,0:T(8,128)S(1)}, bf16[1280,640]{1,0:T(8,128)(2,1)S(1)}, bf16[640,1024]{1,0:T(8,128)(2,1)S(1)}, bf16[256,256]{1,0:T(8,128)(2,1)S(1...) custom-call(bf16[1,4,2,5120]{3,2,1,0:T(2,128)(2,1)} %cache.1, f32[1280]{0:T(1024)} %ln_gain.3, ...), custom_call_target="tpu_custom_call" | custom-call | flops 8589934592 | bytes 3560512 | tf_op jit(solution)/shard_map/pallas_call | solution.py:84
  5.5 0.0 collective-permute-done.1.refs_7_
  5.5 0.1 collective-permute-done.cache
  5.6 0.0 collective-permute-start.6
  5.6 0.0 copy-done
  5.6 0.0 copy-done.3
  5.6 0.3 shard_map.83
  5.9 4.2 %collective-permute-start.2 = (bf16[16,1280]{1,0:T(8,128)(2,1)S(1)}, bf16[16,1280]{1,0:T(8,128)(2,1)S(1)}, u32[]{:S(2)}, u32[]{:S(2)}) collective-permute-start(bf16[16,1280]{1,0:T(8,128)(2,1)S(1)} %get-tuple-element.62), channel_id=1, source_target_pairs={{0,12},{4,8},{8,4},{12,0},{1,13},{5,9},{9,5},{13,1},{2,14},{6,10},... | collective-permute-start | bytes 122888 | tf_op jit(solution)/shard_map/ppermute | solution.py:74
  10.1 0.0 collective-permute-start.3
  10.1 0.6 %collective-permute-start.4 = (bf16[16,1280]{1,0:T(8,128)(2,1)S(1)}, bf16[16,1280]{1,0:T(8,128)(2,1)S(1)}, u32[]{:S(2)}, u32[]{:S(2)}) collective-permute-start(bf16[16,1280]{1,0:T(8,128)(2,1)S(1)} %get-tuple-element.64), channel_id=1, source_target_pairs={{0,4},{4,0},{8,12},{12,8},{1,5},{5,1},{9,13},{13,9},{2,6},{6,2},{1... | collective-permute-start | bytes 122888 | tf_op jit(solution)/shard_map/ppermute | solution.py:74
  10.7 1.6 %collective-permute-done.2.refs_0_ = bf16[16,1280]{1,0:T(8,128)(2,1)S(1)} collective-permute-done((bf16[16,1280]{1,0:T(8,128)(2,1)S(1)}, bf16[16,1280]{1,0:T(8,128)(2,1)S(1)}, u32[]{:S(2)}, u32[]{:S(2)}) %collective-permute-start.2) | collective-permute-done | bytes 40992 | tf_op jit(solution)/shard_map/ppermute | solution.py:74
  12.3 4.0 %collective-permute-start.13 = (bf16[256,256]{1,0:T(8,128)(2,1)S(1)}, bf16[256,256]{1,0:T(8,128)(2,1)S(1)}, u32[]{:S(2)}, u32[]{:S(2)}) collective-permute-start(bf16[256,256]{1,0:T(8,128)(2,1)S(1)} %get-tuple-element.84), channel_id=1, source_target_pairs={{0,12},{4,8},{8,4},{12,0},{16,24},{20,28},{24,16},{28,20},{1,13},{... | collective-permute-start | bytes 393224 | tf_op jit(solution)/shard_map/ppermute | solution.py:358
  16.3 0.0 collective-permute-done.3.refs_1_
  16.3 0.0 collective-permute-done.4.refs_2_
  16.3 0.0 collective-permute-done.5.refs_5_
  16.3 0.7 %shard_map.84 = (bf16[32,640]{1,0:T(8,128)(2,1)S(1)}, bf16[32,640]{1,0:T(8,128)(2,1)S(1)}, bf16[32,640]{1,0:T(8,128)(2,1)S(1)}, bf16[32,640]{1,0:T(8,128)(2,1)S(1)}) custom-call(bf16[16,1280]{1,0:T(8,128)(2,1)S(1)} %collective-permute-done.2.refs_0_, bf16[16,1280]{1,0:T(8,128)(2,1)S(1)} %collective-permute-done.3.refs_1_, ...), custom_call_target="tpu_custom_call" | custom-call | flops 8589934592 | bytes 3440640 | tf_op jit(solution)/shard_map/pallas_call | solution.py:84
  17.0 0.0 collective-permute-done.6.w_other
  17.0 0.1 collective-permute-start.7
  17.1 2.1 %collective-permute-start.8 = (bf16[32,640]{1,0:T(8,128)(2,1)S(1)}, bf16[32,640]{1,0:T(8,128)(2,1)S(1)}, u32[]{:S(2)}, u32[]{:S(2)}) collective-permute-start(bf16[32,640]{1,0:T(8,128)(2,1)S(1)} %get-tuple-element.73), channel_id=1, source_target_pairs={{0,12},{4,8},{8,4},{12,0},{1,13},{5,9},{9,5},{13,1},{2,14},{6,10},... | collective-permute-start | bytes 122888 | tf_op jit(solution)/shard_map/ppermute | solution.py:74
  19.2 1.4 %collective-permute-start.9 = (bf16[32,640]{1,0:T(8,128)(2,1)S(1)}, bf16[32,640]{1,0:T(8,128)(2,1)S(1)}, u32[]{:S(2)}, u32[]{:S(2)}) collective-permute-start(bf16[32,640]{1,0:T(8,128)(2,1)S(1)} %get-tuple-element.74), channel_id=1, source_target_pairs={{0,8},{4,12},{8,0},{12,4},{1,9},{5,13},{9,1},{13,5},{2,10},{6,14},... | collective-permute-start | bytes 122888 | tf_op jit(solution)/shard_map/ppermute | solution.py:74
  20.5 1.0 %collective-permute-start.12 = (bf16[256,256]{1,0:T(8,128)(2,1)S(1)}, bf16[256,256]{1,0:T(8,128)(2,1)S(1)}, u32[]{:S(2)}, u32[]{:S(2)}) collective-permute-start(bf16[256,256]{1,0:T(8,128)(2,1)S(1)} %get-tuple-element.76), channel_id=1, source_target_pairs={{0,4},{4,0},{8,12},{12,8},{1,5},{5,1},{9,13},{13,9},{2,6},{6,2},{1... | collective-permute-start | bytes 393224 | tf_op jit(solution)/shard_map/ppermute | solution.py:74
  21.5 0.0 collective-permute-done.13
  21.5 3.0 %collective-permute-start.14 = (bf16[256,256]{1,0:T(8,128)(2,1)S(1)}, bf16[256,256]{1,0:T(8,128)(2,1)S(1)}, u32[]{:S(2)}, u32[]{:S(2)}) collective-permute-start(bf16[256,256]{1,0:T(8,128)(2,1)S(1)} %collective-permute-done.13), channel_id=1, source_target_pairs={{0,16},{16,0},{1,17},{17,1},{2,18},{18,2},{3,19},{19,3},{4,20},{20... | collective-permute-start | bytes 393224 | tf_op jit(solution)/shard_map/ppermute | solution.py:74
  24.5 0.0 collective-permute-done.7.refs_0_
  24.5 0.0 collective-permute-done.8.refs_1_
  24.5 0.0 collective-permute-done.9.refs_2_
  24.5 0.2 shard_map.85
  24.7 0.7 %collective-permute-start.10 = (bf16[32,640]{1,0:T(8,128)(2,1)S(1)}, bf16[32,640]{1,0:T(8,128)(2,1)S(1)}, u32[]{:S(2)}, u32[]{:S(2)}) collective-permute-start(bf16[32,640]{1,0:T(8,128)(2,1)S(1)} %shard_map.85), channel_id=1, source_target_pairs={{0,0},{2,8},{4,2},{6,10},{8,4},{10,12},{12,6},{14,14},{1,1},{3,9},... | collective-permute-start | bytes 122888 | tf_op jit(solution)/shard_map/ppermute | solution.py:380
  25.4 4.0 %collective-permute-start.11 = (bf16[32,640]{1,0:T(8,128)(2,1)S(1)}, bf16[32,640]{1,0:T(8,128)(2,1)S(1)}, u32[]{:S(2)}, u32[]{:S(2)}) collective-permute-start(bf16[32,640]{1,0:T(8,128)(2,1)S(1)} %shard_map.85), channel_id=1, source_target_pairs={{0,2},{2,10},{4,0},{6,8},{8,6},{10,14},{12,4},{14,12},{1,3},{3,11}... | collective-permute-start | bytes 122888 | tf_op jit(solution)/shard_map/ppermute | solution.py:380
  29.4 0.0 copy-start.1
  29.4 0.0 collective-permute-done.12
  29.4 0.0 collective-permute-done.10.first
  29.4 2.6 %collective-permute-done.11.second = bf16[32,640]{1,0:T(8,128)(2,1)S(1)} collective-permute-done((bf16[32,640]{1,0:T(8,128)(2,1)S(1)}, bf16[32,640]{1,0:T(8,128)(2,1)S(1)}, u32[]{:S(2)}, u32[]{:S(2)}) %collective-permute-start.11) | collective-permute-done | bytes 40992 | tf_op jit(solution)/shard_map/ppermute | solution.py:380
  32.0 0.8 %shard_map.86 = (bf16[64,512]{1,0:T(8,128)(2,1)S(1)}, bf16[64,512]{1,0:T(8,128)(2,1)S(1)}, bf16[64,512]{1,0:T(8,128)(2,1)S(1)}, bf16[64,512]{1,0:T(8,128)(2,1)S(1)}) custom-call(bf16[32,640]{1,0:T(8,128)(2,1)S(1)} %collective-permute-done.10.first, bf16[32,640]{1,0:T(8,128)(2,1)S(1)} %collective-permute-done.11.second, ...), custom_call_target="tpu_custom_call" | custom-call | flops 167772160 | bytes 2703360 | tf_op jit(solution)/shard_map/pallas_call | solution.py:84
  32.8 0.0 copy-start.2
  32.8 0.0 collective-permute-done.14
  32.9 0.1 collective-permute-start.18
  32.9 2.0 %collective-permute-start.15 = (bf16[64,512]{1,0:T(8,128)(2,1)S(1)}, bf16[64,512]{1,0:T(8,128)(2,1)S(1)}, u32[]{:S(2)}, u32[]{:S(2)}) collective-permute-start(bf16[64,512]{1,0:T(8,128)(2,1)S(1)} %get-tuple-element.85), channel_id=1, source_target_pairs={{0,8},{4,12},{8,0},{12,4},{1,9},{5,13},{9,1},{13,5},{2,10},{6,14},... | collective-permute-start | bytes 196616 | tf_op jit(solution)/shard_map/ppermute | solution.py:74
  34.9 0.9 %collective-permute-start.16 = (bf16[64,512]{1,0:T(8,128)(2,1)S(1)}, bf16[64,512]{1,0:T(8,128)(2,1)S(1)}, u32[]{:S(2)}, u32[]{:S(2)}) collective-permute-start(bf16[64,512]{1,0:T(8,128)(2,1)S(1)} %get-tuple-element.86), channel_id=1, source_target_pairs={{0,4},{4,0},{8,12},{12,8},{1,5},{5,1},{9,13},{13,9},{2,6},{6,2},{1... | collective-permute-start | bytes 196616 | tf_op jit(solution)/shard_map/ppermute | solution.py:74
  35.8 2.1 %collective-permute-start.17 = (bf16[64,512]{1,0:T(8,128)(2,1)S(1)}, bf16[64,512]{1,0:T(8,128)(2,1)S(1)}, u32[]{:S(2)}, u32[]{:S(2)}) collective-permute-start(bf16[64,512]{1,0:T(8,128)(2,1)S(1)} %get-tuple-element.87), channel_id=1, source_target_pairs={{0,12},{4,8},{8,4},{12,0},{1,13},{5,9},{9,5},{13,1},{2,14},{6,10},... | collective-permute-start | bytes 196616 | tf_op jit(solution)/shard_map/ppermute | solution.py:74
  37.9 0.5 collective-permute-done.15.refs_0_
  38.4 1.3 %collective-permute-done.16.refs_1_ = bf16[64,512]{1,0:T(8,128)(2,1)S(1)} collective-permute-done((bf16[64,512]{1,0:T(8,128)(2,1)S(1)}, bf16[64,512]{1,0:T(8,128)(2,1)S(1)}, u32[]{:S(2)}, u32[]{:S(2)}) %collective-permute-start.16) | collective-permute-done | bytes 65568 | tf_op jit(solution)/shard_map/ppermute | solution.py:74
  39.7 3.4 %collective-permute-done.17.refs_2_ = bf16[64,512]{1,0:T(8,128)(2,1)S(1)} collective-permute-done((bf16[64,512]{1,0:T(8,128)(2,1)S(1)}, bf16[64,512]{1,0:T(8,128)(2,1)S(1)}, u32[]{:S(2)}, u32[]{:S(2)}) %collective-permute-start.17) | collective-permute-done | bytes 65568 | tf_op jit(solution)/shard_map/ppermute | solution.py:74
  43.1 0.0 collective-permute-done.18.refs_5_
  43.1 0.0 copy-done.1
  43.2 0.3 shard_map.87
  43.5 0.5 collective-permute-start.19
  44.0 3.9 %collective-permute-done.19.came = bf16[32,1152]{1,0:T(8,128)(2,1)S(1)} collective-permute-done((bf16[32,1152]{1,0:T(8,128)(2,1)S(1)}, bf16[32,1152]{1,0:T(8,128)(2,1)S(1)}, u32[]{:S(2)}, u32[]{:S(2)}) %collective-permute-start.19) | collective-permute-done | bytes 73760 | tf_op jit(solution)/shard_map/ppermute | solution.py:74
  47.9 0.0 copy-done.2
  47.9 0.2 shard_map.88
  48.1 1.2 %collective-permute-start.20 = (bf16[8,1152]{1,0:T(8,128)(2,1)S(1)}, bf16[8,1152]{1,0:T(8,128)(2,1)S(1)}, u32[]{:S(2)}, u32[]{:S(2)}) collective-permute-start(bf16[8,1152]{1,0:T(8,128)(2,1)S(1)} %get-tuple-element.95), channel_id=1, source_target_pairs={{0,12},{4,8},{8,4},{12,0},{1,13},{5,9},{9,5},{13,1},{2,14},{6,10},... | collective-permute-start | bytes 55304 | tf_op jit(solution)/shard_map/ppermute | solution.py:74
  49.3 0.0 collective-permute-start.21
  49.3 3.3 %collective-permute-start.22 = (bf16[8,1152]{1,0:T(8,128)(2,1)S(1)}, bf16[8,1152]{1,0:T(8,128)(2,1)S(1)}, u32[]{:S(2)}, u32[]{:S(2)}) collective-permute-start(bf16[8,1152]{1,0:T(8,128)(2,1)S(1)} %get-tuple-element.97), channel_id=1, source_target_pairs={{0,4},{4,0},{8,12},{12,8},{1,5},{5,1},{9,13},{13,9},{2,6},{6,2},{1... | collective-permute-start | bytes 55304 | tf_op jit(solution)/shard_map/ppermute | solution.py:74
  52.5 1.2 %collective-permute-done.20.refs_0_ = bf16[8,1152]{1,0:T(8,128)(2,1)S(1)} collective-permute-done((bf16[8,1152]{1,0:T(8,128)(2,1)S(1)}, bf16[8,1152]{1,0:T(8,128)(2,1)S(1)}, u32[]{:S(2)}, u32[]{:S(2)}) %collective-permute-start.20) | collective-permute-done | bytes 18464 | tf_op jit(solution)/shard_map/ppermute | solution.py:74
  53.7 0.4 collective-permute-done.21.refs_1_
  54.1 0.2 collective-permute-done.22.refs_2_
  54.3 0.8 %shard_map.89 = bf16[1,4,2,1024]{3,2,1,0:T(2,128)(2,1)} custom-call(bf16[8,1152]{1,0:T(8,128)(2,1)S(1)} %collective-permute-done.20.refs_0_, bf16[8,1152]{1,0:T(8,128)(2,1)S(1)} %collective-permute-done.21.refs_1_, bf16[8,1152]{1,0:T(8,128)(2,1)S(1)} %collective-permute-done.22.refs_2_, bf16[8,1152]{1,0:T(8,128)(2,1)S(1)} %get-tuple-element.98.refs_3_, ...), custom_call_target="tpu_custom_call" | custom-call | bytes 73792 | tf_op jit(solution)/shard_map/pallas_call | solution.py:84
  (4 shorter events, 0.0 us)
Async XLA Ops:
  0.0 5.6 %copy-start = (s32[4,4]{1,0:T(4,128)S(1)}, s32[4,4]{1,0:T(4,128)}, u32[]{:S(2)}) copy-start(s32[4,4]{1,0:T(4,128)} %refs_4_.1) | copy-start | bytes 196
  0.0 5.6 %copy-start.3 = (f32[1280]{0:T(1024)S(1)}, f32[1280]{0:T(1024)}, u32[]{:S(2)}) copy-start(f32[1280]{0:T(1024)} %ln_gain.3) | copy-start | bytes 15364
  0.0 5.6 %collective-permute-start = (bf16[1,4,2,5120]{3,2,1,0:T(2,128)(2,1)}, bf16[1,4,2,5120]{3,2,1,0:T(2,128)(2,1)S(1)}, u32[]{:S(2)}, u32[]{:S(2)}) collective-permute-start(bf16[1,4,2,5120]{3,2,1,0:T(2,128)(2,1)} %cache.1), channel_id=1, source_target_pairs={{0,2},{2,0},{1,3},{3,1},{4,6},{6,4},{5,7},{7,5},{8,10},{10,8},{9,1... | collective-permute-start | bytes 245768 | tf_op jit(solution)/shard_map/ppermute | solution.py:74
  2.9 2.5 %collective-permute-start.1 = (f32[1024]{0:T(1024)}, f32[1024]{0:T(1024)S(1)}, u32[]{:S(2)}, u32[]{:S(2)}) collective-permute-start(f32[1024]{0:T(1024)} %refs_6_.1), channel_id=1, source_target_pairs={{0,1},{1,0},{2,3},{3,2},{4,5},{5,4},{6,7},{7,6},{8,9},{9,8},{10,11... | collective-permute-start | bytes 12296 | tf_op jit(solution)/shard_map/ppermute | solution.py:74
  2.9 13.4 %collective-permute-start.5 = (bf16[1280,640]{1,0:T(8,128)(2,1)}, bf16[1280,640]{1,0:T(8,128)(2,1)S(1)}, u32[]{:S(2)}, u32[]{:S(2)}) collective-permute-start(bf16[1280,640]{1,0:T(8,128)(2,1)} %w_fc1.1), channel_id=1, source_target_pairs={{0,1},{1,0},{2,3},{3,2},{4,5},{5,4},{6,7},{7,6},{8,9},{9,8},{10,11... | collective-permute-start | bytes 4915208 | tf_op jit(solution)/shard_map/ppermute | solution.py:74
  5.6 11.4 %collective-permute-start.6 = (bf16[640,1024]{1,0:T(8,128)(2,1)S(1)}, bf16[640,1024]{1,0:T(8,128)(2,1)S(1)}, u32[]{:S(2)}, u32[]{:S(2)}) collective-permute-start(bf16[640,1024]{1,0:T(8,128)(2,1)S(1)} %get-tuple-element.71.w_mine), channel_id=1, source_target_pairs={{0,1},{1,0},{2,3},{3,2},{4,5},{5,4},{6,7},{7,6},{8,9},{9,8},{10,11... | collective-permute-start | bytes 3932168 | tf_op jit(solution)/shard_map/ppermute | solution.py:74
  5.9 6.5 %collective-permute-start.2 = (bf16[16,1280]{1,0:T(8,128)(2,1)S(1)}, bf16[16,1280]{1,0:T(8,128)(2,1)S(1)}, u32[]{:S(2)}, u32[]{:S(2)}) collective-permute-start(bf16[16,1280]{1,0:T(8,128)(2,1)S(1)} %get-tuple-element.62), channel_id=1, source_target_pairs={{0,12},{4,8},{8,4},{12,0},{1,13},{5,9},{9,5},{13,1},{2,14},{6,10},... | collective-permute-start | bytes 122888 | tf_op jit(solution)/shard_map/ppermute | solution.py:74
  10.1 6.3 %collective-permute-start.3 = (bf16[16,1280]{1,0:T(8,128)(2,1)S(1)}, bf16[16,1280]{1,0:T(8,128)(2,1)S(1)}, u32[]{:S(2)}, u32[]{:S(2)}) collective-permute-start(bf16[16,1280]{1,0:T(8,128)(2,1)S(1)} %get-tuple-element.63), channel_id=1, source_target_pairs={{0,8},{4,12},{8,0},{12,4},{1,9},{5,13},{9,1},{13,5},{2,10},{6,14},... | collective-permute-start | bytes 122888 | tf_op jit(solution)/shard_map/ppermute | solution.py:74
  10.1 6.3 %collective-permute-start.4 = (bf16[16,1280]{1,0:T(8,128)(2,1)S(1)}, bf16[16,1280]{1,0:T(8,128)(2,1)S(1)}, u32[]{:S(2)}, u32[]{:S(2)}) collective-permute-start(bf16[16,1280]{1,0:T(8,128)(2,1)S(1)} %get-tuple-element.64), channel_id=1, source_target_pairs={{0,4},{4,0},{8,12},{12,8},{1,5},{5,1},{9,13},{13,9},{2,6},{6,2},{1... | collective-permute-start | bytes 122888 | tf_op jit(solution)/shard_map/ppermute | solution.py:74
  12.3 9.2 %collective-permute-start.13 = (bf16[256,256]{1,0:T(8,128)(2,1)S(1)}, bf16[256,256]{1,0:T(8,128)(2,1)S(1)}, u32[]{:S(2)}, u32[]{:S(2)}) collective-permute-start(bf16[256,256]{1,0:T(8,128)(2,1)S(1)} %get-tuple-element.84), channel_id=1, source_target_pairs={{0,12},{4,8},{8,4},{12,0},{16,24},{20,28},{24,16},{28,20},{1,13},{... | collective-permute-start | bytes 393224 | tf_op jit(solution)/shard_map/ppermute | solution.py:358
  17.0 7.6 %collective-permute-start.7 = (bf16[32,640]{1,0:T(8,128)(2,1)S(1)}, bf16[32,640]{1,0:T(8,128)(2,1)S(1)}, u32[]{:S(2)}, u32[]{:S(2)}) collective-permute-start(bf16[32,640]{1,0:T(8,128)(2,1)S(1)} %get-tuple-element.72), channel_id=1, source_target_pairs={{0,4},{4,0},{8,12},{12,8},{1,5},{5,1},{9,13},{13,9},{2,6},{6,2},{1... | collective-permute-start | bytes 122888 | tf_op jit(solution)/shard_map/ppermute | solution.py:74
  17.1 7.5 %collective-permute-start.8 = (bf16[32,640]{1,0:T(8,128)(2,1)S(1)}, bf16[32,640]{1,0:T(8,128)(2,1)S(1)}, u32[]{:S(2)}, u32[]{:S(2)}) collective-permute-start(bf16[32,640]{1,0:T(8,128)(2,1)S(1)} %get-tuple-element.73), channel_id=1, source_target_pairs={{0,12},{4,8},{8,4},{12,0},{1,13},{5,9},{9,5},{13,1},{2,14},{6,10},... | collective-permute-start | bytes 122888 | tf_op jit(solution)/shard_map/ppermute | solution.py:74
  19.2 5.4 %collective-permute-start.9 = (bf16[32,640]{1,0:T(8,128)(2,1)S(1)}, bf16[32,640]{1,0:T(8,128)(2,1)S(1)}, u32[]{:S(2)}, u32[]{:S(2)}) collective-permute-start(bf16[32,640]{1,0:T(8,128)(2,1)S(1)} %get-tuple-element.74), channel_id=1, source_target_pairs={{0,8},{4,12},{8,0},{12,4},{1,9},{5,13},{9,1},{13,5},{2,10},{6,14},... | collective-permute-start | bytes 122888 | tf_op jit(solution)/shard_map/ppermute | solution.py:74
  20.5 8.9 %collective-permute-start.12 = (bf16[256,256]{1,0:T(8,128)(2,1)S(1)}, bf16[256,256]{1,0:T(8,128)(2,1)S(1)}, u32[]{:S(2)}, u32[]{:S(2)}) collective-permute-start(bf16[256,256]{1,0:T(8,128)(2,1)S(1)} %get-tuple-element.76), channel_id=1, source_target_pairs={{0,4},{4,0},{8,12},{12,8},{1,5},{5,1},{9,13},{13,9},{2,6},{6,2},{1... | collective-permute-start | bytes 393224 | tf_op jit(solution)/shard_map/ppermute | solution.py:74
  21.5 11.3 %collective-permute-start.14 = (bf16[256,256]{1,0:T(8,128)(2,1)S(1)}, bf16[256,256]{1,0:T(8,128)(2,1)S(1)}, u32[]{:S(2)}, u32[]{:S(2)}) collective-permute-start(bf16[256,256]{1,0:T(8,128)(2,1)S(1)} %collective-permute-done.13), channel_id=1, source_target_pairs={{0,16},{16,0},{1,17},{17,1},{2,18},{18,2},{3,19},{19,3},{4,20},{20... | collective-permute-start | bytes 393224 | tf_op jit(solution)/shard_map/ppermute | solution.py:74
  24.7 4.7 %collective-permute-start.10 = (bf16[32,640]{1,0:T(8,128)(2,1)S(1)}, bf16[32,640]{1,0:T(8,128)(2,1)S(1)}, u32[]{:S(2)}, u32[]{:S(2)}) collective-permute-start(bf16[32,640]{1,0:T(8,128)(2,1)S(1)} %shard_map.85), channel_id=1, source_target_pairs={{0,0},{2,8},{4,2},{6,10},{8,4},{10,12},{12,6},{14,14},{1,1},{3,9},... | collective-permute-start | bytes 122888 | tf_op jit(solution)/shard_map/ppermute | solution.py:380
  25.4 6.6 %collective-permute-start.11 = (bf16[32,640]{1,0:T(8,128)(2,1)S(1)}, bf16[32,640]{1,0:T(8,128)(2,1)S(1)}, u32[]{:S(2)}, u32[]{:S(2)}) collective-permute-start(bf16[32,640]{1,0:T(8,128)(2,1)S(1)} %shard_map.85), channel_id=1, source_target_pairs={{0,2},{2,10},{4,0},{6,8},{8,6},{10,14},{12,4},{14,12},{1,3},{3,11}... | collective-permute-start | bytes 122888 | tf_op jit(solution)/shard_map/ppermute | solution.py:380
  29.4 13.8 %copy-start.1 = (f32[1024]{0:T(1024)S(1)}, f32[1024]{0:T(1024)}, u32[]{:S(2)}) copy-start(f32[1024]{0:T(1024)} %refs_6_.1) | copy-start | bytes 12292
  32.8 15.1 %copy-start.2 = (s32[1,4,1]{1,2,0:T(1,128)S(1)}, s32[1,4,1]{1,2,0:T(1,128)}, u32[]{:S(2)}) copy-start(s32[1,4,1]{1,2,0:T(1,128)} %param.15) | copy-start | bytes 52
  32.9 10.3 %collective-permute-start.18 = (bf16[1024,256]{1,0:T(8,128)(2,1)S(1)}, bf16[1024,256]{1,0:T(8,128)(2,1)S(1)}, u32[]{:S(2)}, u32[]{:S(2)}) collective-permute-start(bf16[1024,256]{1,0:T(8,128)(2,1)S(1)} %constant_dynamic-update-slice_fusion.refs_4_), channel_id=1, source_target_pairs={{0,1},{1,0},{2,3},{3,2},{4,5},{5,4},{6,7},{7,6},{8,9},{9,8},{10,11... | collective-permute-start | bytes 1572872 | tf_op jit(solution)/shard_map/ppermute | solution.py:74
  32.9 5.5 %collective-permute-start.15 = (bf16[64,512]{1,0:T(8,128)(2,1)S(1)}, bf16[64,512]{1,0:T(8,128)(2,1)S(1)}, u32[]{:S(2)}, u32[]{:S(2)}) collective-permute-start(bf16[64,512]{1,0:T(8,128)(2,1)S(1)} %get-tuple-element.85), channel_id=1, source_target_pairs={{0,8},{4,12},{8,0},{12,4},{1,9},{5,13},{9,1},{13,5},{2,10},{6,14},... | collective-permute-start | bytes 196616 | tf_op jit(solution)/shard_map/ppermute | solution.py:74
  34.9 4.8 %collective-permute-start.16 = (bf16[64,512]{1,0:T(8,128)(2,1)S(1)}, bf16[64,512]{1,0:T(8,128)(2,1)S(1)}, u32[]{:S(2)}, u32[]{:S(2)}) collective-permute-start(bf16[64,512]{1,0:T(8,128)(2,1)S(1)} %get-tuple-element.86), channel_id=1, source_target_pairs={{0,4},{4,0},{8,12},{12,8},{1,5},{5,1},{9,13},{13,9},{2,6},{6,2},{1... | collective-permute-start | bytes 196616 | tf_op jit(solution)/shard_map/ppermute | solution.py:74
  35.8 7.3 %collective-permute-start.17 = (bf16[64,512]{1,0:T(8,128)(2,1)S(1)}, bf16[64,512]{1,0:T(8,128)(2,1)S(1)}, u32[]{:S(2)}, u32[]{:S(2)}) collective-permute-start(bf16[64,512]{1,0:T(8,128)(2,1)S(1)} %get-tuple-element.87), channel_id=1, source_target_pairs={{0,12},{4,8},{8,4},{12,0},{1,13},{5,9},{9,5},{13,1},{2,14},{6,10},... | collective-permute-start | bytes 196616 | tf_op jit(solution)/shard_map/ppermute | solution.py:74
  43.5 4.4 %collective-permute-start.19 = (bf16[32,1152]{1,0:T(8,128)(2,1)S(1)}, bf16[32,1152]{1,0:T(8,128)(2,1)S(1)}, u32[]{:S(2)}, u32[]{:S(2)}) collective-permute-start(bf16[32,1152]{1,0:T(8,128)(2,1)S(1)} %get-tuple-element.94), channel_id=1, source_target_pairs={{0,2},{2,0},{1,3},{3,1},{4,6},{6,4},{5,7},{7,5},{8,10},{10,8},{9,1... | collective-permute-start | bytes 221192 | tf_op jit(solution)/shard_map/ppermute | solution.py:74
  48.1 5.6 %collective-permute-start.20 = (bf16[8,1152]{1,0:T(8,128)(2,1)S(1)}, bf16[8,1152]{1,0:T(8,128)(2,1)S(1)}, u32[]{:S(2)}, u32[]{:S(2)}) collective-permute-start(bf16[8,1152]{1,0:T(8,128)(2,1)S(1)} %get-tuple-element.95), channel_id=1, source_target_pairs={{0,12},{4,8},{8,4},{12,0},{1,13},{5,9},{9,5},{13,1},{2,14},{6,10},... | collective-permute-start | bytes 55304 | tf_op jit(solution)/shard_map/ppermute | solution.py:74
  49.3 4.8 %collective-permute-start.21 = (bf16[8,1152]{1,0:T(8,128)(2,1)S(1)}, bf16[8,1152]{1,0:T(8,128)(2,1)S(1)}, u32[]{:S(2)}, u32[]{:S(2)}) collective-permute-start(bf16[8,1152]{1,0:T(8,128)(2,1)S(1)} %get-tuple-element.96), channel_id=1, source_target_pairs={{0,8},{4,12},{8,0},{12,4},{1,9},{5,13},{9,1},{13,5},{2,10},{6,14},... | collective-permute-start | bytes 55304 | tf_op jit(solution)/shard_map/ppermute | solution.py:74
  49.3 5.0 %collective-permute-start.22 = (bf16[8,1152]{1,0:T(8,128)(2,1)S(1)}, bf16[8,1152]{1,0:T(8,128)(2,1)S(1)}, u32[]{:S(2)}, u32[]{:S(2)}) collective-permute-start(bf16[8,1152]{1,0:T(8,128)(2,1)S(1)} %get-tuple-element.97), channel_id=1, source_target_pairs={{0,4},{4,0},{8,12},{12,8},{1,5},{5,1},{9,13},{13,9},{2,6},{6,2},{1... | collective-permute-start | bytes 55304 | tf_op jit(solution)/shard_map/ppermute | solution.py:74

commit v5 on v4

--- a/solution.py
+++ b/solution.py
@@ -212,7 +212,7 @@
     source = lax.broadcasted_iota(jnp.int32, (2 * half, half), 1)
     u, owner = to // half, (to % half) // (4 * bb)
     holder, b_of = (to % (4 * bb)) // bb, to % bb
-    wanted = (u ^ (h >> 1)) * half + (holder * 4 + owner) * bb + b_of
+    wanted = (u ^ (h & 1)) * half + (holder * 4 + owner) * bb + b_of
     moved = 0.0
     for p, part in enumerate((first, second)):
         order = jnp.where(source + p * half == wanted, 1.0, 0.0)
@@ -234,8 +234,8 @@
 
 
 def key_kernel(*refs):
-    parts, blocks, gains = refs[:4], refs[4:6], refs[6:8]
-    kept, sent, held = refs[8:]
+    parts, blocks, gains, matching, counts = refs[:4], refs[4:6], refs[6:8], refs[8], refs[9]
+    outs, held = refs[10:14], refs[14]
     h, grp = lax.axis_index("hold"), lax.axis_index("grp")
     merged = sum(part[...].astype(jnp.float32) for part in parts)
     squares = jnp.sum(merged * merged, axis=1, keepdims=True)
@@ -250,50 +250,52 @@
         held[:, pl.ds(pl.multiple_of(place * width, 128), width)] = sum(
             dot(rows[p], blocks[p][i * cols : (i + 1) * cols, :]) for p in range(2)
         )
-    half = kept.shape[0]
     keys = 4 * width
-    kept[:, :keys] = held[:half, :]
-    kept[:, keys:] = jnp.broadcast_to(squares[:half], (half, 128))
-    sent[:, :keys] = held[half:, :].astype(jnp.bfloat16)
-    sent[:, keys:] = two_terms(squares[half:]).astype(jnp.bfloat16)
-
-
-def group_kernel(kept, came, matching, counts, *refs):
-    outs, held = refs[:4], refs[4]
-    h = lax.axis_index("hold")
-    keys = kept.shape[1] - 128
-    held[:, :keys] = kept[:, :keys] + came[:, :keys].astype(jnp.float32)
-    pair = came[:, keys:].astype(jnp.float32)
-    held[:, keys:] = two_terms(kept[:, keys : keys + 1] + pair[:, :1] + pair[:, 127:])
-    rows = outs[0].shape[0]
+    held[:, keys:] = two_terms(squares)
+    half, few = held.shape[0] // 2, held.shape[0] // 8
     rounds = matching.shape[0]
     column = lax.broadcasted_iota(jnp.int32, matching.shape, 1) == h
     owner = jnp.sum(jnp.where(column, matching[...], 0), axis=1, keepdims=True)
-    lane = lax.broadcasted_iota(jnp.int32, (rows, 128), 1)
-    for k in range(4):
-        part = held[pl.ds(pl.multiple_of((h ^ k) * rows, 8), rows), :]
+    lane = lax.broadcasted_iota(jnp.int32, (2 * few, 128), 1)
+    for k, out in enumerate(outs):
+        start = pl.multiple_of((h ^ k) * few, 8)
+        part = jnp.concatenate(
+            [held[pl.ds(start, few), :], held[pl.ds(half + start, few), :]], axis=0
+        )
         live = sum(
             jnp.where(owner[r : r + 1] == (h ^ k), counts[:, r : r + 1], 0) for r in range(rounds)
         )
+        out[:, :keys] = part[:, :keys].astype(out.dtype)
         tail = jnp.where(lane == 32, live.astype(jnp.float32), part[:, keys:])
-        outs[k][:, :keys] = part[:, :keys].astype(jnp.bfloat16)
-        outs[k][:, keys:] = tail.astype(jnp.bfloat16)
-
-
-def last_kernel(width, places, *refs):
-    parts, matching, out, held = refs[:4], refs[4], refs[5], refs[6]
+        out[:, keys:] = tail.astype(out.dtype)
+
+
+def group_kernel(places, *refs):
+    parts, kept, sent, live = refs[:4], refs[4], refs[5], refs[6]
+    h = lax.axis_index("hold")
+    keys = kept.shape[1] - 128
+    total = sum(part[...].astype(jnp.float32) for part in parts)
+    for k, part in zip((*places, 0), parts, strict=True):
+        live[pl.ds(h ^ k, 1), :] = part[:1, keys:].astype(jnp.float32)
+    squares = two_terms(total[:, keys : keys + 1] + total[:, -1:])
+    rows = kept.shape[0]
+    kept[:, :keys] = total[:rows, :keys]
+    kept[:, keys:] = squares[:rows]
+    sent[:, :keys] = total[rows:, :keys].astype(jnp.bfloat16)
+    sent[:, keys:] = squares[rows:].astype(jnp.bfloat16)
+
+
+def last_kernel(width, kept, came, matching, live, out):
     h = lax.axis_index("hold")
     _, rounds, block, features = out.shape
-    total = sum(part[...].astype(jnp.float32) for part in parts)
+    total = kept[...] + came[...].astype(jnp.float32)
     squares = total[:, features : features + 1] + total[:, -1:]
     keys = total[:, :features] * lax.rsqrt(squares / width + EPSILON)
-    for k, part in zip((*places, 0), parts, strict=True):
-        held[pl.ds(h ^ k, 1), :] = part[:1, features:].astype(jnp.float32)
     b_of = lax.broadcasted_iota(jnp.int32, (block, 1), 0).astype(jnp.float32)
     blocks = []
     for i in range(rounds):
-        live = held[i : i + 1, 32:33]
-        blocks.append(jnp.where(b_of < live, keys[i * block : (i + 1) * block], 0.0))
+        part = keys[i * block : (i + 1) * block]
+        blocks.append(jnp.where(b_of < live[i : i + 1, 32:33], part, 0.0))
     for r in range(rounds):
         picked = sum(
             jnp.where(matching[r : r + 1, i : i + 1] == h, blocks[i], 0.0) for i in range(rounds)
@@ -337,8 +339,8 @@
     )
     w_fc1_other = swap(w_fc1, "rep", 2, 1)
     gain_other = swap(norm_gain, "rep", 2, 1)
-    own, cache_other, w_fc2_sent, gain_other = lax.optimization_barrier(
-        (own, cache_other, w_fc2_mine, gain_other)
+    own, cache_other, w_fc2_sent, w_fc1_other, gain_other = lax.optimization_barrier(
+        (own, cache_other, w_fc2_mine, w_fc1_other, gain_other)
     )
     w_fc2_other = swap(w_fc2_sent, "rep", 2, 1)
     pieces = call(
@@ -349,7 +351,6 @@
         ln_gain,
         matching,
         scratch=[vmem((rows, depth), f32)],
-        flops=long,
     )
 
     *pieces, key_1, key_far = lax.optimization_barrier((*pieces, key_1, key_far))
@@ -370,12 +371,15 @@
     *partial, w_fc2_other = lax.optimization_barrier((*partial, w_fc2_other))
     key_near = swap(key_far, "grp", 2, 1)
     parts = exchange(partial, (1, 3, 2))
-    hidden = call(gelu_kernel, like(parts[0].shape), *parts)
+    hidden = call(gelu_kernel, like(parts[0].shape), *parts, flops=long)
+    hidden, key_far = lax.optimization_barrier((hidden, key_far))
 
     halves = []
     for g in range(2):
         perm = [
-            (2 * a + b, 2 * (2 * b + (a >> 1)) + ((a & 1) ^ g)) for a in range(n) for b in range(2)
+            (2 * a + b, 2 * (2 * b + (a >> 1)) + ((a & 1) ^ (a >> 1) ^ b ^ g))
+            for a in range(n)
+            for b in range(2)
         ]
         halves.append(lax.ppermute(hidden, ("hold", "tp"), perm))
     *halves, key_1 = lax.optimization_barrier((*halves, key_1))
@@ -391,33 +395,33 @@
     *merged, key_near = lax.optimization_barrier((*merged, key_near))
     key_mine = jnp.concatenate([key_0, key_1, key_far, key_near])
     key_other = swap(key_mine, "rep", 2, 1)
-    kept, sent = call(
+    wide = n * key_cols + 128
+    keys = call(
         key_kernel,
-        [like((4 * rows, n * key_cols + 128), f32), like((4 * rows, n * key_cols + 128))],
+        [like((2 * rows, wide), f32)] + [like((2 * rows, wide))] * (n - 1),
         *exchange(merged, (2, 1, 3)),
         key_mine,
         key_other,
         norm_gain,
         gain_other,
-        scratch=[vmem((8 * rows, n * key_cols), f32)],
+        matching,
+        counts.reshape(1, rounds),
+        scratch=[vmem((8 * rows, wide), f32)],
         flops=32 * rows * w_key.size,
     )
-    keys = call(
-        group_kernel,
-        [like((rows, n * key_cols + 128))] * n,
+    order = (3, 2, 1)
+    kept, sent, live = call(
+        functools.partial(group_kernel, order),
+        [like((rows, wide), f32), like((rows, wide)), like((n, 128), f32)],
+        *exchange(keys, order),
+    )
+    return call(
+        functools.partial(last_kernel, width),
+        like((1, rounds, block, n * key_cols)),
         kept,
         swap(sent, "tp", 2, 1),
         matching,
-        counts.reshape(1, rounds),
-        scratch=[vmem((4 * rows, n * key_cols + 128), f32)],
-    )
-    order = (3, 2, 1)
-    return call(
-        functools.partial(last_kernel, width, order),
-        like((1, rounds, block, n * key_cols)),
-        *exchange(keys, order),
-        matching,
-        scratch=[vmem((rounds, 128), f32)],
+        live,
     )
 
 

time: 55.2 us -> 54.9 us (level)
  waiting for transfers between devices: 15.2 us -> 14.6 us
    ppermute x20, starting transfers between devices: 25.9 us -> 28.8 us  [swap(): return lax.ppermute(x, axis, [(i, i ^ step) for i in range(n)])]
    ppermute x2, starting transfers between devices: 4.63 us -> 2.19 us  [rows_past_weights(): halves.append(lax.ppermute(hidden, ('hold', 'tp'), perm))]
    ppermute x2, waiting for transfers between devices: 2.57 us -> 1.91 us  [rows_past_weights(): halves.append(lax.ppermute(hidden, ('hold', 'tp'), perm))]
  transfers between devices with their start and end apart: 23 -> 23, of which waited for: 10 -> 9; matrix products, arithmetic and copies ran while one was open for 0% -> 0% of each run, Pallas kernels for 7% -> 7%
where the time goes in v5:
time: 54.9 us; the launch traced here: 54.7 us
  starting transfers between devices  34.7 us (63%)
  waiting for transfers between devices  14.6 us (27%)
  Pallas kernels  5.17 us (9%)
    ppermute x20, starting transfers between devices, swap(): return lax.ppermute(x, axis, [(i, i ^ step) for i in range(n)])  28.8 us
    ppermute x20, waiting for transfers between devices, swap(): return lax.ppermute(x, axis, [(i, i ^ step) for i in range(n)])  12.7 us
    pallas_call x8, Pallas kernels, call(): pl.pallas_call(body, out_shape=outs, scratch_shapes=scratch, cost_estimat...  5.17 us
    ppermute x1, starting transfers between devices, rows_past_weights(): key_far = lax.ppermute(key_far, ('grp', 'hold'), perm)  3.74 us
    ppermute x2, starting transfers between devices, rows_past_weights(): halves.append(lax.ppermute(hidden, ('hold', 'tp'), perm))  2.19 us
    ppermute x2, waiting for transfers between devices, rows_past_weights(): halves.append(lax.ppermute(hidden, ('hold', 'tp'), perm))  1.91 us
  transfers between devices with their start and end apart: 23, of which 9 were waited for; matrix products, arithmetic and copies ran while one was open for 0% of the time, Pallas kernels for 7%

profile of v5, /device:TPU:0, one launch (start us, length us, event | category | flops | bytes accessed | tf_op | source)
XLA Modules:
  0.0 54.7 jit_solution(736070393033554684)
XLA Ops:
  0.0 0.0 copy-start
  0.0 0.0 copy-start.1
  0.0 0.5 collective-permute-start.1
  0.5 0.1 collective-permute-start.2
  0.5 2.9 %collective-permute-start = (bf16[1,4,2,5120]{3,2,1,0:T(2,128)(2,1)}, bf16[1,4,2,5120]{3,2,1,0:T(2,128)(2,1)S(1)}, u32[]{:S(2)}, u32[]{:S(2)}) collective-permute-start(bf16[1,4,2,5120]{3,2,1,0:T(2,128)(2,1)} %cache.1), channel_id=1, source_target_pairs={{0,2},{2,0},{1,3},{3,1},{4,6},{6,4},{5,7},{7,5},{8,10},{10,8},{9,1... | collective-permute-start | bytes 245768 | tf_op jit(solution)/shard_map/ppermute | solution.py:74
  3.5 2.0 %shard_map.82 = (f32[8,5120]{1,0:T(8,128)S(1)}, bf16[1280,640]{1,0:T(8,128)(2,1)S(1)}, bf16[640,1024]{1,0:T(8,128)(2,1)S(1)}, bf16[256,256]{1,0:T(8,128)(2,1)S(1...) custom-call(bf16[1,4,2,5120]{3,2,1,0:T(2,128)(2,1)} %cache.1, f32[1280]{0:T(1024)} %ln_gain.3, ...), custom_call_target="tpu_custom_call" | custom-call | flops 8589934592 | bytes 3560512 | tf_op jit(solution)/shard_map/pallas_call | solution.py:84
  5.5 0.0 collective-permute-done.2.refs_7_
  5.5 0.9 %collective-permute-done.cache = bf16[1,4,2,5120]{3,2,1,0:T(2,128)(2,1)S(1)} collective-permute-done((bf16[1,4,2,5120]{3,2,1,0:T(2,128)(2,1)}, bf16[1,4,2,5120]{3,2,1,0:T(2,128)(2,1)S(1)}, u32[]{:S(2)}, u32[]{:S(2)}) %collective-permute-start) | collective-permute-done | bytes 81952 | tf_op jit(solution)/shard_map/ppermute | solution.py:74
  6.3 0.0 collective-permute-done.1.refs_5_
  6.3 0.0 collective-permute-start.6
  6.4 0.0 copy-done
  6.4 0.0 copy-done.1
  6.4 0.3 shard_map.83
  6.6 3.9 %collective-permute-start.3 = (bf16[16,1280]{1,0:T(8,128)(2,1)S(1)}, bf16[16,1280]{1,0:T(8,128)(2,1)S(1)}, u32[]{:S(2)}, u32[]{:S(2)}) collective-permute-start(bf16[16,1280]{1,0:T(8,128)(2,1)S(1)} %get-tuple-element.66), channel_id=1, source_target_pairs={{0,12},{4,8},{8,4},{12,0},{1,13},{5,9},{9,5},{13,1},{2,14},{6,10},... | collective-permute-start | bytes 122888 | tf_op jit(solution)/shard_map/ppermute | solution.py:74
  10.6 0.0 collective-permute-start.4
  10.6 0.6 %collective-permute-start.5 = (bf16[16,1280]{1,0:T(8,128)(2,1)S(1)}, bf16[16,1280]{1,0:T(8,128)(2,1)S(1)}, u32[]{:S(2)}, u32[]{:S(2)}) collective-permute-start(bf16[16,1280]{1,0:T(8,128)(2,1)S(1)} %get-tuple-element.68), channel_id=1, source_target_pairs={{0,4},{4,0},{8,12},{12,8},{1,5},{5,1},{9,13},{13,9},{2,6},{6,2},{1... | collective-permute-start | bytes 122888 | tf_op jit(solution)/shard_map/ppermute | solution.py:74
  11.2 3.7 %collective-permute-start.10 = (bf16[256,256]{1,0:T(8,128)(2,1)S(1)}, bf16[256,256]{1,0:T(8,128)(2,1)S(1)}, u32[]{:S(2)}, u32[]{:S(2)}) collective-permute-start(bf16[256,256]{1,0:T(8,128)(2,1)S(1)} %get-tuple-element.81), channel_id=1, source_target_pairs={{0,12},{4,8},{8,4},{12,0},{16,24},{20,28},{24,16},{28,20},{1,13},{... | collective-permute-start | bytes 393224 | tf_op jit(solution)/shard_map/ppermute | solution.py:359
  15.0 0.0 collective-permute-done.3.refs_0_
  15.0 0.9 %collective-permute-done.4.refs_1_ = bf16[16,1280]{1,0:T(8,128)(2,1)S(1)} collective-permute-done((bf16[16,1280]{1,0:T(8,128)(2,1)S(1)}, bf16[16,1280]{1,0:T(8,128)(2,1)S(1)}, u32[]{:S(2)}, u32[]{:S(2)}) %collective-permute-start.4) | collective-permute-done | bytes 40992 | tf_op jit(solution)/shard_map/ppermute | solution.py:74
  15.9 0.0 collective-permute-done.5.refs_2_
  15.9 0.7 %shard_map.84 = (bf16[32,640]{1,0:T(8,128)(2,1)S(1)}, bf16[32,640]{1,0:T(8,128)(2,1)S(1)}, bf16[32,640]{1,0:T(8,128)(2,1)S(1)}, bf16[32,640]{1,0:T(8,128)(2,1)S(1)}) custom-call(bf16[16,1280]{1,0:T(8,128)(2,1)S(1)} %collective-permute-done.3.refs_0_, bf16[16,1280]{1,0:T(8,128)(2,1)S(1)} %collective-permute-done.4.refs_1_, ...), custom_call_target="tpu_custom_call" | custom-call | flops 8589934592 | bytes 3440640 | tf_op jit(solution)/shard_map/pallas_call | solution.py:84
  16.5 0.0 collective-permute-done.6.w_other
  16.5 0.5 collective-permute-start.7
  17.1 3.1 %collective-permute-start.8 = (bf16[32,640]{1,0:T(8,128)(2,1)S(1)}, bf16[32,640]{1,0:T(8,128)(2,1)S(1)}, u32[]{:S(2)}, u32[]{:S(2)}) collective-permute-start(bf16[32,640]{1,0:T(8,128)(2,1)S(1)} %get-tuple-element.78), channel_id=1, source_target_pairs={{0,12},{4,8},{8,4},{12,0},{1,13},{5,9},{9,5},{13,1},{2,14},{6,10},... | collective-permute-start | bytes 122888 | tf_op jit(solution)/shard_map/ppermute | solution.py:74
  20.1 0.0 collective-permute-start.9
  20.1 1.3 %collective-permute-start.13 = (bf16[256,256]{1,0:T(8,128)(2,1)S(1)}, bf16[256,256]{1,0:T(8,128)(2,1)S(1)}, u32[]{:S(2)}, u32[]{:S(2)}) collective-permute-start(bf16[256,256]{1,0:T(8,128)(2,1)S(1)} %get-tuple-element.83), channel_id=1, source_target_pairs={{0,4},{4,0},{8,12},{12,8},{1,5},{5,1},{9,13},{13,9},{2,6},{6,2},{1... | collective-permute-start | bytes 393224 | tf_op jit(solution)/shard_map/ppermute | solution.py:74
  21.5 0.0 collective-permute-done.10
  21.5 2.5 %collective-permute-start.14 = (bf16[256,256]{1,0:T(8,128)(2,1)S(1)}, bf16[256,256]{1,0:T(8,128)(2,1)S(1)}, u32[]{:S(2)}, u32[]{:S(2)}) collective-permute-start(bf16[256,256]{1,0:T(8,128)(2,1)S(1)} %collective-permute-done.10), channel_id=1, source_target_pairs={{0,16},{16,0},{1,17},{17,1},{2,18},{18,2},{3,19},{19,3},{4,20},{20... | collective-permute-start | bytes 393224 | tf_op jit(solution)/shard_map/ppermute | solution.py:74
  23.9 0.0 collective-permute-done.7.refs_0_
  24.0 0.0 collective-permute-done.8.refs_1_
  24.0 1.2 %collective-permute-done.9.refs_2_ = bf16[32,640]{1,0:T(8,128)(2,1)S(1)} collective-permute-done((bf16[32,640]{1,0:T(8,128)(2,1)S(1)}, bf16[32,640]{1,0:T(8,128)(2,1)S(1)}, u32[]{:S(2)}, u32[]{:S(2)}) %collective-permute-start.9) | collective-permute-done | bytes 40992 | tf_op jit(solution)/shard_map/ppermute | solution.py:74
  25.1 0.2 shard_map.85
  25.3 1.5 %collective-permute-start.12 = (bf16[32,640]{1,0:T(8,128)(2,1)S(1)}, bf16[32,640]{1,0:T(8,128)(2,1)S(1)}, u32[]{:S(2)}, u32[]{:S(2)}) collective-permute-start(bf16[32,640]{1,0:T(8,128)(2,1)S(1)} %shard_map.85), channel_id=1, source_target_pairs={{0,2},{2,8},{4,0},{6,10},{8,4},{10,14},{12,6},{14,12},{1,3},{3,9},... | collective-permute-start | bytes 122888 | tf_op jit(solution)/shard_map/ppermute | solution.py:384
  26.9 0.7 %collective-permute-start.11 = (bf16[32,640]{1,0:T(8,128)(2,1)S(1)}, bf16[32,640]{1,0:T(8,128)(2,1)S(1)}, u32[]{:S(2)}, u32[]{:S(2)}) collective-permute-start(bf16[32,640]{1,0:T(8,128)(2,1)S(1)} %shard_map.85), channel_id=1, source_target_pairs={{0,0},{2,10},{4,2},{6,8},{8,6},{10,12},{12,4},{14,14},{1,1},{3,11}... | collective-permute-start | bytes 122888 | tf_op jit(solution)/shard_map/ppermute | solution.py:384
  27.6 0.0 copy-start.2
  27.6 0.0 copy-start.3
  27.6 0.0 collective-permute-done.13
  27.6 1.9 %collective-permute-done.12.second = bf16[32,640]{1,0:T(8,128)(2,1)S(1)} collective-permute-done((bf16[32,640]{1,0:T(8,128)(2,1)S(1)}, bf16[32,640]{1,0:T(8,128)(2,1)S(1)}, u32[]{:S(2)}, u32[]{:S(2)}) %collective-permute-start.12) | collective-permute-done | bytes 40992 | tf_op jit(solution)/shard_map/ppermute | solution.py:384
  29.5 0.0 collective-permute-done.11.first
  29.5 0.8 %shard_map.86 = (bf16[64,512]{1,0:T(8,128)(2,1)S(1)}, bf16[64,512]{1,0:T(8,128)(2,1)S(1)}, bf16[64,512]{1,0:T(8,128)(2,1)S(1)}, bf16[64,512]{1,0:T(8,128)(2,1)S(1)}) custom-call(bf16[32,640]{1,0:T(8,128)(2,1)S(1)} %collective-permute-done.11.first, bf16[32,640]{1,0:T(8,128)(2,1)S(1)} %collective-permute-done.12.second, ...), custom_call_target="tpu_custom_call" | custom-call | flops 167772160 | bytes 2703360 | tf_op jit(solution)/shard_map/pallas_call | solution.py:84
  30.3 0.0 collective-permute-done.14
  30.3 0.1 collective-permute-start.18
  30.4 4.1 %collective-permute-start.15 = (bf16[64,512]{1,0:T(8,128)(2,1)S(1)}, bf16[64,512]{1,0:T(8,128)(2,1)S(1)}, u32[]{:S(2)}, u32[]{:S(2)}) collective-permute-start(bf16[64,512]{1,0:T(8,128)(2,1)S(1)} %get-tuple-element.91), channel_id=1, source_target_pairs={{0,8},{4,12},{8,0},{12,4},{1,9},{5,13},{9,1},{13,5},{2,10},{6,14},... | collective-permute-start | bytes 196616 | tf_op jit(solution)/shard_map/ppermute | solution.py:74
  34.5 2.0 %collective-permute-start.16 = (bf16[64,512]{1,0:T(8,128)(2,1)S(1)}, bf16[64,512]{1,0:T(8,128)(2,1)S(1)}, u32[]{:S(2)}, u32[]{:S(2)}) collective-permute-start(bf16[64,512]{1,0:T(8,128)(2,1)S(1)} %get-tuple-element.92), channel_id=1, source_target_pairs={{0,4},{4,0},{8,12},{12,8},{1,5},{5,1},{9,13},{13,9},{2,6},{6,2},{1... | collective-permute-start | bytes 196616 | tf_op jit(solution)/shard_map/ppermute | solution.py:74
  36.5 1.0 %collective-permute-start.17 = (bf16[64,512]{1,0:T(8,128)(2,1)S(1)}, bf16[64,512]{1,0:T(8,128)(2,1)S(1)}, u32[]{:S(2)}, u32[]{:S(2)}) collective-permute-start(bf16[64,512]{1,0:T(8,128)(2,1)S(1)} %get-tuple-element.93), channel_id=1, source_target_pairs={{0,12},{4,8},{8,4},{12,0},{1,13},{5,9},{9,5},{13,1},{2,14},{6,10},... | collective-permute-start | bytes 196616 | tf_op jit(solution)/shard_map/ppermute | solution.py:74
  37.5 0.0 collective-permute-done.15.refs_0_
  37.5 1.4 %collective-permute-done.16.refs_1_ = bf16[64,512]{1,0:T(8,128)(2,1)S(1)} collective-permute-done((bf16[64,512]{1,0:T(8,128)(2,1)S(1)}, bf16[64,512]{1,0:T(8,128)(2,1)S(1)}, u32[]{:S(2)}, u32[]{:S(2)}) %collective-permute-start.16) | collective-permute-done | bytes 65568 | tf_op jit(solution)/shard_map/ppermute | solution.py:74
  38.9 3.9 %collective-permute-done.17.refs_2_ = bf16[64,512]{1,0:T(8,128)(2,1)S(1)} collective-permute-done((bf16[64,512]{1,0:T(8,128)(2,1)S(1)}, bf16[64,512]{1,0:T(8,128)(2,1)S(1)}, u32[]{:S(2)}, u32[]{:S(2)}) %collective-permute-start.17) | collective-permute-done | bytes 65568 | tf_op jit(solution)/shard_map/ppermute | solution.py:74
  42.8 0.0 collective-permute-done.18.refs_5_
  42.8 0.0 copy-done.2
  42.8 0.0 copy-done.3
  42.8 0.3 shard_map.87
  43.1 1.8 %collective-permute-start.19 = (bf16[16,1152]{1,0:T(8,128)(2,1)S(1)}, bf16[16,1152]{1,0:T(8,128)(2,1)S(1)}, u32[]{:S(2)}, u32[]{:S(2)}) collective-permute-start(bf16[16,1152]{1,0:T(8,128)(2,1)S(1)} %get-tuple-element.100), channel_id=1, source_target_pairs={{0,12},{4,8},{8,4},{12,0},{1,13},{5,9},{9,5},{13,1},{2,14},{6,10},... | collective-permute-start | bytes 110600 | tf_op jit(solution)/shard_map/ppermute | solution.py:74
  44.9 0.0 collective-permute-start.20
  44.9 2.7 %collective-permute-start.21 = (bf16[16,1152]{1,0:T(8,128)(2,1)S(1)}, bf16[16,1152]{1,0:T(8,128)(2,1)S(1)}, u32[]{:S(2)}, u32[]{:S(2)}) collective-permute-start(bf16[16,1152]{1,0:T(8,128)(2,1)S(1)} %get-tuple-element.102), channel_id=1, source_target_pairs={{0,4},{4,0},{8,12},{12,8},{1,5},{5,1},{9,13},{13,9},{2,6},{6,2},{1... | collective-permute-start | bytes 110600 | tf_op jit(solution)/shard_map/ppermute | solution.py:74
  47.6 1.7 %collective-permute-done.19.refs_0_ = bf16[16,1152]{1,0:T(8,128)(2,1)S(1)} collective-permute-done((bf16[16,1152]{1,0:T(8,128)(2,1)S(1)}, bf16[16,1152]{1,0:T(8,128)(2,1)S(1)}, u32[]{:S(2)}, u32[]{:S(2)}) %collective-permute-start.19) | collective-permute-done | bytes 36896 | tf_op jit(solution)/shard_map/ppermute | solution.py:74
  49.2 0.8 %collective-permute-done.20.refs_1_ = bf16[16,1152]{1,0:T(8,128)(2,1)S(1)} collective-permute-done((bf16[16,1152]{1,0:T(8,128)(2,1)S(1)}, bf16[16,1152]{1,0:T(8,128)(2,1)S(1)}, u32[]{:S(2)}, u32[]{:S(2)}) %collective-permute-start.20) | collective-permute-done | bytes 36896 | tf_op jit(solution)/shard_map/ppermute | solution.py:74
  50.0 0.0 collective-permute-done.21.refs_2_
  50.0 0.2 shard_map.88
  50.2 1.7 %collective-permute-start.22 = (bf16[8,1152]{1,0:T(8,128)(2,1)S(1)}, bf16[8,1152]{1,0:T(8,128)(2,1)S(1)}, u32[]{:S(2)}, u32[]{:S(2)}) collective-permute-start(bf16[8,1152]{1,0:T(8,128)(2,1)S(1)} %get-tuple-element.105), channel_id=1, source_target_pairs={{0,2},{2,0},{1,3},{3,1},{4,6},{6,4},{5,7},{7,5},{8,10},{10,8},{9,1... | collective-permute-start | bytes 55304 | tf_op jit(solution)/shard_map/ppermute | solution.py:74
  51.9 2.1 %collective-permute-done.22.came = bf16[8,1152]{1,0:T(8,128)(2,1)S(1)} collective-permute-done((bf16[8,1152]{1,0:T(8,128)(2,1)S(1)}, bf16[8,1152]{1,0:T(8,128)(2,1)S(1)}, u32[]{:S(2)}, u32[]{:S(2)}) %collective-permute-start.22) | collective-permute-done | bytes 18464 | tf_op jit(solution)/shard_map/ppermute | solution.py:74
  53.9 0.8 %shard_map.89 = bf16[1,4,2,1024]{3,2,1,0:T(2,128)(2,1)} custom-call(f32[8,1152]{1,0:T(8,128)S(1)} %get-tuple-element.104.kept, bf16[8,1152]{1,0:T(8,128)(2,1)S(1)} %collective-permute-done.22.came, s32[4,4]{1,0:T(4,128)S(1)} %copy-done, f32[4,128]{1,0:T(4,128)S(1)} %get-tuple-element.106.live), custom_call_target="tpu_custom_call" | custom-call | bytes 57408 | tf_op jit(solution)/shard_map/pallas_call | solution.py:84
  (4 shorter events, 0.0 us)
Async XLA Ops:
  0.0 6.4 %copy-start = (s32[4,4]{1,0:T(4,128)S(1)}, s32[4,4]{1,0:T(4,128)}, u32[]{:S(2)}) copy-start(s32[4,4]{1,0:T(4,128)} %matching.5) | copy-start | bytes 196
  0.0 6.4 %copy-start.1 = (f32[1280]{0:T(1024)S(1)}, f32[1280]{0:T(1024)}, u32[]{:S(2)}) copy-start(f32[1280]{0:T(1024)} %ln_gain.3) | copy-start | bytes 15364
  0.0 6.3 %collective-permute-start.1 = (bf16[1280,640]{1,0:T(8,128)(2,1)}, bf16[1280,640]{1,0:T(8,128)(2,1)S(1)}, u32[]{:S(2)}, u32[]{:S(2)}) collective-permute-start(bf16[1280,640]{1,0:T(8,128)(2,1)} %w_fc1.1), channel_id=1, source_target_pairs={{0,1},{1,0},{2,3},{3,2},{4,5},{5,4},{6,7},{7,6},{8,9},{9,8},{10,11... | collective-permute-start | bytes 4915208 | tf_op jit(solution)/shard_map/ppermute | solution.py:74
  0.5 5.0 %collective-permute-start.2 = (f32[1024]{0:T(1024)}, f32[1024]{0:T(1024)S(1)}, u32[]{:S(2)}, u32[]{:S(2)}) collective-permute-start(f32[1024]{0:T(1024)} %refs_6_.1), channel_id=1, source_target_pairs={{0,1},{1,0},{2,3},{3,2},{4,5},{5,4},{6,7},{7,6},{8,9},{9,8},{10,11... | collective-permute-start | bytes 12296 | tf_op jit(solution)/shard_map/ppermute | solution.py:74
  0.5 5.8 %collective-permute-start = (bf16[1,4,2,5120]{3,2,1,0:T(2,128)(2,1)}, bf16[1,4,2,5120]{3,2,1,0:T(2,128)(2,1)S(1)}, u32[]{:S(2)}, u32[]{:S(2)}) collective-permute-start(bf16[1,4,2,5120]{3,2,1,0:T(2,128)(2,1)} %cache.1), channel_id=1, source_target_pairs={{0,2},{2,0},{1,3},{3,1},{4,6},{6,4},{5,7},{7,5},{8,10},{10,8},{9,1... | collective-permute-start | bytes 245768 | tf_op jit(solution)/shard_map/ppermute | solution.py:74
  6.3 10.2 %collective-permute-start.6 = (bf16[640,1024]{1,0:T(8,128)(2,1)S(1)}, bf16[640,1024]{1,0:T(8,128)(2,1)S(1)}, u32[]{:S(2)}, u32[]{:S(2)}) collective-permute-start(bf16[640,1024]{1,0:T(8,128)(2,1)S(1)} %get-tuple-element.76.w_mine), channel_id=1, source_target_pairs={{0,1},{1,0},{2,3},{3,2},{4,5},{5,4},{6,7},{7,6},{8,9},{9,8},{10,11... | collective-permute-start | bytes 3932168 | tf_op jit(solution)/shard_map/ppermute | solution.py:74
  6.6 8.3 %collective-permute-start.3 = (bf16[16,1280]{1,0:T(8,128)(2,1)S(1)}, bf16[16,1280]{1,0:T(8,128)(2,1)S(1)}, u32[]{:S(2)}, u32[]{:S(2)}) collective-permute-start(bf16[16,1280]{1,0:T(8,128)(2,1)S(1)} %get-tuple-element.66), channel_id=1, source_target_pairs={{0,12},{4,8},{8,4},{12,0},{1,13},{5,9},{9,5},{13,1},{2,14},{6,10},... | collective-permute-start | bytes 122888 | tf_op jit(solution)/shard_map/ppermute | solution.py:74
  10.6 5.3 %collective-permute-start.4 = (bf16[16,1280]{1,0:T(8,128)(2,1)S(1)}, bf16[16,1280]{1,0:T(8,128)(2,1)S(1)}, u32[]{:S(2)}, u32[]{:S(2)}) collective-permute-start(bf16[16,1280]{1,0:T(8,128)(2,1)S(1)} %get-tuple-element.67), channel_id=1, source_target_pairs={{0,8},{4,12},{8,0},{12,4},{1,9},{5,13},{9,1},{13,5},{2,10},{6,14},... | collective-permute-start | bytes 122888 | tf_op jit(solution)/shard_map/ppermute | solution.py:74
  10.6 5.3 %collective-permute-start.5 = (bf16[16,1280]{1,0:T(8,128)(2,1)S(1)}, bf16[16,1280]{1,0:T(8,128)(2,1)S(1)}, u32[]{:S(2)}, u32[]{:S(2)}) collective-permute-start(bf16[16,1280]{1,0:T(8,128)(2,1)S(1)} %get-tuple-element.68), channel_id=1, source_target_pairs={{0,4},{4,0},{8,12},{12,8},{1,5},{5,1},{9,13},{13,9},{2,6},{6,2},{1... | collective-permute-start | bytes 122888 | tf_op jit(solution)/shard_map/ppermute | solution.py:74
  11.2 10.2 %collective-permute-start.10 = (bf16[256,256]{1,0:T(8,128)(2,1)S(1)}, bf16[256,256]{1,0:T(8,128)(2,1)S(1)}, u32[]{:S(2)}, u32[]{:S(2)}) collective-permute-start(bf16[256,256]{1,0:T(8,128)(2,1)S(1)} %get-tuple-element.81), channel_id=1, source_target_pairs={{0,12},{4,8},{8,4},{12,0},{16,24},{20,28},{24,16},{28,20},{1,13},{... | collective-permute-start | bytes 393224 | tf_op jit(solution)/shard_map/ppermute | solution.py:359
  16.5 7.4 %collective-permute-start.7 = (bf16[32,640]{1,0:T(8,128)(2,1)S(1)}, bf16[32,640]{1,0:T(8,128)(2,1)S(1)}, u32[]{:S(2)}, u32[]{:S(2)}) collective-permute-start(bf16[32,640]{1,0:T(8,128)(2,1)S(1)} %get-tuple-element.77), channel_id=1, source_target_pairs={{0,4},{4,0},{8,12},{12,8},{1,5},{5,1},{9,13},{13,9},{2,6},{6,2},{1... | collective-permute-start | bytes 122888 | tf_op jit(solution)/shard_map/ppermute | solution.py:74
  17.1 6.9 %collective-permute-start.8 = (bf16[32,640]{1,0:T(8,128)(2,1)S(1)}, bf16[32,640]{1,0:T(8,128)(2,1)S(1)}, u32[]{:S(2)}, u32[]{:S(2)}) collective-permute-start(bf16[32,640]{1,0:T(8,128)(2,1)S(1)} %get-tuple-element.78), channel_id=1, source_target_pairs={{0,12},{4,8},{8,4},{12,0},{1,13},{5,9},{9,5},{13,1},{2,14},{6,10},... | collective-permute-start | bytes 122888 | tf_op jit(solution)/shard_map/ppermute | solution.py:74
  20.1 5.0 %collective-permute-start.9 = (bf16[32,640]{1,0:T(8,128)(2,1)S(1)}, bf16[32,640]{1,0:T(8,128)(2,1)S(1)}, u32[]{:S(2)}, u32[]{:S(2)}) collective-permute-start(bf16[32,640]{1,0:T(8,128)(2,1)S(1)} %get-tuple-element.79), channel_id=1, source_target_pairs={{0,8},{4,12},{8,0},{12,4},{1,9},{5,13},{9,1},{13,5},{2,10},{6,14},... | collective-permute-start | bytes 122888 | tf_op jit(solution)/shard_map/ppermute | solution.py:74
  20.1 7.4 %collective-permute-start.13 = (bf16[256,256]{1,0:T(8,128)(2,1)S(1)}, bf16[256,256]{1,0:T(8,128)(2,1)S(1)}, u32[]{:S(2)}, u32[]{:S(2)}) collective-permute-start(bf16[256,256]{1,0:T(8,128)(2,1)S(1)} %get-tuple-element.83), channel_id=1, source_target_pairs={{0,4},{4,0},{8,12},{12,8},{1,5},{5,1},{9,13},{13,9},{2,6},{6,2},{1... | collective-permute-start | bytes 393224 | tf_op jit(solution)/shard_map/ppermute | solution.py:74
  21.5 8.8 %collective-permute-start.14 = (bf16[256,256]{1,0:T(8,128)(2,1)S(1)}, bf16[256,256]{1,0:T(8,128)(2,1)S(1)}, u32[]{:S(2)}, u32[]{:S(2)}) collective-permute-start(bf16[256,256]{1,0:T(8,128)(2,1)S(1)} %collective-permute-done.10), channel_id=1, source_target_pairs={{0,16},{16,0},{1,17},{17,1},{2,18},{18,2},{3,19},{19,3},{4,20},{20... | collective-permute-start | bytes 393224 | tf_op jit(solution)/shard_map/ppermute | solution.py:74
  25.3 4.2 %collective-permute-start.12 = (bf16[32,640]{1,0:T(8,128)(2,1)S(1)}, bf16[32,640]{1,0:T(8,128)(2,1)S(1)}, u32[]{:S(2)}, u32[]{:S(2)}) collective-permute-start(bf16[32,640]{1,0:T(8,128)(2,1)S(1)} %shard_map.85), channel_id=1, source_target_pairs={{0,2},{2,8},{4,0},{6,10},{8,4},{10,14},{12,6},{14,12},{1,3},{3,9},... | collective-permute-start | bytes 122888 | tf_op jit(solution)/shard_map/ppermute | solution.py:384
  26.9 2.6 %collective-permute-start.11 = (bf16[32,640]{1,0:T(8,128)(2,1)S(1)}, bf16[32,640]{1,0:T(8,128)(2,1)S(1)}, u32[]{:S(2)}, u32[]{:S(2)}) collective-permute-start(bf16[32,640]{1,0:T(8,128)(2,1)S(1)} %shard_map.85), channel_id=1, source_target_pairs={{0,0},{2,10},{4,2},{6,8},{8,6},{10,12},{12,4},{14,14},{1,1},{3,11}... | collective-permute-start | bytes 122888 | tf_op jit(solution)/shard_map/ppermute | solution.py:384
  27.6 15.2 %copy-start.2 = (f32[1024]{0:T(1024)S(1)}, f32[1024]{0:T(1024)}, u32[]{:S(2)}) copy-start(f32[1024]{0:T(1024)} %refs_6_.1) | copy-start | bytes 12292
  27.6 15.2 %copy-start.3 = (s32[1,4,1]{1,2,0:T(1,128)S(1)}, s32[1,4,1]{1,2,0:T(1,128)}, u32[]{:S(2)}) copy-start(s32[1,4,1]{1,2,0:T(1,128)} %param.15) | copy-start | bytes 52
  30.3 12.4 %collective-permute-start.18 = (bf16[1024,256]{1,0:T(8,128)(2,1)S(1)}, bf16[1024,256]{1,0:T(8,128)(2,1)S(1)}, u32[]{:S(2)}, u32[]{:S(2)}) collective-permute-start(bf16[1024,256]{1,0:T(8,128)(2,1)S(1)} %constant_dynamic-update-slice_fusion.refs_4_), channel_id=1, source_target_pairs={{0,1},{1,0},{2,3},{3,2},{4,5},{5,4},{6,7},{7,6},{8,9},{9,8},{10,11... | collective-permute-start | bytes 1572872 | tf_op jit(solution)/shard_map/ppermute | solution.py:74
  30.4 7.1 %collective-permute-start.15 = (bf16[64,512]{1,0:T(8,128)(2,1)S(1)}, bf16[64,512]{1,0:T(8,128)(2,1)S(1)}, u32[]{:S(2)}, u32[]{:S(2)}) collective-permute-start(bf16[64,512]{1,0:T(8,128)(2,1)S(1)} %get-tuple-element.91), channel_id=1, source_target_pairs={{0,8},{4,12},{8,0},{12,4},{1,9},{5,13},{9,1},{13,5},{2,10},{6,14},... | collective-permute-start | bytes 196616 | tf_op jit(solution)/shard_map/ppermute | solution.py:74
  34.5 4.4 %collective-permute-start.16 = (bf16[64,512]{1,0:T(8,128)(2,1)S(1)}, bf16[64,512]{1,0:T(8,128)(2,1)S(1)}, u32[]{:S(2)}, u32[]{:S(2)}) collective-permute-start(bf16[64,512]{1,0:T(8,128)(2,1)S(1)} %get-tuple-element.92), channel_id=1, source_target_pairs={{0,4},{4,0},{8,12},{12,8},{1,5},{5,1},{9,13},{13,9},{2,6},{6,2},{1... | collective-permute-start | bytes 196616 | tf_op jit(solution)/shard_map/ppermute | solution.py:74
  36.5 6.3 %collective-permute-start.17 = (bf16[64,512]{1,0:T(8,128)(2,1)S(1)}, bf16[64,512]{1,0:T(8,128)(2,1)S(1)}, u32[]{:S(2)}, u32[]{:S(2)}) collective-permute-start(bf16[64,512]{1,0:T(8,128)(2,1)S(1)} %get-tuple-element.93), channel_id=1, source_target_pairs={{0,12},{4,8},{8,4},{12,0},{1,13},{5,9},{9,5},{13,1},{2,14},{6,10},... | collective-permute-start | bytes 196616 | tf_op jit(solution)/shard_map/ppermute | solution.py:74
  43.1 6.1 %collective-permute-start.19 = (bf16[16,1152]{1,0:T(8,128)(2,1)S(1)}, bf16[16,1152]{1,0:T(8,128)(2,1)S(1)}, u32[]{:S(2)}, u32[]{:S(2)}) collective-permute-start(bf16[16,1152]{1,0:T(8,128)(2,1)S(1)} %get-tuple-element.100), channel_id=1, source_target_pairs={{0,12},{4,8},{8,4},{12,0},{1,13},{5,9},{9,5},{13,1},{2,14},{6,10},... | collective-permute-start | bytes 110600 | tf_op jit(solution)/shard_map/ppermute | solution.py:74
  44.9 5.1 %collective-permute-start.20 = (bf16[16,1152]{1,0:T(8,128)(2,1)S(1)}, bf16[16,1152]{1,0:T(8,128)(2,1)S(1)}, u32[]{:S(2)}, u32[]{:S(2)}) collective-permute-start(bf16[16,1152]{1,0:T(8,128)(2,1)S(1)} %get-tuple-element.101), channel_id=1, source_target_pairs={{0,8},{4,12},{8,0},{12,4},{1,9},{5,13},{9,1},{13,5},{2,10},{6,14},... | collective-permute-start | bytes 110600 | tf_op jit(solution)/shard_map/ppermute | solution.py:74
  44.9 5.1 %collective-permute-start.21 = (bf16[16,1152]{1,0:T(8,128)(2,1)S(1)}, bf16[16,1152]{1,0:T(8,128)(2,1)S(1)}, u32[]{:S(2)}, u32[]{:S(2)}) collective-permute-start(bf16[16,1152]{1,0:T(8,128)(2,1)S(1)} %get-tuple-element.102), channel_id=1, source_target_pairs={{0,4},{4,0},{8,12},{12,8},{1,5},{5,1},{9,13},{13,9},{2,6},{6,2},{1... | collective-permute-start | bytes 110600 | tf_op jit(solution)/shard_map/ppermute | solution.py:74
  50.2 3.8 %collective-permute-start.22 = (bf16[8,1152]{1,0:T(8,128)(2,1)S(1)}, bf16[8,1152]{1,0:T(8,128)(2,1)S(1)}, u32[]{:S(2)}, u32[]{:S(2)}) collective-permute-start(bf16[8,1152]{1,0:T(8,128)(2,1)S(1)} %get-tuple-element.105), channel_id=1, source_target_pairs={{0,2},{2,0},{1,3},{3,1},{4,6},{6,4},{5,7},{7,5},{8,10},{10,8},{9,1... | collective-permute-start | bytes 55304 | tf_op jit(solution)/shard_map/ppermute | solution.py:74

commit v6 on v5

--- a/solution.py
+++ b/solution.py
@@ -276,7 +276,7 @@
     keys = kept.shape[1] - 128
     total = sum(part[...].astype(jnp.float32) for part in parts)
     for k, part in zip((*places, 0), parts, strict=True):
-        live[pl.ds(h ^ k, 1), :] = part[:1, keys:].astype(jnp.float32)
+        live[pl.ds(h ^ k, 1), :] = part[:, keys:].astype(jnp.float32)[:1]
     squares = two_terms(total[:, keys : keys + 1] + total[:, -1:])
     rows = kept.shape[0]
     kept[:, :keys] = total[:rows, :keys]

time: 54.9 us -> 54.9 us (level)
  no operation moved by 1% of the time
where the time goes in v6:
time: 54.9 us; the launch traced here: 54.7 us
  starting transfers between devices  34.7 us (63%)
  waiting for transfers between devices  14.6 us (27%)
  Pallas kernels  5.17 us (9%)
    ppermute x20, starting transfers between devices, swap(): return lax.ppermute(x, axis, [(i, i ^ step) for i in range(n)])  28.8 us
    ppermute x20, waiting for transfers between devices, swap(): return lax.ppermute(x, axis, [(i, i ^ step) for i in range(n)])  12.7 us
    pallas_call x8, Pallas kernels, call(): pl.pallas_call(body, out_shape=outs, scratch_shapes=scratch, cost_estimat...  5.17 us
    ppermute x1, starting transfers between devices, rows_past_weights(): key_far = lax.ppermute(key_far, ('grp', 'hold'), perm)  3.74 us
    ppermute x2, starting transfers between devices, rows_past_weights(): halves.append(lax.ppermute(hidden, ('hold', 'tp'), perm))  2.19 us
    ppermute x2, waiting for transfers between devices, rows_past_weights(): halves.append(lax.ppermute(hidden, ('hold', 'tp'), perm))  1.91 us
  transfers between devices with their start and end apart: 23, of which 9 were waited for; matrix products, arithmetic and copies ran while one was open for 0% of the time, Pallas kernels for 7%

profile of v6, /device:TPU:0, one launch (start us, length us, event | category | flops | bytes accessed | tf_op | source)
XLA Modules:
  0.0 54.7 jit_solution(6020910972768446029)
XLA Ops:
  0.0 0.0 copy-start
  0.0 0.0 copy-start.1
  0.0 0.5 collective-permute-start.1
  0.5 0.1 collective-permute-start.2
  0.5 2.9 %collective-permute-start = (bf16[1,4,2,5120]{3,2,1,0:T(2,128)(2,1)}, bf16[1,4,2,5120]{3,2,1,0:T(2,128)(2,1)S(1)}, u32[]{:S(2)}, u32[]{:S(2)}) collective-permute-start(bf16[1,4,2,5120]{3,2,1,0:T(2,128)(2,1)} %cache.1), channel_id=1, source_target_pairs={{0,2},{2,0},{1,3},{3,1},{4,6},{6,4},{5,7},{7,5},{8,10},{10,8},{9,1... | collective-permute-start | bytes 245768 | tf_op jit(solution)/shard_map/ppermute | solution.py:74
  3.5 2.0 %shard_map.82 = (f32[8,5120]{1,0:T(8,128)S(1)}, bf16[1280,640]{1,0:T(8,128)(2,1)S(1)}, bf16[640,1024]{1,0:T(8,128)(2,1)S(1)}, bf16[256,256]{1,0:T(8,128)(2,1)S(1...) custom-call(bf16[1,4,2,5120]{3,2,1,0:T(2,128)(2,1)} %cache.1, f32[1280]{0:T(1024)} %ln_gain.3, ...), custom_call_target="tpu_custom_call" | custom-call | flops 8589934592 | bytes 3560512 | tf_op jit(solution)/shard_map/pallas_call | solution.py:84
  5.5 0.0 collective-permute-done.2.refs_7_
  5.5 0.9 %collective-permute-done.cache = bf16[1,4,2,5120]{3,2,1,0:T(2,128)(2,1)S(1)} collective-permute-done((bf16[1,4,2,5120]{3,2,1,0:T(2,128)(2,1)}, bf16[1,4,2,5120]{3,2,1,0:T(2,128)(2,1)S(1)}, u32[]{:S(2)}, u32[]{:S(2)}) %collective-permute-start) | collective-permute-done | bytes 81952 | tf_op jit(solution)/shard_map/ppermute | solution.py:74
  6.3 0.0 collective-permute-done.1.refs_5_
  6.3 0.0 collective-permute-start.6
  6.4 0.0 copy-done
  6.4 0.0 copy-done.1
  6.4 0.3 shard_map.83
  6.6 3.9 %collective-permute-start.3 = (bf16[16,1280]{1,0:T(8,128)(2,1)S(1)}, bf16[16,1280]{1,0:T(8,128)(2,1)S(1)}, u32[]{:S(2)}, u32[]{:S(2)}) collective-permute-start(bf16[16,1280]{1,0:T(8,128)(2,1)S(1)} %get-tuple-element.66), channel_id=1, source_target_pairs={{0,12},{4,8},{8,4},{12,0},{1,13},{5,9},{9,5},{13,1},{2,14},{6,10},... | collective-permute-start | bytes 122888 | tf_op jit(solution)/shard_map/ppermute | solution.py:74
  10.6 0.0 collective-permute-start.4
  10.6 0.6 %collective-permute-start.5 = (bf16[16,1280]{1,0:T(8,128)(2,1)S(1)}, bf16[16,1280]{1,0:T(8,128)(2,1)S(1)}, u32[]{:S(2)}, u32[]{:S(2)}) collective-permute-start(bf16[16,1280]{1,0:T(8,128)(2,1)S(1)} %get-tuple-element.68), channel_id=1, source_target_pairs={{0,4},{4,0},{8,12},{12,8},{1,5},{5,1},{9,13},{13,9},{2,6},{6,2},{1... | collective-permute-start | bytes 122888 | tf_op jit(solution)/shard_map/ppermute | solution.py:74
  11.2 3.7 %collective-permute-start.10 = (bf16[256,256]{1,0:T(8,128)(2,1)S(1)}, bf16[256,256]{1,0:T(8,128)(2,1)S(1)}, u32[]{:S(2)}, u32[]{:S(2)}) collective-permute-start(bf16[256,256]{1,0:T(8,128)(2,1)S(1)} %get-tuple-element.81), channel_id=1, source_target_pairs={{0,12},{4,8},{8,4},{12,0},{16,24},{20,28},{24,16},{28,20},{1,13},{... | collective-permute-start | bytes 393224 | tf_op jit(solution)/shard_map/ppermute | solution.py:359
  15.0 0.0 collective-permute-done.3.refs_0_
  15.0 0.9 %collective-permute-done.4.refs_1_ = bf16[16,1280]{1,0:T(8,128)(2,1)S(1)} collective-permute-done((bf16[16,1280]{1,0:T(8,128)(2,1)S(1)}, bf16[16,1280]{1,0:T(8,128)(2,1)S(1)}, u32[]{:S(2)}, u32[]{:S(2)}) %collective-permute-start.4) | collective-permute-done | bytes 40992 | tf_op jit(solution)/shard_map/ppermute | solution.py:74
  15.9 0.0 collective-permute-done.5.refs_2_
  15.9 0.7 %shard_map.84 = (bf16[32,640]{1,0:T(8,128)(2,1)S(1)}, bf16[32,640]{1,0:T(8,128)(2,1)S(1)}, bf16[32,640]{1,0:T(8,128)(2,1)S(1)}, bf16[32,640]{1,0:T(8,128)(2,1)S(1)}) custom-call(bf16[16,1280]{1,0:T(8,128)(2,1)S(1)} %collective-permute-done.3.refs_0_, bf16[16,1280]{1,0:T(8,128)(2,1)S(1)} %collective-permute-done.4.refs_1_, ...), custom_call_target="tpu_custom_call" | custom-call | flops 8589934592 | bytes 3440640 | tf_op jit(solution)/shard_map/pallas_call | solution.py:84
  16.5 0.0 collective-permute-done.6.w_other
  16.5 0.5 collective-permute-start.7
  17.1 3.1 %collective-permute-start.8 = (bf16[32,640]{1,0:T(8,128)(2,1)S(1)}, bf16[32,640]{1,0:T(8,128)(2,1)S(1)}, u32[]{:S(2)}, u32[]{:S(2)}) collective-permute-start(bf16[32,640]{1,0:T(8,128)(2,1)S(1)} %get-tuple-element.78), channel_id=1, source_target_pairs={{0,12},{4,8},{8,4},{12,0},{1,13},{5,9},{9,5},{13,1},{2,14},{6,10},... | collective-permute-start | bytes 122888 | tf_op jit(solution)/shard_map/ppermute | solution.py:74
  20.1 0.0 collective-permute-start.9
  20.1 1.3 %collective-permute-start.13 = (bf16[256,256]{1,0:T(8,128)(2,1)S(1)}, bf16[256,256]{1,0:T(8,128)(2,1)S(1)}, u32[]{:S(2)}, u32[]{:S(2)}) collective-permute-start(bf16[256,256]{1,0:T(8,128)(2,1)S(1)} %get-tuple-element.83), channel_id=1, source_target_pairs={{0,4},{4,0},{8,12},{12,8},{1,5},{5,1},{9,13},{13,9},{2,6},{6,2},{1... | collective-permute-start | bytes 393224 | tf_op jit(solution)/shard_map/ppermute | solution.py:74
  21.5 0.0 collective-permute-done.10
  21.5 2.5 %collective-permute-start.14 = (bf16[256,256]{1,0:T(8,128)(2,1)S(1)}, bf16[256,256]{1,0:T(8,128)(2,1)S(1)}, u32[]{:S(2)}, u32[]{:S(2)}) collective-permute-start(bf16[256,256]{1,0:T(8,128)(2,1)S(1)} %collective-permute-done.10), channel_id=1, source_target_pairs={{0,16},{16,0},{1,17},{17,1},{2,18},{18,2},{3,19},{19,3},{4,20},{20... | collective-permute-start | bytes 393224 | tf_op jit(solution)/shard_map/ppermute | solution.py:74
  23.9 0.0 collective-permute-done.7.refs_0_
  24.0 0.0 collective-permute-done.8.refs_1_
  24.0 1.2 %collective-permute-done.9.refs_2_ = bf16[32,640]{1,0:T(8,128)(2,1)S(1)} collective-permute-done((bf16[32,640]{1,0:T(8,128)(2,1)S(1)}, bf16[32,640]{1,0:T(8,128)(2,1)S(1)}, u32[]{:S(2)}, u32[]{:S(2)}) %collective-permute-start.9) | collective-permute-done | bytes 40992 | tf_op jit(solution)/shard_map/ppermute | solution.py:74
  25.1 0.2 shard_map.85
  25.3 1.5 %collective-permute-start.12 = (bf16[32,640]{1,0:T(8,128)(2,1)S(1)}, bf16[32,640]{1,0:T(8,128)(2,1)S(1)}, u32[]{:S(2)}, u32[]{:S(2)}) collective-permute-start(bf16[32,640]{1,0:T(8,128)(2,1)S(1)} %shard_map.85), channel_id=1, source_target_pairs={{0,2},{2,8},{4,0},{6,10},{8,4},{10,14},{12,6},{14,12},{1,3},{3,9},... | collective-permute-start | bytes 122888 | tf_op jit(solution)/shard_map/ppermute | solution.py:384
  26.9 0.7 %collective-permute-start.11 = (bf16[32,640]{1,0:T(8,128)(2,1)S(1)}, bf16[32,640]{1,0:T(8,128)(2,1)S(1)}, u32[]{:S(2)}, u32[]{:S(2)}) collective-permute-start(bf16[32,640]{1,0:T(8,128)(2,1)S(1)} %shard_map.85), channel_id=1, source_target_pairs={{0,0},{2,10},{4,2},{6,8},{8,6},{10,12},{12,4},{14,14},{1,1},{3,11}... | collective-permute-start | bytes 122888 | tf_op jit(solution)/shard_map/ppermute | solution.py:384
  27.6 0.0 copy-start.2
  27.6 0.0 copy-start.3
  27.6 0.0 collective-permute-done.13
  27.6 1.9 %collective-permute-done.12.second = bf16[32,640]{1,0:T(8,128)(2,1)S(1)} collective-permute-done((bf16[32,640]{1,0:T(8,128)(2,1)S(1)}, bf16[32,640]{1,0:T(8,128)(2,1)S(1)}, u32[]{:S(2)}, u32[]{:S(2)}) %collective-permute-start.12) | collective-permute-done | bytes 40992 | tf_op jit(solution)/shard_map/ppermute | solution.py:384
  29.5 0.0 collective-permute-done.11.first
  29.5 0.8 %shard_map.86 = (bf16[64,512]{1,0:T(8,128)(2,1)S(1)}, bf16[64,512]{1,0:T(8,128)(2,1)S(1)}, bf16[64,512]{1,0:T(8,128)(2,1)S(1)}, bf16[64,512]{1,0:T(8,128)(2,1)S(1)}) custom-call(bf16[32,640]{1,0:T(8,128)(2,1)S(1)} %collective-permute-done.11.first, bf16[32,640]{1,0:T(8,128)(2,1)S(1)} %collective-permute-done.12.second, ...), custom_call_target="tpu_custom_call" | custom-call | flops 167772160 | bytes 2703360 | tf_op jit(solution)/shard_map/pallas_call | solution.py:84
  30.3 0.0 collective-permute-done.14
  30.3 0.1 collective-permute-start.18
  30.4 4.1 %collective-permute-start.15 = (bf16[64,512]{1,0:T(8,128)(2,1)S(1)}, bf16[64,512]{1,0:T(8,128)(2,1)S(1)}, u32[]{:S(2)}, u32[]{:S(2)}) collective-permute-start(bf16[64,512]{1,0:T(8,128)(2,1)S(1)} %get-tuple-element.91), channel_id=1, source_target_pairs={{0,8},{4,12},{8,0},{12,4},{1,9},{5,13},{9,1},{13,5},{2,10},{6,14},... | collective-permute-start | bytes 196616 | tf_op jit(solution)/shard_map/ppermute | solution.py:74
  34.5 2.0 %collective-permute-start.16 = (bf16[64,512]{1,0:T(8,128)(2,1)S(1)}, bf16[64,512]{1,0:T(8,128)(2,1)S(1)}, u32[]{:S(2)}, u32[]{:S(2)}) collective-permute-start(bf16[64,512]{1,0:T(8,128)(2,1)S(1)} %get-tuple-element.92), channel_id=1, source_target_pairs={{0,4},{4,0},{8,12},{12,8},{1,5},{5,1},{9,13},{13,9},{2,6},{6,2},{1... | collective-permute-start | bytes 196616 | tf_op jit(solution)/shard_map/ppermute | solution.py:74
  36.5 1.0 %collective-permute-start.17 = (bf16[64,512]{1,0:T(8,128)(2,1)S(1)}, bf16[64,512]{1,0:T(8,128)(2,1)S(1)}, u32[]{:S(2)}, u32[]{:S(2)}) collective-permute-start(bf16[64,512]{1,0:T(8,128)(2,1)S(1)} %get-tuple-element.93), channel_id=1, source_target_pairs={{0,12},{4,8},{8,4},{12,0},{1,13},{5,9},{9,5},{13,1},{2,14},{6,10},... | collective-permute-start | bytes 196616 | tf_op jit(solution)/shard_map/ppermute | solution.py:74
  37.5 0.0 collective-permute-done.15.refs_0_
  37.5 1.4 %collective-permute-done.16.refs_1_ = bf16[64,512]{1,0:T(8,128)(2,1)S(1)} collective-permute-done((bf16[64,512]{1,0:T(8,128)(2,1)S(1)}, bf16[64,512]{1,0:T(8,128)(2,1)S(1)}, u32[]{:S(2)}, u32[]{:S(2)}) %collective-permute-start.16) | collective-permute-done | bytes 65568 | tf_op jit(solution)/shard_map/ppermute | solution.py:74
  38.9 3.9 %collective-permute-done.17.refs_2_ = bf16[64,512]{1,0:T(8,128)(2,1)S(1)} collective-permute-done((bf16[64,512]{1,0:T(8,128)(2,1)S(1)}, bf16[64,512]{1,0:T(8,128)(2,1)S(1)}, u32[]{:S(2)}, u32[]{:S(2)}) %collective-permute-start.17) | collective-permute-done | bytes 65568 | tf_op jit(solution)/shard_map/ppermute | solution.py:74
  42.8 0.0 collective-permute-done.18.refs_5_
  42.8 0.0 copy-done.2
  42.8 0.0 copy-done.3
  42.8 0.3 shard_map.87
  43.1 1.8 %collective-permute-start.19 = (bf16[16,1152]{1,0:T(8,128)(2,1)S(1)}, bf16[16,1152]{1,0:T(8,128)(2,1)S(1)}, u32[]{:S(2)}, u32[]{:S(2)}) collective-permute-start(bf16[16,1152]{1,0:T(8,128)(2,1)S(1)} %get-tuple-element.100), channel_id=1, source_target_pairs={{0,12},{4,8},{8,4},{12,0},{1,13},{5,9},{9,5},{13,1},{2,14},{6,10},... | collective-permute-start | bytes 110600 | tf_op jit(solution)/shard_map/ppermute | solution.py:74
  44.9 0.0 collective-permute-start.20
  44.9 2.7 %collective-permute-start.21 = (bf16[16,1152]{1,0:T(8,128)(2,1)S(1)}, bf16[16,1152]{1,0:T(8,128)(2,1)S(1)}, u32[]{:S(2)}, u32[]{:S(2)}) collective-permute-start(bf16[16,1152]{1,0:T(8,128)(2,1)S(1)} %get-tuple-element.102), channel_id=1, source_target_pairs={{0,4},{4,0},{8,12},{12,8},{1,5},{5,1},{9,13},{13,9},{2,6},{6,2},{1... | collective-permute-start | bytes 110600 | tf_op jit(solution)/shard_map/ppermute | solution.py:74
  47.6 1.7 %collective-permute-done.19.refs_0_ = bf16[16,1152]{1,0:T(8,128)(2,1)S(1)} collective-permute-done((bf16[16,1152]{1,0:T(8,128)(2,1)S(1)}, bf16[16,1152]{1,0:T(8,128)(2,1)S(1)}, u32[]{:S(2)}, u32[]{:S(2)}) %collective-permute-start.19) | collective-permute-done | bytes 36896 | tf_op jit(solution)/shard_map/ppermute | solution.py:74
  49.2 0.8 %collective-permute-done.20.refs_1_ = bf16[16,1152]{1,0:T(8,128)(2,1)S(1)} collective-permute-done((bf16[16,1152]{1,0:T(8,128)(2,1)S(1)}, bf16[16,1152]{1,0:T(8,128)(2,1)S(1)}, u32[]{:S(2)}, u32[]{:S(2)}) %collective-permute-start.20) | collective-permute-done | bytes 36896 | tf_op jit(solution)/shard_map/ppermute | solution.py:74
  50.0 0.0 collective-permute-done.21.refs_2_
  50.0 0.2 shard_map.88
  50.2 1.7 %collective-permute-start.22 = (bf16[8,1152]{1,0:T(8,128)(2,1)S(1)}, bf16[8,1152]{1,0:T(8,128)(2,1)S(1)}, u32[]{:S(2)}, u32[]{:S(2)}) collective-permute-start(bf16[8,1152]{1,0:T(8,128)(2,1)S(1)} %get-tuple-element.105), channel_id=1, source_target_pairs={{0,2},{2,0},{1,3},{3,1},{4,6},{6,4},{5,7},{7,5},{8,10},{10,8},{9,1... | collective-permute-start | bytes 55304 | tf_op jit(solution)/shard_map/ppermute | solution.py:74
  51.9 2.1 %collective-permute-done.22.came = bf16[8,1152]{1,0:T(8,128)(2,1)S(1)} collective-permute-done((bf16[8,1152]{1,0:T(8,128)(2,1)S(1)}, bf16[8,1152]{1,0:T(8,128)(2,1)S(1)}, u32[]{:S(2)}, u32[]{:S(2)}) %collective-permute-start.22) | collective-permute-done | bytes 18464 | tf_op jit(solution)/shard_map/ppermute | solution.py:74
  53.9 0.8 %shard_map.89 = bf16[1,4,2,1024]{3,2,1,0:T(2,128)(2,1)} custom-call(f32[8,1152]{1,0:T(8,128)S(1)} %get-tuple-element.104.kept, bf16[8,1152]{1,0:T(8,128)(2,1)S(1)} %collective-permute-done.22.came, s32[4,4]{1,0:T(4,128)S(1)} %copy-done, f32[4,128]{1,0:T(4,128)S(1)} %get-tuple-element.106.live), custom_call_target="tpu_custom_call" | custom-call | bytes 57408 | tf_op jit(solution)/shard_map/pallas_call | solution.py:84
  (4 shorter events, 0.0 us)
Async XLA Ops:
  0.0 6.4 %copy-start = (s32[4,4]{1,0:T(4,128)S(1)}, s32[4,4]{1,0:T(4,128)}, u32[]{:S(2)}) copy-start(s32[4,4]{1,0:T(4,128)} %matching.5) | copy-start | bytes 196
  0.0 6.4 %copy-start.1 = (f32[1280]{0:T(1024)S(1)}, f32[1280]{0:T(1024)}, u32[]{:S(2)}) copy-start(f32[1280]{0:T(1024)} %ln_gain.3) | copy-start | bytes 15364
  0.0 6.3 %collective-permute-start.1 = (bf16[1280,640]{1,0:T(8,128)(2,1)}, bf16[1280,640]{1,0:T(8,128)(2,1)S(1)}, u32[]{:S(2)}, u32[]{:S(2)}) collective-permute-start(bf16[1280,640]{1,0:T(8,128)(2,1)} %w_fc1.1), channel_id=1, source_target_pairs={{0,1},{1,0},{2,3},{3,2},{4,5},{5,4},{6,7},{7,6},{8,9},{9,8},{10,11... | collective-permute-start | bytes 4915208 | tf_op jit(solution)/shard_map/ppermute | solution.py:74
  0.5 5.0 %collective-permute-start.2 = (f32[1024]{0:T(1024)}, f32[1024]{0:T(1024)S(1)}, u32[]{:S(2)}, u32[]{:S(2)}) collective-permute-start(f32[1024]{0:T(1024)} %refs_6_.1), channel_id=1, source_target_pairs={{0,1},{1,0},{2,3},{3,2},{4,5},{5,4},{6,7},{7,6},{8,9},{9,8},{10,11... | collective-permute-start | bytes 12296 | tf_op jit(solution)/shard_map/ppermute | solution.py:74
  0.5 5.8 %collective-permute-start = (bf16[1,4,2,5120]{3,2,1,0:T(2,128)(2,1)}, bf16[1,4,2,5120]{3,2,1,0:T(2,128)(2,1)S(1)}, u32[]{:S(2)}, u32[]{:S(2)}) collective-permute-start(bf16[1,4,2,5120]{3,2,1,0:T(2,128)(2,1)} %cache.1), channel_id=1, source_target_pairs={{0,2},{2,0},{1,3},{3,1},{4,6},{6,4},{5,7},{7,5},{8,10},{10,8},{9,1... | collective-permute-start | bytes 245768 | tf_op jit(solution)/shard_map/ppermute | solution.py:74
  6.3 10.2 %collective-permute-start.6 = (bf16[640,1024]{1,0:T(8,128)(2,1)S(1)}, bf16[640,1024]{1,0:T(8,128)(2,1)S(1)}, u32[]{:S(2)}, u32[]{:S(2)}) collective-permute-start(bf16[640,1024]{1,0:T(8,128)(2,1)S(1)} %get-tuple-element.76.w_mine), channel_id=1, source_target_pairs={{0,1},{1,0},{2,3},{3,2},{4,5},{5,4},{6,7},{7,6},{8,9},{9,8},{10,11... | collective-permute-start | bytes 3932168 | tf_op jit(solution)/shard_map/ppermute | solution.py:74
  6.6 8.3 %collective-permute-start.3 = (bf16[16,1280]{1,0:T(8,128)(2,1)S(1)}, bf16[16,1280]{1,0:T(8,128)(2,1)S(1)}, u32[]{:S(2)}, u32[]{:S(2)}) collective-permute-start(bf16[16,1280]{1,0:T(8,128)(2,1)S(1)} %get-tuple-element.66), channel_id=1, source_target_pairs={{0,12},{4,8},{8,4},{12,0},{1,13},{5,9},{9,5},{13,1},{2,14},{6,10},... | collective-permute-start | bytes 122888 | tf_op jit(solution)/shard_map/ppermute | solution.py:74
  10.6 5.3 %collective-permute-start.4 = (bf16[16,1280]{1,0:T(8,128)(2,1)S(1)}, bf16[16,1280]{1,0:T(8,128)(2,1)S(1)}, u32[]{:S(2)}, u32[]{:S(2)}) collective-permute-start(bf16[16,1280]{1,0:T(8,128)(2,1)S(1)} %get-tuple-element.67), channel_id=1, source_target_pairs={{0,8},{4,12},{8,0},{12,4},{1,9},{5,13},{9,1},{13,5},{2,10},{6,14},... | collective-permute-start | bytes 122888 | tf_op jit(solution)/shard_map/ppermute | solution.py:74
  10.6 5.3 %collective-permute-start.5 = (bf16[16,1280]{1,0:T(8,128)(2,1)S(1)}, bf16[16,1280]{1,0:T(8,128)(2,1)S(1)}, u32[]{:S(2)}, u32[]{:S(2)}) collective-permute-start(bf16[16,1280]{1,0:T(8,128)(2,1)S(1)} %get-tuple-element.68), channel_id=1, source_target_pairs={{0,4},{4,0},{8,12},{12,8},{1,5},{5,1},{9,13},{13,9},{2,6},{6,2},{1... | collective-permute-start | bytes 122888 | tf_op jit(solution)/shard_map/ppermute | solution.py:74
  11.2 10.2 %collective-permute-start.10 = (bf16[256,256]{1,0:T(8,128)(2,1)S(1)}, bf16[256,256]{1,0:T(8,128)(2,1)S(1)}, u32[]{:S(2)}, u32[]{:S(2)}) collective-permute-start(bf16[256,256]{1,0:T(8,128)(2,1)S(1)} %get-tuple-element.81), channel_id=1, source_target_pairs={{0,12},{4,8},{8,4},{12,0},{16,24},{20,28},{24,16},{28,20},{1,13},{... | collective-permute-start | bytes 393224 | tf_op jit(solution)/shard_map/ppermute | solution.py:359
  16.5 7.4 %collective-permute-start.7 = (bf16[32,640]{1,0:T(8,128)(2,1)S(1)}, bf16[32,640]{1,0:T(8,128)(2,1)S(1)}, u32[]{:S(2)}, u32[]{:S(2)}) collective-permute-start(bf16[32,640]{1,0:T(8,128)(2,1)S(1)} %get-tuple-element.77), channel_id=1, source_target_pairs={{0,4},{4,0},{8,12},{12,8},{1,5},{5,1},{9,13},{13,9},{2,6},{6,2},{1... | collective-permute-start | bytes 122888 | tf_op jit(solution)/shard_map/ppermute | solution.py:74
  17.1 6.9 %collective-permute-start.8 = (bf16[32,640]{1,0:T(8,128)(2,1)S(1)}, bf16[32,640]{1,0:T(8,128)(2,1)S(1)}, u32[]{:S(2)}, u32[]{:S(2)}) collective-permute-start(bf16[32,640]{1,0:T(8,128)(2,1)S(1)} %get-tuple-element.78), channel_id=1, source_target_pairs={{0,12},{4,8},{8,4},{12,0},{1,13},{5,9},{9,5},{13,1},{2,14},{6,10},... | collective-permute-start | bytes 122888 | tf_op jit(solution)/shard_map/ppermute | solution.py:74
  20.1 5.0 %collective-permute-start.9 = (bf16[32,640]{1,0:T(8,128)(2,1)S(1)}, bf16[32,640]{1,0:T(8,128)(2,1)S(1)}, u32[]{:S(2)}, u32[]{:S(2)}) collective-permute-start(bf16[32,640]{1,0:T(8,128)(2,1)S(1)} %get-tuple-element.79), channel_id=1, source_target_pairs={{0,8},{4,12},{8,0},{12,4},{1,9},{5,13},{9,1},{13,5},{2,10},{6,14},... | collective-permute-start | bytes 122888 | tf_op jit(solution)/shard_map/ppermute | solution.py:74
  20.1 7.4 %collective-permute-start.13 = (bf16[256,256]{1,0:T(8,128)(2,1)S(1)}, bf16[256,256]{1,0:T(8,128)(2,1)S(1)}, u32[]{:S(2)}, u32[]{:S(2)}) collective-permute-start(bf16[256,256]{1,0:T(8,128)(2,1)S(1)} %get-tuple-element.83), channel_id=1, source_target_pairs={{0,4},{4,0},{8,12},{12,8},{1,5},{5,1},{9,13},{13,9},{2,6},{6,2},{1... | collective-permute-start | bytes 393224 | tf_op jit(solution)/shard_map/ppermute | solution.py:74
  21.5 8.8 %collective-permute-start.14 = (bf16[256,256]{1,0:T(8,128)(2,1)S(1)}, bf16[256,256]{1,0:T(8,128)(2,1)S(1)}, u32[]{:S(2)}, u32[]{:S(2)}) collective-permute-start(bf16[256,256]{1,0:T(8,128)(2,1)S(1)} %collective-permute-done.10), channel_id=1, source_target_pairs={{0,16},{16,0},{1,17},{17,1},{2,18},{18,2},{3,19},{19,3},{4,20},{20... | collective-permute-start | bytes 393224 | tf_op jit(solution)/shard_map/ppermute | solution.py:74
  25.3 4.2 %collective-permute-start.12 = (bf16[32,640]{1,0:T(8,128)(2,1)S(1)}, bf16[32,640]{1,0:T(8,128)(2,1)S(1)}, u32[]{:S(2)}, u32[]{:S(2)}) collective-permute-start(bf16[32,640]{1,0:T(8,128)(2,1)S(1)} %shard_map.85), channel_id=1, source_target_pairs={{0,2},{2,8},{4,0},{6,10},{8,4},{10,14},{12,6},{14,12},{1,3},{3,9},... | collective-permute-start | bytes 122888 | tf_op jit(solution)/shard_map/ppermute | solution.py:384
  26.9 2.6 %collective-permute-start.11 = (bf16[32,640]{1,0:T(8,128)(2,1)S(1)}, bf16[32,640]{1,0:T(8,128)(2,1)S(1)}, u32[]{:S(2)}, u32[]{:S(2)}) collective-permute-start(bf16[32,640]{1,0:T(8,128)(2,1)S(1)} %shard_map.85), channel_id=1, source_target_pairs={{0,0},{2,10},{4,2},{6,8},{8,6},{10,12},{12,4},{14,14},{1,1},{3,11}... | collective-permute-start | bytes 122888 | tf_op jit(solution)/shard_map/ppermute | solution.py:384
  27.6 15.2 %copy-start.2 = (f32[1024]{0:T(1024)S(1)}, f32[1024]{0:T(1024)}, u32[]{:S(2)}) copy-start(f32[1024]{0:T(1024)} %refs_6_.1) | copy-start | bytes 12292
  27.6 15.2 %copy-start.3 = (s32[1,4,1]{1,2,0:T(1,128)S(1)}, s32[1,4,1]{1,2,0:T(1,128)}, u32[]{:S(2)}) copy-start(s32[1,4,1]{1,2,0:T(1,128)} %param.15) | copy-start | bytes 52
  30.3 12.4 %collective-permute-start.18 = (bf16[1024,256]{1,0:T(8,128)(2,1)S(1)}, bf16[1024,256]{1,0:T(8,128)(2,1)S(1)}, u32[]{:S(2)}, u32[]{:S(2)}) collective-permute-start(bf16[1024,256]{1,0:T(8,128)(2,1)S(1)} %constant_dynamic-update-slice_fusion.refs_4_), channel_id=1, source_target_pairs={{0,1},{1,0},{2,3},{3,2},{4,5},{5,4},{6,7},{7,6},{8,9},{9,8},{10,11... | collective-permute-start | bytes 1572872 | tf_op jit(solution)/shard_map/ppermute | solution.py:74
  30.4 7.1 %collective-permute-start.15 = (bf16[64,512]{1,0:T(8,128)(2,1)S(1)}, bf16[64,512]{1,0:T(8,128)(2,1)S(1)}, u32[]{:S(2)}, u32[]{:S(2)}) collective-permute-start(bf16[64,512]{1,0:T(8,128)(2,1)S(1)} %get-tuple-element.91), channel_id=1, source_target_pairs={{0,8},{4,12},{8,0},{12,4},{1,9},{5,13},{9,1},{13,5},{2,10},{6,14},... | collective-permute-start | bytes 196616 | tf_op jit(solution)/shard_map/ppermute | solution.py:74
  34.5 4.4 %collective-permute-start.16 = (bf16[64,512]{1,0:T(8,128)(2,1)S(1)}, bf16[64,512]{1,0:T(8,128)(2,1)S(1)}, u32[]{:S(2)}, u32[]{:S(2)}) collective-permute-start(bf16[64,512]{1,0:T(8,128)(2,1)S(1)} %get-tuple-element.92), channel_id=1, source_target_pairs={{0,4},{4,0},{8,12},{12,8},{1,5},{5,1},{9,13},{13,9},{2,6},{6,2},{1... | collective-permute-start | bytes 196616 | tf_op jit(solution)/shard_map/ppermute | solution.py:74
  36.5 6.3 %collective-permute-start.17 = (bf16[64,512]{1,0:T(8,128)(2,1)S(1)}, bf16[64,512]{1,0:T(8,128)(2,1)S(1)}, u32[]{:S(2)}, u32[]{:S(2)}) collective-permute-start(bf16[64,512]{1,0:T(8,128)(2,1)S(1)} %get-tuple-element.93), channel_id=1, source_target_pairs={{0,12},{4,8},{8,4},{12,0},{1,13},{5,9},{9,5},{13,1},{2,14},{6,10},... | collective-permute-start | bytes 196616 | tf_op jit(solution)/shard_map/ppermute | solution.py:74
  43.1 6.1 %collective-permute-start.19 = (bf16[16,1152]{1,0:T(8,128)(2,1)S(1)}, bf16[16,1152]{1,0:T(8,128)(2,1)S(1)}, u32[]{:S(2)}, u32[]{:S(2)}) collective-permute-start(bf16[16,1152]{1,0:T(8,128)(2,1)S(1)} %get-tuple-element.100), channel_id=1, source_target_pairs={{0,12},{4,8},{8,4},{12,0},{1,13},{5,9},{9,5},{13,1},{2,14},{6,10},... | collective-permute-start | bytes 110600 | tf_op jit(solution)/shard_map/ppermute | solution.py:74
  44.9 5.1 %collective-permute-start.20 = (bf16[16,1152]{1,0:T(8,128)(2,1)S(1)}, bf16[16,1152]{1,0:T(8,128)(2,1)S(1)}, u32[]{:S(2)}, u32[]{:S(2)}) collective-permute-start(bf16[16,1152]{1,0:T(8,128)(2,1)S(1)} %get-tuple-element.101), channel_id=1, source_target_pairs={{0,8},{4,12},{8,0},{12,4},{1,9},{5,13},{9,1},{13,5},{2,10},{6,14},... | collective-permute-start | bytes 110600 | tf_op jit(solution)/shard_map/ppermute | solution.py:74
  44.9 5.1 %collective-permute-start.21 = (bf16[16,1152]{1,0:T(8,128)(2,1)S(1)}, bf16[16,1152]{1,0:T(8,128)(2,1)S(1)}, u32[]{:S(2)}, u32[]{:S(2)}) collective-permute-start(bf16[16,1152]{1,0:T(8,128)(2,1)S(1)} %get-tuple-element.102), channel_id=1, source_target_pairs={{0,4},{4,0},{8,12},{12,8},{1,5},{5,1},{9,13},{13,9},{2,6},{6,2},{1... | collective-permute-start | bytes 110600 | tf_op jit(solution)/shard_map/ppermute | solution.py:74
  50.2 3.8 %collective-permute-start.22 = (bf16[8,1152]{1,0:T(8,128)(2,1)S(1)}, bf16[8,1152]{1,0:T(8,128)(2,1)S(1)}, u32[]{:S(2)}, u32[]{:S(2)}) collective-permute-start(bf16[8,1152]{1,0:T(8,128)(2,1)S(1)} %get-tuple-element.105), channel_id=1, source_target_pairs={{0,2},{2,0},{1,3},{3,1},{4,6},{6,4},{5,7},{7,5},{8,10},{10,8},{9,1... | collective-permute-start | bytes 55304 | tf_op jit(solution)/shard_map/ppermute | solution.py:74

commit v7 on v6

--- a/solution.py
+++ b/solution.py
@@ -200,31 +200,29 @@
 
 def gelu_kernel(*refs):
     x = sum(part[...].astype(jnp.float32) for part in refs[:4])
-    refs[4][...] = (0.5 * x * erfc(-x * 0.5**0.5)).astype(jnp.bfloat16)
+    hidden = (0.5 * x * erfc(-x * 0.5**0.5)).astype(jnp.bfloat16)
+    total = x.shape[0]
+    bb = total // 16
+    to = lax.broadcasted_iota(jnp.int32, (total, total), 0)
+    source = lax.broadcasted_iota(jnp.int32, (total, total), 1)
+    owner, holder = to // (4 * bb), (to % (4 * bb)) // bb
+    order = jnp.where(source == (holder * 4 + owner) * bb + to % bb, 1.0, 0.0)
+    refs[4][...] = dot(order.astype(jnp.bfloat16), hidden).astype(jnp.bfloat16)
 
 
 def second_kernel(first, second, w_mine, w_other, *refs):
-    outs, sums = refs[:4], refs[4]
+    outs, rows = refs[:4], refs[4]
     h = lax.axis_index("hold")
     half = first.shape[0]
-    bb = half // 16
-    to = lax.broadcasted_iota(jnp.int32, (2 * half, half), 0)
-    source = lax.broadcasted_iota(jnp.int32, (2 * half, half), 1)
-    u, owner = to // half, (to % half) // (4 * bb)
-    holder, b_of = (to % (4 * bb)) // bb, to % bb
-    wanted = (u ^ (h & 1)) * half + (holder * 4 + owner) * bb + b_of
-    moved = 0.0
-    for p, part in enumerate((first, second)):
-        order = jnp.where(source + p * half == wanted, 1.0, 0.0)
-        moved += dot(order.astype(jnp.bfloat16), part[...])
-    moved = moved.astype(jnp.bfloat16)
+    for g, part in enumerate((first, second)):
+        rows[pl.ds(pl.multiple_of((g ^ (h & 1)) * half, 16), half), :] = part[...]
+    x = rows[...]
     cols = outs[0].shape[1] // 2
     for p, weight in enumerate((w_mine, w_other)):
-        sums[p] = dot(moved, weight[...])
-        for k in range(4):
+        for k, out in enumerate(outs):
             start = pl.multiple_of((h ^ k) * cols, 128)
-            part = sums[p, :, pl.ds(start, cols)].astype(jnp.bfloat16)
-            outs[k][:, p * cols : (p + 1) * cols] = part
+            part = dot(x, weight[:, pl.ds(start, cols)]).astype(jnp.bfloat16)
+            out[:, p * cols : (p + 1) * cols] = part
 
 
 def two_terms(x):
@@ -308,7 +306,7 @@
     rounds, block, depth = cache.shape[1:]
     rows = rounds * block
     chunk = depth // n
-    hidden_cols, out_cols, key_cols = w_fc1.shape[1], w_fc2.shape[1], w_key.shape[1]
+    hidden_cols, key_cols = w_fc1.shape[1], w_key.shape[1]
     share = w_key.shape[0] // n
     f32, bf16 = jnp.float32, jnp.bfloat16
     vmem = pltpu.VMEM
@@ -389,7 +387,7 @@
         *halves,
         w_fc2_mine,
         w_fc2_other,
-        scratch=[vmem((2, 8 * rows, out_cols), f32)],
+        scratch=[vmem((8 * rows, hidden_cols), bf16)],
         flops=32 * rows * w_fc2.size,
     )
     *merged, key_near = lax.optimization_barrier((*merged, key_near))
@@ -409,7 +407,7 @@
         scratch=[vmem((8 * rows, wide), f32)],
         flops=32 * rows * w_key.size,
     )
-    order = (3, 2, 1)
+    order = (3, 1, 2)
     kept, sent, live = call(
         functools.partial(group_kernel, order),
         [like((rows, wide), f32), like((rows, wide)), like((n, 128), f32)],

time: 54.9 us -> 54.7 us (level)
  no operation moved by 1% of the time
where the time goes in v7:
time: 54.7 us; the launch traced here: 54.6 us
  starting transfers between devices  34.4 us (63%)
  waiting for transfers between devices  14.8 us (27%)
  Pallas kernels  5.14 us (9%)
    ppermute x20, starting transfers between devices, swap(): return lax.ppermute(x, axis, [(i, i ^ step) for i in range(n)])  28.5 us
    ppermute x20, waiting for transfers between devices, swap(): return lax.ppermute(x, axis, [(i, i ^ step) for i in range(n)])  12.9 us
    pallas_call x8, Pallas kernels, call(): pl.pallas_call(body, out_shape=outs, scratch_shapes=scratch, cost_estimat...  5.14 us
    ppermute x1, starting transfers between devices, rows_past_weights(): key_far = lax.ppermute(key_far, ('grp', 'hold'), perm)  3.74 us
    ppermute x2, starting transfers between devices, rows_past_weights(): halves.append(lax.ppermute(hidden, ('hold', 'tp'), perm))  2.19 us
    ppermute x2, waiting for transfers between devices, rows_past_weights(): halves.append(lax.ppermute(hidden, ('hold', 'tp'), perm))  1.91 us
  transfers between devices with their start and end apart: 23, of which 9 were waited for; matrix products, arithmetic and copies ran while one was open for 0% of the time, Pallas kernels for 7%

profile of v7, /device:TPU:0, one launch (start us, length us, event | category | flops | bytes accessed | tf_op | source)
XLA Modules:
  0.0 54.6 jit_solution(13068467345281836629)
XLA Ops:
  0.0 0.0 copy-start
  0.0 0.0 copy-start.1
  0.0 0.5 collective-permute-start.1
  0.5 0.1 collective-permute-start.2
  0.5 2.9 %collective-permute-start = (bf16[1,4,2,5120]{3,2,1,0:T(2,128)(2,1)}, bf16[1,4,2,5120]{3,2,1,0:T(2,128)(2,1)S(1)}, u32[]{:S(2)}, u32[]{:S(2)}) collective-permute-start(bf16[1,4,2,5120]{3,2,1,0:T(2,128)(2,1)} %cache.1), channel_id=1, source_target_pairs={{0,2},{2,0},{1,3},{3,1},{4,6},{6,4},{5,7},{7,5},{8,10},{10,8},{9,1... | collective-permute-start | bytes 245768 | tf_op jit(solution)/shard_map/ppermute | solution.py:74
  3.5 2.0 %shard_map.82 = (f32[8,5120]{1,0:T(8,128)S(1)}, bf16[1280,640]{1,0:T(8,128)(2,1)S(1)}, bf16[640,1024]{1,0:T(8,128)(2,1)S(1)}, bf16[256,256]{1,0:T(8,128)(2,1)S(1...) custom-call(bf16[1,4,2,5120]{3,2,1,0:T(2,128)(2,1)} %cache.1, f32[1280]{0:T(1024)} %ln_gain.3, ...), custom_call_target="tpu_custom_call" | custom-call | flops 8589934592 | bytes 3560512 | tf_op jit(solution)/shard_map/pallas_call | solution.py:84
  5.5 0.0 collective-permute-done.2.refs_7_
  5.5 0.9 %collective-permute-done.cache = bf16[1,4,2,5120]{3,2,1,0:T(2,128)(2,1)S(1)} collective-permute-done((bf16[1,4,2,5120]{3,2,1,0:T(2,128)(2,1)}, bf16[1,4,2,5120]{3,2,1,0:T(2,128)(2,1)S(1)}, u32[]{:S(2)}, u32[]{:S(2)}) %collective-permute-start) | collective-permute-done | bytes 81952 | tf_op jit(solution)/shard_map/ppermute | solution.py:74
  6.3 0.0 collective-permute-done.1.refs_5_
  6.3 0.0 collective-permute-start.6
  6.4 0.0 copy-done
  6.4 0.0 copy-done.1
  6.4 0.3 shard_map.83
  6.6 3.9 %collective-permute-start.3 = (bf16[16,1280]{1,0:T(8,128)(2,1)S(1)}, bf16[16,1280]{1,0:T(8,128)(2,1)S(1)}, u32[]{:S(2)}, u32[]{:S(2)}) collective-permute-start(bf16[16,1280]{1,0:T(8,128)(2,1)S(1)} %get-tuple-element.66), channel_id=1, source_target_pairs={{0,12},{4,8},{8,4},{12,0},{1,13},{5,9},{9,5},{13,1},{2,14},{6,10},... | collective-permute-start | bytes 122888 | tf_op jit(solution)/shard_map/ppermute | solution.py:74
  10.6 0.0 collective-permute-start.4
  10.6 0.6 %collective-permute-start.5 = (bf16[16,1280]{1,0:T(8,128)(2,1)S(1)}, bf16[16,1280]{1,0:T(8,128)(2,1)S(1)}, u32[]{:S(2)}, u32[]{:S(2)}) collective-permute-start(bf16[16,1280]{1,0:T(8,128)(2,1)S(1)} %get-tuple-element.68), channel_id=1, source_target_pairs={{0,4},{4,0},{8,12},{12,8},{1,5},{5,1},{9,13},{13,9},{2,6},{6,2},{1... | collective-permute-start | bytes 122888 | tf_op jit(solution)/shard_map/ppermute | solution.py:74
  11.2 3.7 %collective-permute-start.10 = (bf16[256,256]{1,0:T(8,128)(2,1)S(1)}, bf16[256,256]{1,0:T(8,128)(2,1)S(1)}, u32[]{:S(2)}, u32[]{:S(2)}) collective-permute-start(bf16[256,256]{1,0:T(8,128)(2,1)S(1)} %get-tuple-element.81), channel_id=1, source_target_pairs={{0,12},{4,8},{8,4},{12,0},{16,24},{20,28},{24,16},{28,20},{1,13},{... | collective-permute-start | bytes 393224 | tf_op jit(solution)/shard_map/ppermute | solution.py:357
  15.0 0.0 collective-permute-done.3.refs_0_
  15.0 0.9 %collective-permute-done.4.refs_1_ = bf16[16,1280]{1,0:T(8,128)(2,1)S(1)} collective-permute-done((bf16[16,1280]{1,0:T(8,128)(2,1)S(1)}, bf16[16,1280]{1,0:T(8,128)(2,1)S(1)}, u32[]{:S(2)}, u32[]{:S(2)}) %collective-permute-start.4) | collective-permute-done | bytes 40992 | tf_op jit(solution)/shard_map/ppermute | solution.py:74
  15.9 0.0 collective-permute-done.5.refs_2_
  15.9 0.7 %shard_map.84 = (bf16[32,640]{1,0:T(8,128)(2,1)S(1)}, bf16[32,640]{1,0:T(8,128)(2,1)S(1)}, bf16[32,640]{1,0:T(8,128)(2,1)S(1)}, bf16[32,640]{1,0:T(8,128)(2,1)S(1)}) custom-call(bf16[16,1280]{1,0:T(8,128)(2,1)S(1)} %collective-permute-done.3.refs_0_, bf16[16,1280]{1,0:T(8,128)(2,1)S(1)} %collective-permute-done.4.refs_1_, ...), custom_call_target="tpu_custom_call" | custom-call | flops 8589934592 | bytes 3440640 | tf_op jit(solution)/shard_map/pallas_call | solution.py:84
  16.5 0.0 collective-permute-done.6.w_other
  16.5 0.5 collective-permute-start.7
  17.1 3.1 %collective-permute-start.8 = (bf16[32,640]{1,0:T(8,128)(2,1)S(1)}, bf16[32,640]{1,0:T(8,128)(2,1)S(1)}, u32[]{:S(2)}, u32[]{:S(2)}) collective-permute-start(bf16[32,640]{1,0:T(8,128)(2,1)S(1)} %get-tuple-element.78), channel_id=1, source_target_pairs={{0,12},{4,8},{8,4},{12,0},{1,13},{5,9},{9,5},{13,1},{2,14},{6,10},... | collective-permute-start | bytes 122888 | tf_op jit(solution)/shard_map/ppermute | solution.py:74
  20.1 0.0 collective-permute-start.9
  20.1 1.3 %collective-permute-start.13 = (bf16[256,256]{1,0:T(8,128)(2,1)S(1)}, bf16[256,256]{1,0:T(8,128)(2,1)S(1)}, u32[]{:S(2)}, u32[]{:S(2)}) collective-permute-start(bf16[256,256]{1,0:T(8,128)(2,1)S(1)} %get-tuple-element.83), channel_id=1, source_target_pairs={{0,4},{4,0},{8,12},{12,8},{1,5},{5,1},{9,13},{13,9},{2,6},{6,2},{1... | collective-permute-start | bytes 393224 | tf_op jit(solution)/shard_map/ppermute | solution.py:74
  21.5 0.0 collective-permute-done.10
  21.5 2.5 %collective-permute-start.14 = (bf16[256,256]{1,0:T(8,128)(2,1)S(1)}, bf16[256,256]{1,0:T(8,128)(2,1)S(1)}, u32[]{:S(2)}, u32[]{:S(2)}) collective-permute-start(bf16[256,256]{1,0:T(8,128)(2,1)S(1)} %collective-permute-done.10), channel_id=1, source_target_pairs={{0,16},{16,0},{1,17},{17,1},{2,18},{18,2},{3,19},{19,3},{4,20},{20... | collective-permute-start | bytes 393224 | tf_op jit(solution)/shard_map/ppermute | solution.py:74
  23.9 0.0 collective-permute-done.7.refs_0_
  24.0 0.0 collective-permute-done.8.refs_1_
  24.0 1.2 %collective-permute-done.9.refs_2_ = bf16[32,640]{1,0:T(8,128)(2,1)S(1)} collective-permute-done((bf16[32,640]{1,0:T(8,128)(2,1)S(1)}, bf16[32,640]{1,0:T(8,128)(2,1)S(1)}, u32[]{:S(2)}, u32[]{:S(2)}) %collective-permute-start.9) | collective-permute-done | bytes 40992 | tf_op jit(solution)/shard_map/ppermute | solution.py:74
  25.1 0.3 shard_map.85
  25.5 1.5 %collective-permute-start.12 = (bf16[32,640]{1,0:T(8,128)(2,1)S(1)}, bf16[32,640]{1,0:T(8,128)(2,1)S(1)}, u32[]{:S(2)}, u32[]{:S(2)}) collective-permute-start(bf16[32,640]{1,0:T(8,128)(2,1)S(1)} %shard_map.85), channel_id=1, source_target_pairs={{0,2},{2,8},{4,0},{6,10},{8,4},{10,14},{12,6},{14,12},{1,3},{3,9},... | collective-permute-start | bytes 122888 | tf_op jit(solution)/shard_map/ppermute | solution.py:382
  27.0 0.7 %collective-permute-start.11 = (bf16[32,640]{1,0:T(8,128)(2,1)S(1)}, bf16[32,640]{1,0:T(8,128)(2,1)S(1)}, u32[]{:S(2)}, u32[]{:S(2)}) collective-permute-start(bf16[32,640]{1,0:T(8,128)(2,1)S(1)} %shard_map.85), channel_id=1, source_target_pairs={{0,0},{2,10},{4,2},{6,8},{8,6},{10,12},{12,4},{14,14},{1,1},{3,11}... | collective-permute-start | bytes 122888 | tf_op jit(solution)/shard_map/ppermute | solution.py:382
  27.7 0.0 copy-start.2
  27.7 0.0 copy-start.3
  27.7 0.0 collective-permute-done.13
  27.7 1.9 %collective-permute-done.12.second = bf16[32,640]{1,0:T(8,128)(2,1)S(1)} collective-permute-done((bf16[32,640]{1,0:T(8,128)(2,1)S(1)}, bf16[32,640]{1,0:T(8,128)(2,1)S(1)}, u32[]{:S(2)}, u32[]{:S(2)}) %collective-permute-start.12) | collective-permute-done | bytes 40992 | tf_op jit(solution)/shard_map/ppermute | solution.py:382
  29.6 0.0 collective-permute-done.11.first
  29.6 0.6 %shard_map.86 = (bf16[64,512]{1,0:T(8,128)(2,1)S(1)}, bf16[64,512]{1,0:T(8,128)(2,1)S(1)}, bf16[64,512]{1,0:T(8,128)(2,1)S(1)}, bf16[64,512]{1,0:T(8,128)(2,1)S(1)}) custom-call(bf16[32,640]{1,0:T(8,128)(2,1)S(1)} %collective-permute-done.11.first, bf16[32,640]{1,0:T(8,128)(2,1)S(1)} %collective-permute-done.12.second, ...), custom_call_target="tpu_custom_call" | custom-call | flops 167772160 | bytes 2703360 | tf_op jit(solution)/shard_map/pallas_call | solution.py:84
  30.2 0.0 collective-permute-done.14
  30.3 0.1 collective-permute-start.18
  30.4 4.1 %collective-permute-start.15 = (bf16[64,512]{1,0:T(8,128)(2,1)S(1)}, bf16[64,512]{1,0:T(8,128)(2,1)S(1)}, u32[]{:S(2)}, u32[]{:S(2)}) collective-permute-start(bf16[64,512]{1,0:T(8,128)(2,1)S(1)} %get-tuple-element.91), channel_id=1, source_target_pairs={{0,8},{4,12},{8,0},{12,4},{1,9},{5,13},{9,1},{13,5},{2,10},{6,14},... | collective-permute-start | bytes 196616 | tf_op jit(solution)/shard_map/ppermute | solution.py:74
  34.4 2.0 %collective-permute-start.16 = (bf16[64,512]{1,0:T(8,128)(2,1)S(1)}, bf16[64,512]{1,0:T(8,128)(2,1)S(1)}, u32[]{:S(2)}, u32[]{:S(2)}) collective-permute-start(bf16[64,512]{1,0:T(8,128)(2,1)S(1)} %get-tuple-element.92), channel_id=1, source_target_pairs={{0,4},{4,0},{8,12},{12,8},{1,5},{5,1},{9,13},{13,9},{2,6},{6,2},{1... | collective-permute-start | bytes 196616 | tf_op jit(solution)/shard_map/ppermute | solution.py:74
  36.4 1.1 %collective-permute-start.17 = (bf16[64,512]{1,0:T(8,128)(2,1)S(1)}, bf16[64,512]{1,0:T(8,128)(2,1)S(1)}, u32[]{:S(2)}, u32[]{:S(2)}) collective-permute-start(bf16[64,512]{1,0:T(8,128)(2,1)S(1)} %get-tuple-element.93), channel_id=1, source_target_pairs={{0,12},{4,8},{8,4},{12,0},{1,13},{5,9},{9,5},{13,1},{2,14},{6,10},... | collective-permute-start | bytes 196616 | tf_op jit(solution)/shard_map/ppermute | solution.py:74
  37.5 0.0 collective-permute-done.15.refs_0_
  37.5 1.4 %collective-permute-done.16.refs_1_ = bf16[64,512]{1,0:T(8,128)(2,1)S(1)} collective-permute-done((bf16[64,512]{1,0:T(8,128)(2,1)S(1)}, bf16[64,512]{1,0:T(8,128)(2,1)S(1)}, u32[]{:S(2)}, u32[]{:S(2)}) %collective-permute-start.16) | collective-permute-done | bytes 65568 | tf_op jit(solution)/shard_map/ppermute | solution.py:74
  38.9 3.9 %collective-permute-done.17.refs_2_ = bf16[64,512]{1,0:T(8,128)(2,1)S(1)} collective-permute-done((bf16[64,512]{1,0:T(8,128)(2,1)S(1)}, bf16[64,512]{1,0:T(8,128)(2,1)S(1)}, u32[]{:S(2)}, u32[]{:S(2)}) %collective-permute-start.17) | collective-permute-done | bytes 65568 | tf_op jit(solution)/shard_map/ppermute | solution.py:74
  42.7 0.0 collective-permute-done.18.refs_5_
  42.7 0.0 copy-done.2
  42.7 0.0 copy-done.3
  42.7 0.3 shard_map.87
  43.1 1.8 %collective-permute-start.19 = (bf16[16,1152]{1,0:T(8,128)(2,1)S(1)}, bf16[16,1152]{1,0:T(8,128)(2,1)S(1)}, u32[]{:S(2)}, u32[]{:S(2)}) collective-permute-start(bf16[16,1152]{1,0:T(8,128)(2,1)S(1)} %get-tuple-element.100), channel_id=1, source_target_pairs={{0,12},{4,8},{8,4},{12,0},{1,13},{5,9},{9,5},{13,1},{2,14},{6,10},... | collective-permute-start | bytes 110600 | tf_op jit(solution)/shard_map/ppermute | solution.py:74
  44.8 0.2 collective-permute-start.20
  45.0 2.5 %collective-permute-start.21 = (bf16[16,1152]{1,0:T(8,128)(2,1)S(1)}, bf16[16,1152]{1,0:T(8,128)(2,1)S(1)}, u32[]{:S(2)}, u32[]{:S(2)}) collective-permute-start(bf16[16,1152]{1,0:T(8,128)(2,1)S(1)} %get-tuple-element.102), channel_id=1, source_target_pairs={{0,8},{4,12},{8,0},{12,4},{1,9},{5,13},{9,1},{13,5},{2,10},{6,14},... | collective-permute-start | bytes 110600 | tf_op jit(solution)/shard_map/ppermute | solution.py:74
  47.5 1.7 %collective-permute-done.19.refs_0_ = bf16[16,1152]{1,0:T(8,128)(2,1)S(1)} collective-permute-done((bf16[16,1152]{1,0:T(8,128)(2,1)S(1)}, bf16[16,1152]{1,0:T(8,128)(2,1)S(1)}, u32[]{:S(2)}, u32[]{:S(2)}) %collective-permute-start.19) | collective-permute-done | bytes 36896 | tf_op jit(solution)/shard_map/ppermute | solution.py:74
  49.2 0.0 collective-permute-done.20.refs_1_
  49.2 0.7 %collective-permute-done.21.refs_2_ = bf16[16,1152]{1,0:T(8,128)(2,1)S(1)} collective-permute-done((bf16[16,1152]{1,0:T(8,128)(2,1)S(1)}, bf16[16,1152]{1,0:T(8,128)(2,1)S(1)}, u32[]{:S(2)}, u32[]{:S(2)}) %collective-permute-start.21) | collective-permute-done | bytes 36896 | tf_op jit(solution)/shard_map/ppermute | solution.py:74
  49.9 0.2 shard_map.88
  50.0 1.4 %collective-permute-start.22 = (bf16[8,1152]{1,0:T(8,128)(2,1)S(1)}, bf16[8,1152]{1,0:T(8,128)(2,1)S(1)}, u32[]{:S(2)}, u32[]{:S(2)}) collective-permute-start(bf16[8,1152]{1,0:T(8,128)(2,1)S(1)} %get-tuple-element.105), channel_id=1, source_target_pairs={{0,2},{2,0},{1,3},{3,1},{4,6},{6,4},{5,7},{7,5},{8,10},{10,8},{9,1... | collective-permute-start | bytes 55304 | tf_op jit(solution)/shard_map/ppermute | solution.py:74
  51.4 2.4 %collective-permute-done.22.came = bf16[8,1152]{1,0:T(8,128)(2,1)S(1)} collective-permute-done((bf16[8,1152]{1,0:T(8,128)(2,1)S(1)}, bf16[8,1152]{1,0:T(8,128)(2,1)S(1)}, u32[]{:S(2)}, u32[]{:S(2)}) %collective-permute-start.22) | collective-permute-done | bytes 18464 | tf_op jit(solution)/shard_map/ppermute | solution.py:74
  53.8 0.8 %shard_map.89 = bf16[1,4,2,1024]{3,2,1,0:T(2,128)(2,1)} custom-call(f32[8,1152]{1,0:T(8,128)S(1)} %get-tuple-element.104.kept, bf16[8,1152]{1,0:T(8,128)(2,1)S(1)} %collective-permute-done.22.came, s32[4,4]{1,0:T(4,128)S(1)} %copy-done, f32[4,128]{1,0:T(4,128)S(1)} %get-tuple-element.106.live), custom_call_target="tpu_custom_call" | custom-call | bytes 57408 | tf_op jit(solution)/shard_map/pallas_call | solution.py:84
  (4 shorter events, 0.0 us)
Async XLA Ops:
  0.0 6.4 %copy-start = (s32[4,4]{1,0:T(4,128)S(1)}, s32[4,4]{1,0:T(4,128)}, u32[]{:S(2)}) copy-start(s32[4,4]{1,0:T(4,128)} %matching.5) | copy-start | bytes 196
  0.0 6.4 %copy-start.1 = (f32[1280]{0:T(1024)S(1)}, f32[1280]{0:T(1024)}, u32[]{:S(2)}) copy-start(f32[1280]{0:T(1024)} %ln_gain.3) | copy-start | bytes 15364
  0.0 6.3 %collective-permute-start.1 = (bf16[1280,640]{1,0:T(8,128)(2,1)}, bf16[1280,640]{1,0:T(8,128)(2,1)S(1)}, u32[]{:S(2)}, u32[]{:S(2)}) collective-permute-start(bf16[1280,640]{1,0:T(8,128)(2,1)} %w_fc1.1), channel_id=1, source_target_pairs={{0,1},{1,0},{2,3},{3,2},{4,5},{5,4},{6,7},{7,6},{8,9},{9,8},{10,11... | collective-permute-start | bytes 4915208 | tf_op jit(solution)/shard_map/ppermute | solution.py:74
  0.5 5.0 %collective-permute-start.2 = (f32[1024]{0:T(1024)}, f32[1024]{0:T(1024)S(1)}, u32[]{:S(2)}, u32[]{:S(2)}) collective-permute-start(f32[1024]{0:T(1024)} %refs_6_.1), channel_id=1, source_target_pairs={{0,1},{1,0},{2,3},{3,2},{4,5},{5,4},{6,7},{7,6},{8,9},{9,8},{10,11... | collective-permute-start | bytes 12296 | tf_op jit(solution)/shard_map/ppermute | solution.py:74
  0.5 5.8 %collective-permute-start = (bf16[1,4,2,5120]{3,2,1,0:T(2,128)(2,1)}, bf16[1,4,2,5120]{3,2,1,0:T(2,128)(2,1)S(1)}, u32[]{:S(2)}, u32[]{:S(2)}) collective-permute-start(bf16[1,4,2,5120]{3,2,1,0:T(2,128)(2,1)} %cache.1), channel_id=1, source_target_pairs={{0,2},{2,0},{1,3},{3,1},{4,6},{6,4},{5,7},{7,5},{8,10},{10,8},{9,1... | collective-permute-start | bytes 245768 | tf_op jit(solution)/shard_map/ppermute | solution.py:74
  6.3 10.2 %collective-permute-start.6 = (bf16[640,1024]{1,0:T(8,128)(2,1)S(1)}, bf16[640,1024]{1,0:T(8,128)(2,1)S(1)}, u32[]{:S(2)}, u32[]{:S(2)}) collective-permute-start(bf16[640,1024]{1,0:T(8,128)(2,1)S(1)} %get-tuple-element.76.w_mine), channel_id=1, source_target_pairs={{0,1},{1,0},{2,3},{3,2},{4,5},{5,4},{6,7},{7,6},{8,9},{9,8},{10,11... | collective-permute-start | bytes 3932168 | tf_op jit(solution)/shard_map/ppermute | solution.py:74
  6.6 8.3 %collective-permute-start.3 = (bf16[16,1280]{1,0:T(8,128)(2,1)S(1)}, bf16[16,1280]{1,0:T(8,128)(2,1)S(1)}, u32[]{:S(2)}, u32[]{:S(2)}) collective-permute-start(bf16[16,1280]{1,0:T(8,128)(2,1)S(1)} %get-tuple-element.66), channel_id=1, source_target_pairs={{0,12},{4,8},{8,4},{12,0},{1,13},{5,9},{9,5},{13,1},{2,14},{6,10},... | collective-permute-start | bytes 122888 | tf_op jit(solution)/shard_map/ppermute | solution.py:74
  10.6 5.3 %collective-permute-start.4 = (bf16[16,1280]{1,0:T(8,128)(2,1)S(1)}, bf16[16,1280]{1,0:T(8,128)(2,1)S(1)}, u32[]{:S(2)}, u32[]{:S(2)}) collective-permute-start(bf16[16,1280]{1,0:T(8,128)(2,1)S(1)} %get-tuple-element.67), channel_id=1, source_target_pairs={{0,8},{4,12},{8,0},{12,4},{1,9},{5,13},{9,1},{13,5},{2,10},{6,14},... | collective-permute-start | bytes 122888 | tf_op jit(solution)/shard_map/ppermute | solution.py:74
  10.6 5.3 %collective-permute-start.5 = (bf16[16,1280]{1,0:T(8,128)(2,1)S(1)}, bf16[16,1280]{1,0:T(8,128)(2,1)S(1)}, u32[]{:S(2)}, u32[]{:S(2)}) collective-permute-start(bf16[16,1280]{1,0:T(8,128)(2,1)S(1)} %get-tuple-element.68), channel_id=1, source_target_pairs={{0,4},{4,0},{8,12},{12,8},{1,5},{5,1},{9,13},{13,9},{2,6},{6,2},{1... | collective-permute-start | bytes 122888 | tf_op jit(solution)/shard_map/ppermute | solution.py:74
  11.2 10.2 %collective-permute-start.10 = (bf16[256,256]{1,0:T(8,128)(2,1)S(1)}, bf16[256,256]{1,0:T(8,128)(2,1)S(1)}, u32[]{:S(2)}, u32[]{:S(2)}) collective-permute-start(bf16[256,256]{1,0:T(8,128)(2,1)S(1)} %get-tuple-element.81), channel_id=1, source_target_pairs={{0,12},{4,8},{8,4},{12,0},{16,24},{20,28},{24,16},{28,20},{1,13},{... | collective-permute-start | bytes 393224 | tf_op jit(solution)/shard_map/ppermute | solution.py:357
  16.5 7.4 %collective-permute-start.7 = (bf16[32,640]{1,0:T(8,128)(2,1)S(1)}, bf16[32,640]{1,0:T(8,128)(2,1)S(1)}, u32[]{:S(2)}, u32[]{:S(2)}) collective-permute-start(bf16[32,640]{1,0:T(8,128)(2,1)S(1)} %get-tuple-element.77), channel_id=1, source_target_pairs={{0,4},{4,0},{8,12},{12,8},{1,5},{5,1},{9,13},{13,9},{2,6},{6,2},{1... | collective-permute-start | bytes 122888 | tf_op jit(solution)/shard_map/ppermute | solution.py:74
  17.1 6.9 %collective-permute-start.8 = (bf16[32,640]{1,0:T(8,128)(2,1)S(1)}, bf16[32,640]{1,0:T(8,128)(2,1)S(1)}, u32[]{:S(2)}, u32[]{:S(2)}) collective-permute-start(bf16[32,640]{1,0:T(8,128)(2,1)S(1)} %get-tuple-element.78), channel_id=1, source_target_pairs={{0,12},{4,8},{8,4},{12,0},{1,13},{5,9},{9,5},{13,1},{2,14},{6,10},... | collective-permute-start | bytes 122888 | tf_op jit(solution)/shard_map/ppermute | solution.py:74
  20.1 5.0 %collective-permute-start.9 = (bf16[32,640]{1,0:T(8,128)(2,1)S(1)}, bf16[32,640]{1,0:T(8,128)(2,1)S(1)}, u32[]{:S(2)}, u32[]{:S(2)}) collective-permute-start(bf16[32,640]{1,0:T(8,128)(2,1)S(1)} %get-tuple-element.79), channel_id=1, source_target_pairs={{0,8},{4,12},{8,0},{12,4},{1,9},{5,13},{9,1},{13,5},{2,10},{6,14},... | collective-permute-start | bytes 122888 | tf_op jit(solution)/shard_map/ppermute | solution.py:74
  20.1 7.6 %collective-permute-start.13 = (bf16[256,256]{1,0:T(8,128)(2,1)S(1)}, bf16[256,256]{1,0:T(8,128)(2,1)S(1)}, u32[]{:S(2)}, u32[]{:S(2)}) collective-permute-start(bf16[256,256]{1,0:T(8,128)(2,1)S(1)} %get-tuple-element.83), channel_id=1, source_target_pairs={{0,4},{4,0},{8,12},{12,8},{1,5},{5,1},{9,13},{13,9},{2,6},{6,2},{1... | collective-permute-start | bytes 393224 | tf_op jit(solution)/shard_map/ppermute | solution.py:74
  21.5 8.8 %collective-permute-start.14 = (bf16[256,256]{1,0:T(8,128)(2,1)S(1)}, bf16[256,256]{1,0:T(8,128)(2,1)S(1)}, u32[]{:S(2)}, u32[]{:S(2)}) collective-permute-start(bf16[256,256]{1,0:T(8,128)(2,1)S(1)} %collective-permute-done.10), channel_id=1, source_target_pairs={{0,16},{16,0},{1,17},{17,1},{2,18},{18,2},{3,19},{19,3},{4,20},{20... | collective-permute-start | bytes 393224 | tf_op jit(solution)/shard_map/ppermute | solution.py:74
  25.5 4.2 %collective-permute-start.12 = (bf16[32,640]{1,0:T(8,128)(2,1)S(1)}, bf16[32,640]{1,0:T(8,128)(2,1)S(1)}, u32[]{:S(2)}, u32[]{:S(2)}) collective-permute-start(bf16[32,640]{1,0:T(8,128)(2,1)S(1)} %shard_map.85), channel_id=1, source_target_pairs={{0,2},{2,8},{4,0},{6,10},{8,4},{10,14},{12,6},{14,12},{1,3},{3,9},... | collective-permute-start | bytes 122888 | tf_op jit(solution)/shard_map/ppermute | solution.py:382
  27.0 2.6 %collective-permute-start.11 = (bf16[32,640]{1,0:T(8,128)(2,1)S(1)}, bf16[32,640]{1,0:T(8,128)(2,1)S(1)}, u32[]{:S(2)}, u32[]{:S(2)}) collective-permute-start(bf16[32,640]{1,0:T(8,128)(2,1)S(1)} %shard_map.85), channel_id=1, source_target_pairs={{0,0},{2,10},{4,2},{6,8},{8,6},{10,12},{12,4},{14,14},{1,1},{3,11}... | collective-permute-start | bytes 122888 | tf_op jit(solution)/shard_map/ppermute | solution.py:382
  27.7 15.1 %copy-start.2 = (f32[1024]{0:T(1024)S(1)}, f32[1024]{0:T(1024)}, u32[]{:S(2)}) copy-start(f32[1024]{0:T(1024)} %refs_6_.1) | copy-start | bytes 12292
  27.7 15.1 %copy-start.3 = (s32[1,4,1]{1,2,0:T(1,128)S(1)}, s32[1,4,1]{1,2,0:T(1,128)}, u32[]{:S(2)}) copy-start(s32[1,4,1]{1,2,0:T(1,128)} %param.15) | copy-start | bytes 52
  30.3 12.4 %collective-permute-start.18 = (bf16[1024,256]{1,0:T(8,128)(2,1)S(1)}, bf16[1024,256]{1,0:T(8,128)(2,1)S(1)}, u32[]{:S(2)}, u32[]{:S(2)}) collective-permute-start(bf16[1024,256]{1,0:T(8,128)(2,1)S(1)} %constant_dynamic-update-slice_fusion.refs_4_), channel_id=1, source_target_pairs={{0,1},{1,0},{2,3},{3,2},{4,5},{5,4},{6,7},{7,6},{8,9},{9,8},{10,11... | collective-permute-start | bytes 1572872 | tf_op jit(solution)/shard_map/ppermute | solution.py:74
  30.4 7.1 %collective-permute-start.15 = (bf16[64,512]{1,0:T(8,128)(2,1)S(1)}, bf16[64,512]{1,0:T(8,128)(2,1)S(1)}, u32[]{:S(2)}, u32[]{:S(2)}) collective-permute-start(bf16[64,512]{1,0:T(8,128)(2,1)S(1)} %get-tuple-element.91), channel_id=1, source_target_pairs={{0,8},{4,12},{8,0},{12,4},{1,9},{5,13},{9,1},{13,5},{2,10},{6,14},... | collective-permute-start | bytes 196616 | tf_op jit(solution)/shard_map/ppermute | solution.py:74
  34.4 4.4 %collective-permute-start.16 = (bf16[64,512]{1,0:T(8,128)(2,1)S(1)}, bf16[64,512]{1,0:T(8,128)(2,1)S(1)}, u32[]{:S(2)}, u32[]{:S(2)}) collective-permute-start(bf16[64,512]{1,0:T(8,128)(2,1)S(1)} %get-tuple-element.92), channel_id=1, source_target_pairs={{0,4},{4,0},{8,12},{12,8},{1,5},{5,1},{9,13},{13,9},{2,6},{6,2},{1... | collective-permute-start | bytes 196616 | tf_op jit(solution)/shard_map/ppermute | solution.py:74
  36.4 6.3 %collective-permute-start.17 = (bf16[64,512]{1,0:T(8,128)(2,1)S(1)}, bf16[64,512]{1,0:T(8,128)(2,1)S(1)}, u32[]{:S(2)}, u32[]{:S(2)}) collective-permute-start(bf16[64,512]{1,0:T(8,128)(2,1)S(1)} %get-tuple-element.93), channel_id=1, source_target_pairs={{0,12},{4,8},{8,4},{12,0},{1,13},{5,9},{9,5},{13,1},{2,14},{6,10},... | collective-permute-start | bytes 196616 | tf_op jit(solution)/shard_map/ppermute | solution.py:74
  43.1 6.1 %collective-permute-start.19 = (bf16[16,1152]{1,0:T(8,128)(2,1)S(1)}, bf16[16,1152]{1,0:T(8,128)(2,1)S(1)}, u32[]{:S(2)}, u32[]{:S(2)}) collective-permute-start(bf16[16,1152]{1,0:T(8,128)(2,1)S(1)} %get-tuple-element.100), channel_id=1, source_target_pairs={{0,12},{4,8},{8,4},{12,0},{1,13},{5,9},{9,5},{13,1},{2,14},{6,10},... | collective-permute-start | bytes 110600 | tf_op jit(solution)/shard_map/ppermute | solution.py:74
  44.8 4.4 %collective-permute-start.20 = (bf16[16,1152]{1,0:T(8,128)(2,1)S(1)}, bf16[16,1152]{1,0:T(8,128)(2,1)S(1)}, u32[]{:S(2)}, u32[]{:S(2)}) collective-permute-start(bf16[16,1152]{1,0:T(8,128)(2,1)S(1)} %get-tuple-element.101), channel_id=1, source_target_pairs={{0,4},{4,0},{8,12},{12,8},{1,5},{5,1},{9,13},{13,9},{2,6},{6,2},{1... | collective-permute-start | bytes 110600 | tf_op jit(solution)/shard_map/ppermute | solution.py:74
  45.0 4.9 %collective-permute-start.21 = (bf16[16,1152]{1,0:T(8,128)(2,1)S(1)}, bf16[16,1152]{1,0:T(8,128)(2,1)S(1)}, u32[]{:S(2)}, u32[]{:S(2)}) collective-permute-start(bf16[16,1152]{1,0:T(8,128)(2,1)S(1)} %get-tuple-element.102), channel_id=1, source_target_pairs={{0,8},{4,12},{8,0},{12,4},{1,9},{5,13},{9,1},{13,5},{2,10},{6,14},... | collective-permute-start | bytes 110600 | tf_op jit(solution)/shard_map/ppermute | solution.py:74
  50.0 3.8 %collective-permute-start.22 = (bf16[8,1152]{1,0:T(8,128)(2,1)S(1)}, bf16[8,1152]{1,0:T(8,128)(2,1)S(1)}, u32[]{:S(2)}, u32[]{:S(2)}) collective-permute-start(bf16[8,1152]{1,0:T(8,128)(2,1)S(1)} %get-tuple-element.105), channel_id=1, source_target_pairs={{0,2},{2,0},{1,3},{3,1},{4,6},{6,4},{5,7},{7,5},{8,10},{10,8},{9,1... | collective-permute-start | bytes 55304 | tf_op jit(solution)/shard_map/ppermute | solution.py:74

commit v8 on v7

--- a/solution.py
+++ b/solution.py
@@ -145,7 +145,7 @@
 
 def first_kernel(places, *refs):
     pieces, weights, outs = refs[:4], refs[4:6], refs[6:10]
-    rows, sums = refs[10:]
+    rows = refs[10]
     h, rep = lax.axis_index("hold"), lax.axis_index("rep")
     size = pieces[0].shape[0] // 2
     half = 4 * size
@@ -155,11 +155,10 @@
             start = pl.multiple_of(b * half + (h ^ k) * size, 8)
             rows[pl.ds(start, size), :] = part[b * size : (b + 1) * size]
     x = rows[...].astype(jnp.bfloat16)
-    for i, weight in enumerate(weights):
-        sums[rep ^ i] = dot(x, weight[...])
+    mine, other = (dot(x, weight[...]).astype(jnp.bfloat16) for weight in weights)
     for k, out in enumerate(outs):
-        start = pl.multiple_of(((h ^ k) & 1) * half, 16)
-        out[...] = sums[(h ^ k) >> 1, pl.ds(start, half), :].astype(jnp.bfloat16)
+        part = jnp.where((h ^ k) >> 1 == rep, mine, other)
+        out[...] = jnp.where((h ^ k) & 1 == 0, part[:half], part[half:])
 
 
 ERFC_NEAR = (
@@ -363,7 +362,7 @@
         *exchange(pieces, order),
         w_fc1_mine,
         w_fc1_other,
-        scratch=[vmem((8 * rows, chunk), f32), vmem((2, 8 * rows, hidden_cols), f32)],
+        scratch=[vmem((8 * rows, chunk), f32)],
         flops=long,
     )
     *partial, w_fc2_other = lax.optimization_barrier((*partial, w_fc2_other))

time: 54.7 us -> 54.7 us (level)
  no operation moved by 1% of the time
where the time goes in v8:
time: 54.7 us; the launch traced here: 54.6 us
  starting transfers between devices  34.4 us (63%)
  waiting for transfers between devices  14.9 us (27%)
  Pallas kernels  5.12 us (9%)
    ppermute x20, starting transfers between devices, swap(): return lax.ppermute(x, axis, [(i, i ^ step) for i in range(n)])  28.4 us
    ppermute x20, waiting for transfers between devices, swap(): return lax.ppermute(x, axis, [(i, i ^ step) for i in range(n)])  12.9 us
    pallas_call x8, Pallas kernels, call(): pl.pallas_call(body, out_shape=outs, scratch_shapes=scratch, cost_estimat...  5.12 us
    ppermute x1, starting transfers between devices, rows_past_weights(): key_far = lax.ppermute(key_far, ('grp', 'hold'), perm)  3.74 us
    ppermute x2, starting transfers between devices, rows_past_weights(): halves.append(lax.ppermute(hidden, ('hold', 'tp'), perm))  2.19 us
    ppermute x2, waiting for transfers between devices, rows_past_weights(): halves.append(lax.ppermute(hidden, ('hold', 'tp'), perm))  1.97 us
  transfers between devices with their start and end apart: 23, of which 9 were waited for; matrix products, arithmetic and copies ran while one was open for 0% of the time, Pallas kernels for 7%

profile of v8, /device:TPU:0, one launch (start us, length us, event | category | flops | bytes accessed | tf_op | source)
XLA Modules:
  0.0 54.6 jit_solution(9609116856401949691)
XLA Ops:
  0.0 0.0 copy-start
  0.0 0.0 copy-start.1
  0.0 0.5 collective-permute-start.1
  0.5 0.1 collective-permute-start.2
  0.5 2.9 %collective-permute-start = (bf16[1,4,2,5120]{3,2,1,0:T(2,128)(2,1)}, bf16[1,4,2,5120]{3,2,1,0:T(2,128)(2,1)S(1)}, u32[]{:S(2)}, u32[]{:S(2)}) collective-permute-start(bf16[1,4,2,5120]{3,2,1,0:T(2,128)(2,1)} %cache.1), channel_id=1, source_target_pairs={{0,2},{2,0},{1,3},{3,1},{4,6},{6,4},{5,7},{7,5},{8,10},{10,8},{9,1... | collective-permute-start | bytes 245768 | tf_op jit(solution)/shard_map/ppermute | solution.py:74
  3.5 2.0 %shard_map.82 = (f32[8,5120]{1,0:T(8,128)S(1)}, bf16[1280,640]{1,0:T(8,128)(2,1)S(1)}, bf16[640,1024]{1,0:T(8,128)(2,1)S(1)}, bf16[256,256]{1,0:T(8,128)(2,1)S(1...) custom-call(bf16[1,4,2,5120]{3,2,1,0:T(2,128)(2,1)} %cache.1, f32[1280]{0:T(1024)} %ln_gain.3, ...), custom_call_target="tpu_custom_call" | custom-call | flops 8589934592 | bytes 3560512 | tf_op jit(solution)/shard_map/pallas_call | solution.py:84
  5.5 0.0 collective-permute-done.2.refs_7_
  5.5 0.9 %collective-permute-done.cache = bf16[1,4,2,5120]{3,2,1,0:T(2,128)(2,1)S(1)} collective-permute-done((bf16[1,4,2,5120]{3,2,1,0:T(2,128)(2,1)}, bf16[1,4,2,5120]{3,2,1,0:T(2,128)(2,1)S(1)}, u32[]{:S(2)}, u32[]{:S(2)}) %collective-permute-start) | collective-permute-done | bytes 81952 | tf_op jit(solution)/shard_map/ppermute | solution.py:74
  6.3 0.0 collective-permute-done.1.refs_5_
  6.3 0.0 collective-permute-start.6
  6.4 0.0 copy-done
  6.4 0.0 copy-done.1
  6.4 0.3 shard_map.83
  6.6 3.9 %collective-permute-start.3 = (bf16[16,1280]{1,0:T(8,128)(2,1)S(1)}, bf16[16,1280]{1,0:T(8,128)(2,1)S(1)}, u32[]{:S(2)}, u32[]{:S(2)}) collective-permute-start(bf16[16,1280]{1,0:T(8,128)(2,1)S(1)} %get-tuple-element.66), channel_id=1, source_target_pairs={{0,12},{4,8},{8,4},{12,0},{1,13},{5,9},{9,5},{13,1},{2,14},{6,10},... | collective-permute-start | bytes 122888 | tf_op jit(solution)/shard_map/ppermute | solution.py:74
  10.6 0.0 collective-permute-start.4
  10.6 0.6 %collective-permute-start.5 = (bf16[16,1280]{1,0:T(8,128)(2,1)S(1)}, bf16[16,1280]{1,0:T(8,128)(2,1)S(1)}, u32[]{:S(2)}, u32[]{:S(2)}) collective-permute-start(bf16[16,1280]{1,0:T(8,128)(2,1)S(1)} %get-tuple-element.68), channel_id=1, source_target_pairs={{0,4},{4,0},{8,12},{12,8},{1,5},{5,1},{9,13},{13,9},{2,6},{6,2},{1... | collective-permute-start | bytes 122888 | tf_op jit(solution)/shard_map/ppermute | solution.py:74
  11.2 3.7 %collective-permute-start.10 = (bf16[256,256]{1,0:T(8,128)(2,1)S(1)}, bf16[256,256]{1,0:T(8,128)(2,1)S(1)}, u32[]{:S(2)}, u32[]{:S(2)}) collective-permute-start(bf16[256,256]{1,0:T(8,128)(2,1)S(1)} %get-tuple-element.81), channel_id=1, source_target_pairs={{0,12},{4,8},{8,4},{12,0},{16,24},{20,28},{24,16},{28,20},{1,13},{... | collective-permute-start | bytes 393224 | tf_op jit(solution)/shard_map/ppermute | solution.py:356
  15.0 0.0 collective-permute-done.3.refs_0_
  15.0 0.9 %collective-permute-done.4.refs_1_ = bf16[16,1280]{1,0:T(8,128)(2,1)S(1)} collective-permute-done((bf16[16,1280]{1,0:T(8,128)(2,1)S(1)}, bf16[16,1280]{1,0:T(8,128)(2,1)S(1)}, u32[]{:S(2)}, u32[]{:S(2)}) %collective-permute-start.4) | collective-permute-done | bytes 40992 | tf_op jit(solution)/shard_map/ppermute | solution.py:74
  15.9 0.0 collective-permute-done.5.refs_2_
  15.9 0.6 %shard_map.84 = (bf16[32,640]{1,0:T(8,128)(2,1)S(1)}, bf16[32,640]{1,0:T(8,128)(2,1)S(1)}, bf16[32,640]{1,0:T(8,128)(2,1)S(1)}, bf16[32,640]{1,0:T(8,128)(2,1)S(1)}) custom-call(bf16[16,1280]{1,0:T(8,128)(2,1)S(1)} %collective-permute-done.3.refs_0_, bf16[16,1280]{1,0:T(8,128)(2,1)S(1)} %collective-permute-done.4.refs_1_, ...), custom_call_target="tpu_custom_call" | custom-call | flops 8589934592 | bytes 3440640 | tf_op jit(solution)/shard_map/pallas_call | solution.py:84
  16.5 0.0 collective-permute-done.6.w_other
  16.5 0.5 collective-permute-start.7
  17.1 3.1 %collective-permute-start.8 = (bf16[32,640]{1,0:T(8,128)(2,1)S(1)}, bf16[32,640]{1,0:T(8,128)(2,1)S(1)}, u32[]{:S(2)}, u32[]{:S(2)}) collective-permute-start(bf16[32,640]{1,0:T(8,128)(2,1)S(1)} %get-tuple-element.78), channel_id=1, source_target_pairs={{0,12},{4,8},{8,4},{12,0},{1,13},{5,9},{9,5},{13,1},{2,14},{6,10},... | collective-permute-start | bytes 122888 | tf_op jit(solution)/shard_map/ppermute | solution.py:74
  20.1 0.0 collective-permute-start.9
  20.1 1.3 %collective-permute-start.13 = (bf16[256,256]{1,0:T(8,128)(2,1)S(1)}, bf16[256,256]{1,0:T(8,128)(2,1)S(1)}, u32[]{:S(2)}, u32[]{:S(2)}) collective-permute-start(bf16[256,256]{1,0:T(8,128)(2,1)S(1)} %get-tuple-element.83), channel_id=1, source_target_pairs={{0,4},{4,0},{8,12},{12,8},{1,5},{5,1},{9,13},{13,9},{2,6},{6,2},{1... | collective-permute-start | bytes 393224 | tf_op jit(solution)/shard_map/ppermute | solution.py:74
  21.4 0.0 collective-permute-done.10
  21.4 2.5 %collective-permute-start.14 = (bf16[256,256]{1,0:T(8,128)(2,1)S(1)}, bf16[256,256]{1,0:T(8,128)(2,1)S(1)}, u32[]{:S(2)}, u32[]{:S(2)}) collective-permute-start(bf16[256,256]{1,0:T(8,128)(2,1)S(1)} %collective-permute-done.10), channel_id=1, source_target_pairs={{0,16},{16,0},{1,17},{17,1},{2,18},{18,2},{3,19},{19,3},{4,20},{20... | collective-permute-start | bytes 393224 | tf_op jit(solution)/shard_map/ppermute | solution.py:74
  23.9 0.0 collective-permute-done.7.refs_0_
  24.0 0.0 collective-permute-done.8.refs_1_
  24.0 1.2 %collective-permute-done.9.refs_2_ = bf16[32,640]{1,0:T(8,128)(2,1)S(1)} collective-permute-done((bf16[32,640]{1,0:T(8,128)(2,1)S(1)}, bf16[32,640]{1,0:T(8,128)(2,1)S(1)}, u32[]{:S(2)}, u32[]{:S(2)}) %collective-permute-start.9) | collective-permute-done | bytes 40992 | tf_op jit(solution)/shard_map/ppermute | solution.py:74
  25.1 0.3 shard_map.85
  25.4 1.5 %collective-permute-start.12 = (bf16[32,640]{1,0:T(8,128)(2,1)S(1)}, bf16[32,640]{1,0:T(8,128)(2,1)S(1)}, u32[]{:S(2)}, u32[]{:S(2)}) collective-permute-start(bf16[32,640]{1,0:T(8,128)(2,1)S(1)} %shard_map.85), channel_id=1, source_target_pairs={{0,2},{2,8},{4,0},{6,10},{8,4},{10,14},{12,6},{14,12},{1,3},{3,9},... | collective-permute-start | bytes 122888 | tf_op jit(solution)/shard_map/ppermute | solution.py:381
  27.0 0.7 %collective-permute-start.11 = (bf16[32,640]{1,0:T(8,128)(2,1)S(1)}, bf16[32,640]{1,0:T(8,128)(2,1)S(1)}, u32[]{:S(2)}, u32[]{:S(2)}) collective-permute-start(bf16[32,640]{1,0:T(8,128)(2,1)S(1)} %shard_map.85), channel_id=1, source_target_pairs={{0,0},{2,10},{4,2},{6,8},{8,6},{10,12},{12,4},{14,14},{1,1},{3,11}... | collective-permute-start | bytes 122888 | tf_op jit(solution)/shard_map/ppermute | solution.py:381
  27.7 0.0 copy-start.2
  27.7 0.0 copy-start.3
  27.7 0.0 collective-permute-done.13
  27.7 2.0 %collective-permute-done.12.second = bf16[32,640]{1,0:T(8,128)(2,1)S(1)} collective-permute-done((bf16[32,640]{1,0:T(8,128)(2,1)S(1)}, bf16[32,640]{1,0:T(8,128)(2,1)S(1)}, u32[]{:S(2)}, u32[]{:S(2)}) %collective-permute-start.12) | collective-permute-done | bytes 40992 | tf_op jit(solution)/shard_map/ppermute | solution.py:381
  29.7 0.0 collective-permute-done.11.first
  29.7 0.6 %shard_map.86 = (bf16[64,512]{1,0:T(8,128)(2,1)S(1)}, bf16[64,512]{1,0:T(8,128)(2,1)S(1)}, bf16[64,512]{1,0:T(8,128)(2,1)S(1)}, bf16[64,512]{1,0:T(8,128)(2,1)S(1)}) custom-call(bf16[32,640]{1,0:T(8,128)(2,1)S(1)} %collective-permute-done.11.first, bf16[32,640]{1,0:T(8,128)(2,1)S(1)} %collective-permute-done.12.second, ...), custom_call_target="tpu_custom_call" | custom-call | flops 167772160 | bytes 2703360 | tf_op jit(solution)/shard_map/pallas_call | solution.py:84
  30.3 0.0 collective-permute-done.14
  30.3 0.1 collective-permute-start.18
  30.4 4.0 %collective-permute-start.15 = (bf16[64,512]{1,0:T(8,128)(2,1)S(1)}, bf16[64,512]{1,0:T(8,128)(2,1)S(1)}, u32[]{:S(2)}, u32[]{:S(2)}) collective-permute-start(bf16[64,512]{1,0:T(8,128)(2,1)S(1)} %get-tuple-element.91), channel_id=1, source_target_pairs={{0,8},{4,12},{8,0},{12,4},{1,9},{5,13},{9,1},{13,5},{2,10},{6,14},... | collective-permute-start | bytes 196616 | tf_op jit(solution)/shard_map/ppermute | solution.py:74
  34.4 2.0 %collective-permute-start.16 = (bf16[64,512]{1,0:T(8,128)(2,1)S(1)}, bf16[64,512]{1,0:T(8,128)(2,1)S(1)}, u32[]{:S(2)}, u32[]{:S(2)}) collective-permute-start(bf16[64,512]{1,0:T(8,128)(2,1)S(1)} %get-tuple-element.92), channel_id=1, source_target_pairs={{0,4},{4,0},{8,12},{12,8},{1,5},{5,1},{9,13},{13,9},{2,6},{6,2},{1... | collective-permute-start | bytes 196616 | tf_op jit(solution)/shard_map/ppermute | solution.py:74
  36.4 1.1 %collective-permute-start.17 = (bf16[64,512]{1,0:T(8,128)(2,1)S(1)}, bf16[64,512]{1,0:T(8,128)(2,1)S(1)}, u32[]{:S(2)}, u32[]{:S(2)}) collective-permute-start(bf16[64,512]{1,0:T(8,128)(2,1)S(1)} %get-tuple-element.93), channel_id=1, source_target_pairs={{0,12},{4,8},{8,4},{12,0},{1,13},{5,9},{9,5},{13,1},{2,14},{6,10},... | collective-permute-start | bytes 196616 | tf_op jit(solution)/shard_map/ppermute | solution.py:74
  37.5 0.0 collective-permute-done.15.refs_0_
  37.5 1.3 %collective-permute-done.16.refs_1_ = bf16[64,512]{1,0:T(8,128)(2,1)S(1)} collective-permute-done((bf16[64,512]{1,0:T(8,128)(2,1)S(1)}, bf16[64,512]{1,0:T(8,128)(2,1)S(1)}, u32[]{:S(2)}, u32[]{:S(2)}) %collective-permute-start.16) | collective-permute-done | bytes 65568 | tf_op jit(solution)/shard_map/ppermute | solution.py:74
  38.8 3.9 %collective-permute-done.17.refs_2_ = bf16[64,512]{1,0:T(8,128)(2,1)S(1)} collective-permute-done((bf16[64,512]{1,0:T(8,128)(2,1)S(1)}, bf16[64,512]{1,0:T(8,128)(2,1)S(1)}, u32[]{:S(2)}, u32[]{:S(2)}) %collective-permute-start.17) | collective-permute-done | bytes 65568 | tf_op jit(solution)/shard_map/ppermute | solution.py:74
  42.7 0.0 collective-permute-done.18.refs_5_
  42.7 0.0 copy-done.2
  42.7 0.0 copy-done.3
  42.7 0.3 shard_map.87
  43.1 1.8 %collective-permute-start.19 = (bf16[16,1152]{1,0:T(8,128)(2,1)S(1)}, bf16[16,1152]{1,0:T(8,128)(2,1)S(1)}, u32[]{:S(2)}, u32[]{:S(2)}) collective-permute-start(bf16[16,1152]{1,0:T(8,128)(2,1)S(1)} %get-tuple-element.100), channel_id=1, source_target_pairs={{0,12},{4,8},{8,4},{12,0},{1,13},{5,9},{9,5},{13,1},{2,14},{6,10},... | collective-permute-start | bytes 110600 | tf_op jit(solution)/shard_map/ppermute | solution.py:74
  44.8 0.2 collective-permute-start.20
  45.0 2.5 %collective-permute-start.21 = (bf16[16,1152]{1,0:T(8,128)(2,1)S(1)}, bf16[16,1152]{1,0:T(8,128)(2,1)S(1)}, u32[]{:S(2)}, u32[]{:S(2)}) collective-permute-start(bf16[16,1152]{1,0:T(8,128)(2,1)S(1)} %get-tuple-element.102), channel_id=1, source_target_pairs={{0,8},{4,12},{8,0},{12,4},{1,9},{5,13},{9,1},{13,5},{2,10},{6,14},... | collective-permute-start | bytes 110600 | tf_op jit(solution)/shard_map/ppermute | solution.py:74
  47.5 1.7 %collective-permute-done.19.refs_0_ = bf16[16,1152]{1,0:T(8,128)(2,1)S(1)} collective-permute-done((bf16[16,1152]{1,0:T(8,128)(2,1)S(1)}, bf16[16,1152]{1,0:T(8,128)(2,1)S(1)}, u32[]{:S(2)}, u32[]{:S(2)}) %collective-permute-start.19) | collective-permute-done | bytes 36896 | tf_op jit(solution)/shard_map/ppermute | solution.py:74
  49.2 0.0 collective-permute-done.20.refs_1_
  49.2 0.7 %collective-permute-done.21.refs_2_ = bf16[16,1152]{1,0:T(8,128)(2,1)S(1)} collective-permute-done((bf16[16,1152]{1,0:T(8,128)(2,1)S(1)}, bf16[16,1152]{1,0:T(8,128)(2,1)S(1)}, u32[]{:S(2)}, u32[]{:S(2)}) %collective-permute-start.21) | collective-permute-done | bytes 36896 | tf_op jit(solution)/shard_map/ppermute | solution.py:74
  49.9 0.2 shard_map.88
  50.0 1.4 %collective-permute-start.22 = (bf16[8,1152]{1,0:T(8,128)(2,1)S(1)}, bf16[8,1152]{1,0:T(8,128)(2,1)S(1)}, u32[]{:S(2)}, u32[]{:S(2)}) collective-permute-start(bf16[8,1152]{1,0:T(8,128)(2,1)S(1)} %get-tuple-element.105), channel_id=1, source_target_pairs={{0,2},{2,0},{1,3},{3,1},{4,6},{6,4},{5,7},{7,5},{8,10},{10,8},{9,1... | collective-permute-start | bytes 55304 | tf_op jit(solution)/shard_map/ppermute | solution.py:74
  51.4 2.4 %collective-permute-done.22.came = bf16[8,1152]{1,0:T(8,128)(2,1)S(1)} collective-permute-done((bf16[8,1152]{1,0:T(8,128)(2,1)S(1)}, bf16[8,1152]{1,0:T(8,128)(2,1)S(1)}, u32[]{:S(2)}, u32[]{:S(2)}) %collective-permute-start.22) | collective-permute-done | bytes 18464 | tf_op jit(solution)/shard_map/ppermute | solution.py:74
  53.8 0.8 %shard_map.89 = bf16[1,4,2,1024]{3,2,1,0:T(2,128)(2,1)} custom-call(f32[8,1152]{1,0:T(8,128)S(1)} %get-tuple-element.104.kept, bf16[8,1152]{1,0:T(8,128)(2,1)S(1)} %collective-permute-done.22.came, s32[4,4]{1,0:T(4,128)S(1)} %copy-done, f32[4,128]{1,0:T(4,128)S(1)} %get-tuple-element.106.live), custom_call_target="tpu_custom_call" | custom-call | bytes 57408 | tf_op jit(solution)/shard_map/pallas_call | solution.py:84
  (4 shorter events, 0.0 us)
Async XLA Ops:
  0.0 6.4 %copy-start = (s32[4,4]{1,0:T(4,128)S(1)}, s32[4,4]{1,0:T(4,128)}, u32[]{:S(2)}) copy-start(s32[4,4]{1,0:T(4,128)} %matching.5) | copy-start | bytes 196
  0.0 6.4 %copy-start.1 = (f32[1280]{0:T(1024)S(1)}, f32[1280]{0:T(1024)}, u32[]{:S(2)}) copy-start(f32[1280]{0:T(1024)} %ln_gain.3) | copy-start | bytes 15364
  0.0 6.3 %collective-permute-start.1 = (bf16[1280,640]{1,0:T(8,128)(2,1)}, bf16[1280,640]{1,0:T(8,128)(2,1)S(1)}, u32[]{:S(2)}, u32[]{:S(2)}) collective-permute-start(bf16[1280,640]{1,0:T(8,128)(2,1)} %w_fc1.1), channel_id=1, source_target_pairs={{0,1},{1,0},{2,3},{3,2},{4,5},{5,4},{6,7},{7,6},{8,9},{9,8},{10,11... | collective-permute-start | bytes 4915208 | tf_op jit(solution)/shard_map/ppermute | solution.py:74
  0.5 5.0 %collective-permute-start.2 = (f32[1024]{0:T(1024)}, f32[1024]{0:T(1024)S(1)}, u32[]{:S(2)}, u32[]{:S(2)}) collective-permute-start(f32[1024]{0:T(1024)} %refs_6_.1), channel_id=1, source_target_pairs={{0,1},{1,0},{2,3},{3,2},{4,5},{5,4},{6,7},{7,6},{8,9},{9,8},{10,11... | collective-permute-start | bytes 12296 | tf_op jit(solution)/shard_map/ppermute | solution.py:74
  0.5 5.8 %collective-permute-start = (bf16[1,4,2,5120]{3,2,1,0:T(2,128)(2,1)}, bf16[1,4,2,5120]{3,2,1,0:T(2,128)(2,1)S(1)}, u32[]{:S(2)}, u32[]{:S(2)}) collective-permute-start(bf16[1,4,2,5120]{3,2,1,0:T(2,128)(2,1)} %cache.1), channel_id=1, source_target_pairs={{0,2},{2,0},{1,3},{3,1},{4,6},{6,4},{5,7},{7,5},{8,10},{10,8},{9,1... | collective-permute-start | bytes 245768 | tf_op jit(solution)/shard_map/ppermute | solution.py:74
  6.3 10.2 %collective-permute-start.6 = (bf16[640,1024]{1,0:T(8,128)(2,1)S(1)}, bf16[640,1024]{1,0:T(8,128)(2,1)S(1)}, u32[]{:S(2)}, u32[]{:S(2)}) collective-permute-start(bf16[640,1024]{1,0:T(8,128)(2,1)S(1)} %get-tuple-element.76.w_mine), channel_id=1, source_target_pairs={{0,1},{1,0},{2,3},{3,2},{4,5},{5,4},{6,7},{7,6},{8,9},{9,8},{10,11... | collective-permute-start | bytes 3932168 | tf_op jit(solution)/shard_map/ppermute | solution.py:74
  6.6 8.3 %collective-permute-start.3 = (bf16[16,1280]{1,0:T(8,128)(2,1)S(1)}, bf16[16,1280]{1,0:T(8,128)(2,1)S(1)}, u32[]{:S(2)}, u32[]{:S(2)}) collective-permute-start(bf16[16,1280]{1,0:T(8,128)(2,1)S(1)} %get-tuple-element.66), channel_id=1, source_target_pairs={{0,12},{4,8},{8,4},{12,0},{1,13},{5,9},{9,5},{13,1},{2,14},{6,10},... | collective-permute-start | bytes 122888 | tf_op jit(solution)/shard_map/ppermute | solution.py:74
  10.6 5.3 %collective-permute-start.4 = (bf16[16,1280]{1,0:T(8,128)(2,1)S(1)}, bf16[16,1280]{1,0:T(8,128)(2,1)S(1)}, u32[]{:S(2)}, u32[]{:S(2)}) collective-permute-start(bf16[16,1280]{1,0:T(8,128)(2,1)S(1)} %get-tuple-element.67), channel_id=1, source_target_pairs={{0,8},{4,12},{8,0},{12,4},{1,9},{5,13},{9,1},{13,5},{2,10},{6,14},... | collective-permute-start | bytes 122888 | tf_op jit(solution)/shard_map/ppermute | solution.py:74
  10.6 5.3 %collective-permute-start.5 = (bf16[16,1280]{1,0:T(8,128)(2,1)S(1)}, bf16[16,1280]{1,0:T(8,128)(2,1)S(1)}, u32[]{:S(2)}, u32[]{:S(2)}) collective-permute-start(bf16[16,1280]{1,0:T(8,128)(2,1)S(1)} %get-tuple-element.68), channel_id=1, source_target_pairs={{0,4},{4,0},{8,12},{12,8},{1,5},{5,1},{9,13},{13,9},{2,6},{6,2},{1... | collective-permute-start | bytes 122888 | tf_op jit(solution)/shard_map/ppermute | solution.py:74
  11.2 10.2 %collective-permute-start.10 = (bf16[256,256]{1,0:T(8,128)(2,1)S(1)}, bf16[256,256]{1,0:T(8,128)(2,1)S(1)}, u32[]{:S(2)}, u32[]{:S(2)}) collective-permute-start(bf16[256,256]{1,0:T(8,128)(2,1)S(1)} %get-tuple-element.81), channel_id=1, source_target_pairs={{0,12},{4,8},{8,4},{12,0},{16,24},{20,28},{24,16},{28,20},{1,13},{... | collective-permute-start | bytes 393224 | tf_op jit(solution)/shard_map/ppermute | solution.py:356
  16.5 7.4 %collective-permute-start.7 = (bf16[32,640]{1,0:T(8,128)(2,1)S(1)}, bf16[32,640]{1,0:T(8,128)(2,1)S(1)}, u32[]{:S(2)}, u32[]{:S(2)}) collective-permute-start(bf16[32,640]{1,0:T(8,128)(2,1)S(1)} %get-tuple-element.77), channel_id=1, source_target_pairs={{0,4},{4,0},{8,12},{12,8},{1,5},{5,1},{9,13},{13,9},{2,6},{6,2},{1... | collective-permute-start | bytes 122888 | tf_op jit(solution)/shard_map/ppermute | solution.py:74
  17.1 6.9 %collective-permute-start.8 = (bf16[32,640]{1,0:T(8,128)(2,1)S(1)}, bf16[32,640]{1,0:T(8,128)(2,1)S(1)}, u32[]{:S(2)}, u32[]{:S(2)}) collective-permute-start(bf16[32,640]{1,0:T(8,128)(2,1)S(1)} %get-tuple-element.78), channel_id=1, source_target_pairs={{0,12},{4,8},{8,4},{12,0},{1,13},{5,9},{9,5},{13,1},{2,14},{6,10},... | collective-permute-start | bytes 122888 | tf_op jit(solution)/shard_map/ppermute | solution.py:74
  20.1 5.0 %collective-permute-start.9 = (bf16[32,640]{1,0:T(8,128)(2,1)S(1)}, bf16[32,640]{1,0:T(8,128)(2,1)S(1)}, u32[]{:S(2)}, u32[]{:S(2)}) collective-permute-start(bf16[32,640]{1,0:T(8,128)(2,1)S(1)} %get-tuple-element.79), channel_id=1, source_target_pairs={{0,8},{4,12},{8,0},{12,4},{1,9},{5,13},{9,1},{13,5},{2,10},{6,14},... | collective-permute-start | bytes 122888 | tf_op jit(solution)/shard_map/ppermute | solution.py:74
  20.1 7.6 %collective-permute-start.13 = (bf16[256,256]{1,0:T(8,128)(2,1)S(1)}, bf16[256,256]{1,0:T(8,128)(2,1)S(1)}, u32[]{:S(2)}, u32[]{:S(2)}) collective-permute-start(bf16[256,256]{1,0:T(8,128)(2,1)S(1)} %get-tuple-element.83), channel_id=1, source_target_pairs={{0,4},{4,0},{8,12},{12,8},{1,5},{5,1},{9,13},{13,9},{2,6},{6,2},{1... | collective-permute-start | bytes 393224 | tf_op jit(solution)/shard_map/ppermute | solution.py:74
  21.4 8.8 %collective-permute-start.14 = (bf16[256,256]{1,0:T(8,128)(2,1)S(1)}, bf16[256,256]{1,0:T(8,128)(2,1)S(1)}, u32[]{:S(2)}, u32[]{:S(2)}) collective-permute-start(bf16[256,256]{1,0:T(8,128)(2,1)S(1)} %collective-permute-done.10), channel_id=1, source_target_pairs={{0,16},{16,0},{1,17},{17,1},{2,18},{18,2},{3,19},{19,3},{4,20},{20... | collective-permute-start | bytes 393224 | tf_op jit(solution)/shard_map/ppermute | solution.py:74
  25.4 4.2 %collective-permute-start.12 = (bf16[32,640]{1,0:T(8,128)(2,1)S(1)}, bf16[32,640]{1,0:T(8,128)(2,1)S(1)}, u32[]{:S(2)}, u32[]{:S(2)}) collective-permute-start(bf16[32,640]{1,0:T(8,128)(2,1)S(1)} %shard_map.85), channel_id=1, source_target_pairs={{0,2},{2,8},{4,0},{6,10},{8,4},{10,14},{12,6},{14,12},{1,3},{3,9},... | collective-permute-start | bytes 122888 | tf_op jit(solution)/shard_map/ppermute | solution.py:381
  27.0 2.7 %collective-permute-start.11 = (bf16[32,640]{1,0:T(8,128)(2,1)S(1)}, bf16[32,640]{1,0:T(8,128)(2,1)S(1)}, u32[]{:S(2)}, u32[]{:S(2)}) collective-permute-start(bf16[32,640]{1,0:T(8,128)(2,1)S(1)} %shard_map.85), channel_id=1, source_target_pairs={{0,0},{2,10},{4,2},{6,8},{8,6},{10,12},{12,4},{14,14},{1,1},{3,11}... | collective-permute-start | bytes 122888 | tf_op jit(solution)/shard_map/ppermute | solution.py:381
  27.7 15.1 %copy-start.2 = (f32[1024]{0:T(1024)S(1)}, f32[1024]{0:T(1024)}, u32[]{:S(2)}) copy-start(f32[1024]{0:T(1024)} %refs_6_.1) | copy-start | bytes 12292
  27.7 15.1 %copy-start.3 = (s32[1,4,1]{1,2,0:T(1,128)S(1)}, s32[1,4,1]{1,2,0:T(1,128)}, u32[]{:S(2)}) copy-start(s32[1,4,1]{1,2,0:T(1,128)} %param.15) | copy-start | bytes 52
  30.3 12.4 %collective-permute-start.18 = (bf16[1024,256]{1,0:T(8,128)(2,1)S(1)}, bf16[1024,256]{1,0:T(8,128)(2,1)S(1)}, u32[]{:S(2)}, u32[]{:S(2)}) collective-permute-start(bf16[1024,256]{1,0:T(8,128)(2,1)S(1)} %constant_dynamic-update-slice_fusion.refs_4_), channel_id=1, source_target_pairs={{0,1},{1,0},{2,3},{3,2},{4,5},{5,4},{6,7},{7,6},{8,9},{9,8},{10,11... | collective-permute-start | bytes 1572872 | tf_op jit(solution)/shard_map/ppermute | solution.py:74
  30.4 7.1 %collective-permute-start.15 = (bf16[64,512]{1,0:T(8,128)(2,1)S(1)}, bf16[64,512]{1,0:T(8,128)(2,1)S(1)}, u32[]{:S(2)}, u32[]{:S(2)}) collective-permute-start(bf16[64,512]{1,0:T(8,128)(2,1)S(1)} %get-tuple-element.91), channel_id=1, source_target_pairs={{0,8},{4,12},{8,0},{12,4},{1,9},{5,13},{9,1},{13,5},{2,10},{6,14},... | collective-permute-start | bytes 196616 | tf_op jit(solution)/shard_map/ppermute | solution.py:74
  34.4 4.4 %collective-permute-start.16 = (bf16[64,512]{1,0:T(8,128)(2,1)S(1)}, bf16[64,512]{1,0:T(8,128)(2,1)S(1)}, u32[]{:S(2)}, u32[]{:S(2)}) collective-permute-start(bf16[64,512]{1,0:T(8,128)(2,1)S(1)} %get-tuple-element.92), channel_id=1, source_target_pairs={{0,4},{4,0},{8,12},{12,8},{1,5},{5,1},{9,13},{13,9},{2,6},{6,2},{1... | collective-permute-start | bytes 196616 | tf_op jit(solution)/shard_map/ppermute | solution.py:74
  36.4 6.3 %collective-permute-start.17 = (bf16[64,512]{1,0:T(8,128)(2,1)S(1)}, bf16[64,512]{1,0:T(8,128)(2,1)S(1)}, u32[]{:S(2)}, u32[]{:S(2)}) collective-permute-start(bf16[64,512]{1,0:T(8,128)(2,1)S(1)} %get-tuple-element.93), channel_id=1, source_target_pairs={{0,12},{4,8},{8,4},{12,0},{1,13},{5,9},{9,5},{13,1},{2,14},{6,10},... | collective-permute-start | bytes 196616 | tf_op jit(solution)/shard_map/ppermute | solution.py:74
  43.1 6.1 %collective-permute-start.19 = (bf16[16,1152]{1,0:T(8,128)(2,1)S(1)}, bf16[16,1152]{1,0:T(8,128)(2,1)S(1)}, u32[]{:S(2)}, u32[]{:S(2)}) collective-permute-start(bf16[16,1152]{1,0:T(8,128)(2,1)S(1)} %get-tuple-element.100), channel_id=1, source_target_pairs={{0,12},{4,8},{8,4},{12,0},{1,13},{5,9},{9,5},{13,1},{2,14},{6,10},... | collective-permute-start | bytes 110600 | tf_op jit(solution)/shard_map/ppermute | solution.py:74
  44.8 4.4 %collective-permute-start.20 = (bf16[16,1152]{1,0:T(8,128)(2,1)S(1)}, bf16[16,1152]{1,0:T(8,128)(2,1)S(1)}, u32[]{:S(2)}, u32[]{:S(2)}) collective-permute-start(bf16[16,1152]{1,0:T(8,128)(2,1)S(1)} %get-tuple-element.101), channel_id=1, source_target_pairs={{0,4},{4,0},{8,12},{12,8},{1,5},{5,1},{9,13},{13,9},{2,6},{6,2},{1... | collective-permute-start | bytes 110600 | tf_op jit(solution)/shard_map/ppermute | solution.py:74
  45.0 4.9 %collective-permute-start.21 = (bf16[16,1152]{1,0:T(8,128)(2,1)S(1)}, bf16[16,1152]{1,0:T(8,128)(2,1)S(1)}, u32[]{:S(2)}, u32[]{:S(2)}) collective-permute-start(bf16[16,1152]{1,0:T(8,128)(2,1)S(1)} %get-tuple-element.102), channel_id=1, source_target_pairs={{0,8},{4,12},{8,0},{12,4},{1,9},{5,13},{9,1},{13,5},{2,10},{6,14},... | collective-permute-start | bytes 110600 | tf_op jit(solution)/shard_map/ppermute | solution.py:74
  50.0 3.8 %collective-permute-start.22 = (bf16[8,1152]{1,0:T(8,128)(2,1)S(1)}, bf16[8,1152]{1,0:T(8,128)(2,1)S(1)}, u32[]{:S(2)}, u32[]{:S(2)}) collective-permute-start(bf16[8,1152]{1,0:T(8,128)(2,1)S(1)} %get-tuple-element.105), channel_id=1, source_target_pairs={{0,2},{2,0},{1,3},{3,1},{4,6},{6,4},{5,7},{7,5},{8,10},{10,8},{9,1... | collective-permute-start | bytes 55304 | tf_op jit(solution)/shard_map/ppermute | solution.py:74
